TPU v7x, 256 devices: a whole 4x4x8 slice. The times are simulated.
256 devices in a mesh: dp: 32 (over y, x, z_lo), mp: 8 (over z_hi, core).
Axes of the slice: x: 4, y: 4, z: 8 (z_hi: 4, z_lo: 2; z = z_hi * 2 + z_lo), core: 2. Of those that a mesh axis runs over, the one named last changes fastest.
Arguments:
- tokens: bfloat16 [17408, 4096], P('dp'), may hold values from -16 to 16
- out_grad: bfloat16 [17408, 8192], P('dp', 'mp'), may hold values from -64 to 64
- weight: float32 [4096, 8192], P('dp', 'mp'), may hold values from -0.09375 to 0.09375
- momentum: float32 [4096, 8192], P('dp', 'mp'), may hold values from -1.2 to 1.2
- next_tokens: bfloat16 [17408, 4096], P('dp'), may hold values from -6 to 6
Outputs:
- new_weight: float32 [4096, 8192], P('dp', 'mp')
- new_momentum: float32 [4096, 8192], P('dp', 'mp')
- projected: bfloat16 [17408, 8192], P('dp', 'mp')
All inputs are finite; a program needn't handle non-finite values.
Results may differ from a plain program's by a relative error of at most 0.0012.
The roundings to bfloat16 on the way count: a program that leaves them out, or rounds other values in their place, can miss the bound.
Values may be sent and summed in bfloat16 or wider, within the bound.
No kernel may reach another device: no remote copies, remote signals or barrier semaphores. Data moves between devices by JAX's collectives and lax.ppermute only.
A program may use at most 128 MiB of HBM per device.

v0:
```python
import jax
import jax.numpy as jnp
from jax import lax
from jax.sharding import PartitionSpec as P

BLK = 128


EPSILON = 1e-06
DECAY = 0.9
STEP_SIZE = 0.005


def swapped(block, axis, distance):
    count = lax.axis_size(axis)
    route = []
    for low in range(count):
        high = low | 1 << distance
        if high != low and high < count:
            route += [(low, high), (high, low)]
    return lax.ppermute(block, axis, route)


def gradient(token_cols, grad_rows):
    product = lax.dot_general(
        token_cols, grad_rows, (((0,), (0,)), ((), ())), preferred_element_type=jnp.float32
    )
    return product / token_cols.shape[0]


def combine(kept_part, incoming):
    column_count = kept_part.shape[1]
    block_count = kept_part.shape[0] // BLK
    kept_blocks = kept_part.reshape(block_count, BLK, column_count)
    other_blocks = incoming.reshape(block_count, BLK, column_count)
    partial_sums = (
        jnp.sum(kept_blocks * other_blocks, axis=(1, 2)),
        jnp.sum(kept_blocks * kept_blocks, axis=(1, 2)),
        jnp.sum(other_blocks * other_blocks, axis=(1, 2)),
    )
    cross_sum, kept_norm, other_norm = lax.psum(
        (partial_sums[0], partial_sums[1], partial_sums[2]), "mp"
    )
    kept_factor = 1.0 - cross_sum / (2.0 * (kept_norm + EPSILON))
    other_factor = 1.0 - cross_sum / (2.0 * (other_norm + EPSILON))
    mixed = kept_factor[:, None, None] * kept_blocks + other_factor[:, None, None] * other_blocks
    return mixed.reshape(kept_part.shape)


def shards(tokens, out_grad, weight, momentum, next_tokens):
    level_count = lax.axis_size("dp").bit_length() - 1
    device_index = lax.axis_index("dp")
    current = gradient(tokens, out_grad)
    begin_section = 0
    for section_step in range(begin_section, level_count):
        bit_number = level_count - 1 - section_step
        upper_side = device_index >> bit_number & 1
        half_rows = current.shape[0] // 2
        kept_part = lax.dynamic_slice_in_dim(current, upper_side * half_rows, half_rows, 0)
        outgoing = lax.dynamic_slice_in_dim(current, (1 - upper_side) * half_rows, half_rows, 0)
        incoming = swapped(outgoing, "dp", bit_number)
        current = combine(kept_part, incoming)
    new_momentum = DECAY * momentum + current
    new_weight = weight - STEP_SIZE * new_momentum
    weight_half = new_weight.astype(jnp.bfloat16)
    projected = jnp.dot(
        next_tokens,
        lax.all_gather(weight_half, "dp", axis=0, tiled=True),
        preferred_element_type=jnp.float32,
    )
    return (new_weight, new_momentum, projected.astype(jnp.bfloat16))


def solution(mesh):
    return jax.shard_map(
        shards,
        mesh=mesh,
        in_specs=(P("dp", None), P("dp", "mp"), P("dp", "mp"), P("dp", "mp"), P("dp", None)),
        out_specs=(P("dp", "mp"), P("dp", "mp"), P("dp", "mp")),
        check_vma=False,
    )
```

profile of v0, /device:TPU:30, one launch (start us, length us, event | category | flops | bytes accessed | tf_op | source)
XLA Modules:
  0.0 742.0 jit_solution(14439463908951069259)
XLA Ops:
  8.4 8.8 %broadcast_multiply_fusion = f32[4096,1024]{0,1:T(8,128)S(1)} fusion(bf16[544,4096]{1,0:T(8,128)(2,1)} %param.5, bf16[544,1024]{1,0:T(8,128)(2,1)S(1)} %copy-done), kind=kOutput, calls=%fused_computation.4 | convolution fusion | flops 4567597056 | bytes 22347776 | tf_op jit(solution)/shard_map/dot_general | solution.py:25
  17.3 4.2 constant_dynamic-slice_fusion.4
  21.5 4.0 copy-done.2
  26.7 182.8 %collective-permute-done = f32[2048,1024]{0,1:T(8,128)} collective-permute-done((f32[2048,1024]{0,1:T(8,128)}, f32[2048,1024]{0,1:T(8,128)}, u32[]{:S(2)}, u32[]{:S(2)}) %collective-permute-start) | collective-permute-done | bytes 8388640 | tf_op jit(solution)/shard_map/ppermute | solution.py:21
  209.5 6.8 multiply_reduce_fusion.1
  216.6 19.1 %all-reduce.4 = (f32[16]{0:T(128)S(1)}, f32[16]{0:T(128)S(1)}, f32[16]{0:T(128)S(1)}) all-reduce(f32[16]{0:T(128)S(1)} %bitcast_reduce_fusion.2, f32[16]{0:T(128)S(1)} %get-tuple-element.50, f32[16]{0:T(128)S(1)} %get-tuple-element.51), channel_id=1, replica_groups=mesh['dp'=32,'mp'=8] {'mp'}, use_global_device_ids=true, to_apply=%region_2.0 | all-reduce | flops 48 | bytes 384 | tf_op jit(solution)/shard_map/psum | solution.py:41
  235.8 11.9 %multiply_add_fusion = f32[2048,1024]{0,1:T(8,128)} fusion(f32[2048,1024]{0,1:T(8,128)} %collective-permute-done, f32[4096,1024]{0,1:T(8,128)} %copy-done.2, s32[]{:T(128)S(6)} %select_n.30, f32[2048]{0:T(1024)S(1)} %broadcast_bitcast_fusion, f32[2048]{0:T(1024)S(1)} %broadcast_bitcast_fusion.1), kind=kLoop, calls=%fused_computation | loop fusion | flops 6291456 | bytes 25182212 | tf_op jit(solution)/shard_map/add | solution.py:46
  247.8 4.7 constant_dynamic-slice_fusion.3
  253.2 89.6 %collective-permute-done.1 = f32[1024,1024]{0,1:T(8,128)} collective-permute-done((f32[1024,1024]{0,1:T(8,128)}, f32[1024,1024]{0,1:T(8,128)}, u32[]{:S(2)}, u32[]{:S(2)}) %collective-permute-start.1) | collective-permute-done | bytes 4194336 | tf_op jit(solution)/shard_map/ppermute | solution.py:21
  342.9 4.6 multiply_reduce_fusion.4
  347.8 16.1 %all-reduce.3 = (f32[8]{0:T(128)S(1)}, f32[8]{0:T(128)S(1)}, f32[8]{0:T(128)S(1)}) all-reduce(f32[8]{0:T(128)S(1)} %bitcast_reduce_fusion.5, f32[8]{0:T(128)S(1)} %bitcast_reduce_fusion.3, f32[8]{0:T(128)S(1)} %bitcast_reduce_fusion.4), channel_id=1, replica_groups=mesh['dp'=32,'mp'=8] {'mp'}, use_global_device_ids=true, to_apply=%region_11.0 | all-reduce | flops 24 | bytes 192 | tf_op jit(solution)/shard_map/psum | solution.py:41
  364.0 4.5 multiply_add_fusion.1
  368.5 1.9 copy-done.3
  373.3 45.8 %collective-permute-done.2 = f32[512,1024]{0,1:T(8,128)S(1)} collective-permute-done((f32[512,1024]{0,1:T(8,128)}, f32[512,1024]{0,1:T(8,128)S(1)}, u32[]{:S(2)}, u32[]{:S(2)}) %collective-permute-start.2) | collective-permute-done | bytes 2097184 | tf_op jit(solution)/shard_map/ppermute | solution.py:21
  419.2 2.8 multiply_reduce_fusion.7
  422.3 15.2 %all-reduce.2 = (f32[4]{0:T(128)S(1)}, f32[4]{0:T(128)S(1)}, f32[4]{0:T(128)S(1)}) all-reduce(f32[4]{0:T(128)S(1)} %bitcast_reduce_fusion.8, f32[4]{0:T(128)S(1)} %bitcast_reduce_fusion.6, f32[4]{0:T(128)S(1)} %bitcast_reduce_fusion.7), channel_id=1, replica_groups=mesh['dp'=32,'mp'=8] {'mp'}, use_global_device_ids=true, to_apply=%region_20.0 | all-reduce | flops 12 | bytes 96 | tf_op jit(solution)/shard_map/psum | solution.py:41
  437.7 2.7 multiply_add_fusion.2
  442.3 23.3 %collective-permute-done.3 = f32[256,1024]{0,1:T(8,128)S(1)} collective-permute-done((f32[256,1024]{0,1:T(8,128)}, f32[256,1024]{0,1:T(8,128)S(1)}, u32[]{:S(2)}, u32[]{:S(2)}) %collective-permute-start.3) | collective-permute-done | bytes 1048608 | tf_op jit(solution)/shard_map/ppermute | solution.py:21
  466.3 14.2 %all-reduce.1 = (f32[2]{0:T(128)S(1)}, f32[2]{0:T(128)S(1)}, f32[2]{0:T(128)S(1)}) all-reduce(f32[2]{0:T(128)S(1)} %bitcast_reduce_fusion.11, f32[2]{0:T(128)S(1)} %bitcast_reduce_fusion.9, f32[2]{0:T(128)S(1)} %bitcast_reduce_fusion.10), channel_id=1, replica_groups=mesh['dp'=32,'mp'=8] {'mp'}, use_global_device_ids=true, to_apply=%region_29.0 | all-reduce | flops 6 | bytes 48 | tf_op jit(solution)/shard_map/psum | solution.py:41
  485.8 10.2 %collective-permute-done.4 = f32[128,1024]{0,1:T(8,128)S(1)} collective-permute-done((f32[128,1024]{0,1:T(8,128)S(1)}, f32[128,1024]{0,1:T(8,128)S(1)}, u32[]{:S(2)}, u32[]{:S(2)}) %collective-permute-start.4) | collective-permute-done | bytes 524320 | tf_op jit(solution)/shard_map/ppermute | solution.py:21
  496.7 14.8 %all-reduce = (f32[1]{0:T(128)}, f32[1]{0:T(128)}, f32[1]{0:T(128)}) all-reduce(f32[1]{0:T(128)} %bitcast.20, f32[1]{0:T(128)} %bitcast.23, f32[1]{0:T(128)} %bitcast.21), channel_id=1, replica_groups=mesh['dp'=32,'mp'=8] {'mp'}, use_global_device_ids=true, to_apply=%region_37.38 | all-reduce | flops 3 | bytes 24 | tf_op jit(solution)/shard_map/psum | solution.py:41
  515.2 2.0 copy.14
  518.2 206.3 %all-gather.2.cloned.1.call-done = bf16[4096,1024]{0,1:T(8,128)(2,1)} async-done(((bf16[128,1024]{0,1:T(8,128)(2,1)}), bf16[4096,1024]{0,1:T(8,128)(2,1)}) %all-gather.2.cloned.1.call-update) | async-done | bytes 8388624 | tf_op jit(solution)/shard_map/all_gather | solution.py:68
  724.6 10.5 %fusion = bf16[544,1024]{1,0:T(8,128)(2,1)} fusion(bf16[4096,1024]{0,1:T(8,128)(2,1)} %all-gather.2.cloned.1.call-done, bf16[544,4096]{1,0:T(8,128)(2,1)} %param.9), kind=kOutput, calls=%fused_computation.14 | convolution fusion | flops 4563959808 | bytes 13959168 | tf_op jit(solution)/shard_map/dot_general | solution.py:66
  (50 shorter events, 18.1 us)
Async XLA Ops:
  7.2 1.3 copy-start
  7.2 717.4 %all-gather.2.cloned.1.call-start = ((), (), s32[]{:S(2)}) async-start(), calls=%async_computation | async-start | bytes 8650752 | tf_op jit(solution)/shard_map/all_gather | solution.py:68
  17.3 8.2 %copy-start.2 = (f32[4096,1024]{0,1:T(8,128)}, f32[4096,1024]{0,1:T(8,128)S(1)}, u32[]{:S(2)}) copy-start(f32[4096,1024]{0,1:T(8,128)S(1)} %broadcast_multiply_fusion) | copy-start | bytes 50331652
  25.5 184.0 %collective-permute-start = (f32[2048,1024]{0,1:T(8,128)}, f32[2048,1024]{0,1:T(8,128)}, u32[]{:S(2)}, u32[]{:S(2)}) collective-permute-start(f32[2048,1024]{0,1:T(8,128)} %constant_dynamic-slice_fusion.4), channel_id=1, source_target_pairs={{0,128},{128,0},{8,136},{136,8},{16,144},{144,16},{24,152},{152,24... | collective-permute-start | bytes 25165832 | tf_op jit(solution)/shard_map/ppermute | solution.py:21
  252.5 90.4 %collective-permute-start.1 = (f32[1024,1024]{0,1:T(8,128)}, f32[1024,1024]{0,1:T(8,128)}, u32[]{:S(2)}, u32[]{:S(2)}) collective-permute-start(f32[1024,1024]{0,1:T(8,128)} %constant_dynamic-slice_fusion.3), channel_id=1, source_target_pairs={{0,64},{64,0},{8,72},{72,8},{16,80},{80,16},{24,88},{88,24},{32,96... | collective-permute-start | bytes 12582920 | tf_op jit(solution)/shard_map/ppermute | solution.py:21
  368.5 1.9 copy-start.3
  371.9 47.3 %collective-permute-start.2 = (f32[512,1024]{0,1:T(8,128)}, f32[512,1024]{0,1:T(8,128)S(1)}, u32[]{:S(2)}, u32[]{:S(2)}) collective-permute-start(f32[512,1024]{0,1:T(8,128)} %constant_dynamic-slice_fusion.2), channel_id=1, source_target_pairs={{0,32},{32,0},{8,40},{40,8},{16,48},{48,16},{24,56},{56,24},{64,96... | collective-permute-start | bytes 6291464 | tf_op jit(solution)/shard_map/ppermute | solution.py:21
  419.2 18.4 %copy-start.4 = (f32[512,1024]{0,1:T(8,128)}, f32[512,1024]{0,1:T(8,128)S(1)}, u32[]{:S(2)}) copy-start(f32[512,1024]{0,1:T(8,128)S(1)} %collective-permute-done.2) | copy-start | bytes 6291460
  441.5 24.1 %collective-permute-start.3 = (f32[256,1024]{0,1:T(8,128)}, f32[256,1024]{0,1:T(8,128)S(1)}, u32[]{:S(2)}, u32[]{:S(2)}) collective-permute-start(f32[256,1024]{0,1:T(8,128)} %constant_dynamic-slice_fusion.1), channel_id=1, source_target_pairs={{0,16},{16,0},{8,24},{24,8},{32,48},{48,32},{40,56},{56,40},{64,80... | collective-permute-start | bytes 3145736 | tf_op jit(solution)/shard_map/ppermute | solution.py:21
  465.6 14.9 %copy-start.5 = (f32[256,1024]{0,1:T(8,128)}, f32[256,1024]{0,1:T(8,128)S(1)}, u32[]{:S(2)}) copy-start(f32[256,1024]{0,1:T(8,128)S(1)} %collective-permute-done.3) | copy-start | bytes 3145732
  482.2 13.8 %collective-permute-start.4 = (f32[128,1024]{0,1:T(8,128)S(1)}, f32[128,1024]{0,1:T(8,128)S(1)}, u32[]{:S(2)}, u32[]{:S(2)}) collective-permute-start(f32[128,1024]{0,1:T(8,128)S(1)} %constant_dynamic-slice_fusion), channel_id=1, source_target_pairs={{0,8},{8,0},{16,24},{24,16},{32,40},{40,32},{48,56},{56,48},{64,72... | collective-permute-start | bytes 1572872 | tf_op jit(solution)/shard_map/ppermute | solution.py:21
  724.6 10.5 %copy-start.1 = (bf16[544,1024]{1,0:T(8,128)(2,1)S(1)}, bf16[544,1024]{1,0:T(8,128)(2,1)}, u32[]{:S(2)}) copy-start(bf16[544,1024]{1,0:T(8,128)(2,1)} %param.6) | copy-start | bytes 3342340
Sparse Core Ops, SparseCore 0:
  515.3 209.2 all-gather.1
where the time goes:
time: 743 us; the launch traced here: 742 us
  waiting for transfers between devices  558 us (75%)
  blocking collectives  79.4 us (11%)
  other arithmetic  38.2 us (5%)
  local copies, waits for them, and re-layouts  24.8 us (3%)
  matrix products  19.4 us (3%)
  between operations  16.8 us (2%)
    ppermute x5, waiting for transfers between devices, swapped(): return lax.ppermute(block, axis, route)  352 us
    all_gather x1, waiting for transfers between devices, shards(): lax.all_gather(weight_half, 'dp', axis=0, tiled=True)  206 us
    psum x5, blocking collectives, combine(): lax.psum((partial_sums[0], partial_sums[1], partial_sums[2]), 'mp')  79.4 us
    add x4, other arithmetic, combine(): kept_factor[:, None, None] * kept_blocks  20.6 us
    reduce_sum x8, other arithmetic, combine(): jnp.sum(kept_blocks * kept_blocks, axis=(1, 2))  15.6 us
  transfers between devices with their start and end apart: 6, of which 6 were waited for; matrix products, arithmetic and copies ran while one was open for 1% of the time, Pallas kernels for 0%

commit v1 on v0

v1 whole, which is shorter than its diff:
```python
import functools

import jax
import jax.numpy as jnp
from jax import lax
from jax.experimental import pallas as pl
from jax.experimental.pallas import tpu as pltpu
from jax.sharding import PartitionSpec as P

BLK = 128
EPSILON = 1e-06
DECAY = 0.9
STEP_SIZE = 0.005

NY, NX, NZ, NH, NC = 4, 4, 2, 4, 2
PAIRS_Y = [(0, 0), (1, 1), (2, 2), (3, 3), (0, 2), (1, 3), (0, 1), (0, 3), (1, 2), (2, 3)]
PAIRS_XZ = [(i, j) for i in range(8) for j in range(i, 8)]
F32 = jnp.float32


def move_dp(block, dy=0, dx=0, dz=0):
    route = []
    for y in range(NY):
        for x in range(NX):
            for z in range(NZ):
                target = (((y + dy) % NY) * NX + (x + dx) % NX) * NZ + (z + dz) % NZ
                route.append(((y * NX + x) * NZ + z, target))
    return lax.ppermute(block, "dp", route)


def move_mp(block, dh=0, dc=0):
    route = []
    for h in range(NH):
        for c in range(NC):
            route.append((h * NC + c, ((h + dh) % NH) * NC + (c + dc) % NC))
    return lax.ppermute(block, "mp", route)


def sum_mp(part):
    part = part + move_mp(part, dc=1)
    one, two, three = move_mp(part, dh=1), move_mp(part, dh=2), move_mp(part, dh=3)
    return (part + two) + (one + three)


def turn_kernel(place, tokens_ref, mine_ref, other_ref, turned_ref):
    core = place[2]
    for which, ref in ((0, mine_ref), (1, other_ref)):
        side = core if which == 0 else 1 - core
        own = tokens_ref[:, pl.ds(pl.multiple_of(side * BLK, BLK), BLK)]
        for k, cols in enumerate([own, ref[0, 0], ref[0, 1], ref[0, 2]]):
            turned_ref[k, pl.ds(pl.multiple_of(side * BLK, BLK), BLK), :] = cols.T


def turn(place, tokens, mine, other):
    tok_dev = tokens.shape[0]
    recv = pl.BlockSpec((1, 3, tok_dev, BLK), lambda j, p: (j, 0, 0, 0))
    return pl.pallas_call(
        turn_kernel,
        grid_spec=pltpu.PrefetchScalarGridSpec(
            num_scalar_prefetch=1,
            grid=(NH,),
            in_specs=[
                pl.BlockSpec((tok_dev, 2 * BLK), lambda j, p: (0, p[0] * NH + lax.rem(p[1] - j + NH, NH))),
                recv,
                recv,
            ],
            out_specs=pl.BlockSpec((4, 2 * BLK, tok_dev), lambda j, p: (0, lax.rem(p[1] - j + NH, NH), 0)),
        ),
        out_shape=jax.ShapeDtypeStruct((4, 2 * NH * BLK, tok_dev), jnp.bfloat16),
        compiler_params=pltpu.CompilerParams(vmem_limit_bytes=24 * 2**20),
    )(place, tokens, mine, other)


def grads_kernel(turned_ref, o0_ref, o1_ref, o2_ref, o3_ref, grads_ref, gram_ref, sums_ref):
    step = pl.program_id(0)

    @pl.when(step == 0)
    def _():
        sums_ref[...] = jnp.zeros_like(sums_ref)

    blocks, _, _, span = grads_ref.shape
    for k, o_ref in enumerate((o0_ref, o1_ref, o2_ref, o3_ref)):
        product = jnp.dot(turned_ref[k], o_ref[...], preferred_element_type=F32)
        grads_ref[:, k] = product.reshape(blocks, BLK, span)

    def one_block(m, _):
        sums = [sums_ref[m, n] for n in range(len(PAIRS_Y))]
        for t in range(BLK // 8):
            for part in range(span // 128):
                at, lanes = pl.ds(t * 8, 8), pl.ds(part * 128, 128)
                g = [grads_ref[m, k, at, lanes] for k in range(4)]
                for n, (i, j) in enumerate(PAIRS_Y):
                    sums[n] = sums[n] + g[i] * g[j]
        for n in range(len(PAIRS_Y)):
            sums_ref[m, n] = sums[n]
        return 0

    lax.fori_loop(0, blocks, one_block, 0)

    @pl.when(step == pl.num_programs(0) - 1)
    def _():
        rows = jnp.sum(sums_ref[...], axis=2).reshape(blocks * 16, 128)
        gram_ref[...] = jnp.broadcast_to(jnp.sum(rows.T, axis=0, keepdims=True), gram_ref.shape)


def grads_and_gram(turned, outs):
    tok_dev, cols = outs[0].shape
    span = 256
    blocks = turned.shape[1] // BLK
    out_cols = pl.BlockSpec((tok_dev, span), lambda n: (0, n))
    return pl.pallas_call(
        grads_kernel,
        grid=(cols // span,),
        in_specs=[pl.BlockSpec(turned.shape, lambda n: (0, 0, 0)), out_cols, out_cols, out_cols, out_cols],
        out_specs=[
            pl.BlockSpec((blocks, 4, BLK, span), lambda n: (0, 0, 0, n)),
            pl.BlockSpec((8, 128), lambda n: (0, 0)),
        ],
        out_shape=[
            jax.ShapeDtypeStruct((blocks, 4, BLK, cols), F32),
            jax.ShapeDtypeStruct((8, 128), F32),
        ],
        scratch_shapes=[pltpu.VMEM((blocks, 16, 8, 128), F32)],
        compiler_params=pltpu.CompilerParams(vmem_limit_bytes=48 * 2**20),
    )(turned, *outs)


def mix_kernel(tok_dev, gram_ref, grads_ref, coded_ref):
    step = pl.program_id(0)
    g = gram_ref[...] * (1.0 / (tok_dev * tok_dev))
    at = {}
    for n, pair in enumerate(PAIRS_Y):
        at[pair] = g if n == 0 else pltpu.roll(g, 128 - n, 1)
    p = [at[(k, k)] for k in range(4)]
    c02, c13 = at[(0, 2)], at[(1, 3)]
    a0 = 1.0 - c02 / (2.0 * (p[0] + EPSILON))
    a2 = 1.0 - c02 / (2.0 * (p[2] + EPSILON))
    a1 = 1.0 - c13 / (2.0 * (p[1] + EPSILON))
    a3 = 1.0 - c13 / (2.0 * (p[3] + EPSILON))
    even = jnp.maximum((a0 * a0) * p[0] + 2.0 * ((a0 * a2) * c02) + (a2 * a2) * p[2], 0.0)
    odd = jnp.maximum((a1 * a1) * p[1] + 2.0 * ((a1 * a3) * c13) + (a3 * a3) * p[3], 0.0)
    cross = (a0 * a1) * at[(0, 1)] + (a0 * a3) * at[(0, 3)] + (a2 * a1) * at[(1, 2)] + (a2 * a3) * at[(2, 3)]
    f_even = 1.0 - cross / (2.0 * (even + EPSILON))
    f_odd = 1.0 - cross / (2.0 * (odd + EPSILON))
    w = [f_even * a0, f_odd * a1, f_even * a2, f_odd * a3]
    here = lax.broadcasted_iota(jnp.int32, g.shape, 1) == step * 16
    s = [
        jnp.sum(jnp.where(here, w[k] * (1.0 / tok_dev), 0.0), axis=1, keepdims=True)[:1] for k in range(4)
    ]
    span = 256
    for first in range(0, grads_ref.shape[3], span):
        lanes = pl.ds(first, span)
        mixed = (s[0] * grads_ref[0, 0, :, lanes] + s[2] * grads_ref[0, 2, :, lanes]) + (
            s[1] * grads_ref[0, 1, :, lanes] + s[3] * grads_ref[0, 3, :, lanes]
        )
        peak = jnp.maximum(jnp.max(jnp.abs(mixed), axis=0, keepdims=True), 1e-30)
        exponent = jnp.ceil(jnp.log2(peak))
        mantissa = jnp.ceil(peak * jnp.exp2(-exponent) * 512.0) * (1.0 / 512.0)
        level = mixed * (LEVELS * jnp.exp2(-exponent) / mantissa)
        size = jnp.abs(level)
        whole = jnp.floor(size)
        code = jnp.exp2(whole - 14.0) * (1.0 + (size - whole))
        coded_ref[0, :BLK, lanes] = jnp.where(level < 0.0, -code, code)
        row = lax.broadcasted_iota(jnp.int32, (8, span), 0)
        coded_ref[0, BLK:, lanes] = jnp.where(row == 0, exponent, mantissa)


LEVELS = 29.9


def decode(landed):
    code = landed[:, :BLK].astype(F32)
    exponent = landed[:, BLK : BLK + 1].astype(F32)
    mantissa = landed[:, BLK + 1 : BLK + 2].astype(F32)
    size = jnp.abs(code)
    whole = jnp.floor(jnp.log2(size))
    level = (whole + 13.0) + size * jnp.exp2(-whole)
    return jnp.where(code < 0.0, -level, level) * (jnp.exp2(exponent) * mantissa * (1.0 / LEVELS))


def mix(gram, grads, tok_dev):
    blocks, _, _, cols = grads.shape
    return pl.pallas_call(
        functools.partial(mix_kernel, tok_dev),
        grid=(blocks,),
        in_specs=[
            pl.BlockSpec((8, 128), lambda m: (0, 0)),
            pl.BlockSpec((1, 4, BLK, cols), lambda m: (m, 0, 0, 0)),
        ],
        out_specs=pl.BlockSpec((1, BLK + 8, cols), lambda m: (m, 0, 0)),
        out_shape=jax.ShapeDtypeStruct((blocks, BLK + 8, cols), F32),
        compiler_params=pltpu.CompilerParams(vmem_limit_bytes=56 * 2**20),
    )(gram, grads)


def gram8_kernel(parts_ref, gram_ref):
    def tile(t, sums):
        at = pl.ds(pl.multiple_of(t * 8, 8), 8)
        sums = list(sums)
        for span in range(parts_ref.shape[2] // 128):
            h = [parts_ref[k, at, pl.ds(span * 128, 128)] for k in range(8)]
            for n, (i, j) in enumerate(PAIRS_XZ):
                sums[n] = sums[n] + h[i] * h[j]
        return tuple(sums)

    zero = tuple(jnp.zeros((8, 128), F32) for _ in PAIRS_XZ)
    sums = lax.fori_loop(0, BLK // 8, tile, zero)
    for n, s in enumerate(sums):
        gram_ref[n : n + 1, :] = jnp.sum(s, axis=0, keepdims=True)
    gram_ref[len(sums) :, :] = jnp.zeros((gram_ref.shape[0] - len(sums), 128), F32)


def gram8(parts):
    return pl.pallas_call(
        gram8_kernel,
        out_shape=jax.ShapeDtypeStruct((40, 128), F32),
        compiler_params=pltpu.CompilerParams(vmem_limit_bytes=32 * 2**20),
    )(parts)


def update_kernel(gram_ref, parts_ref, weight_ref, momentum_ref, new_weight_ref, new_momentum_ref, half_ref):
    sums = jnp.sum(gram_ref[...], axis=1, keepdims=True)
    g = {}
    for n, (i, j) in enumerate(PAIRS_XZ):
        g[i, j] = g[j, i] = sums[n : n + 1, :]
    w = [None] * 8
    groups = [[k] for k in range(8)]
    while len(groups) > 1:
        half = len(groups) // 2
        factor = {}
        for a in range(half):
            b = a + half
            factor[a] = 1.0 - g[a, b] / (2.0 * (g[a, a] + EPSILON))
            factor[b] = 1.0 - g[a, b] / (2.0 * (g[b, b] + EPSILON))
        for a, members in enumerate(groups):
            for k in members:
                w[k] = factor[a] if w[k] is None else w[k] * factor[a]
        scaled = {(i, j): (factor[i] * factor[j]) * g[i, j] for i in factor for j in factor}
        g = {}
        for a in range(half):
            for b in range(half):
                total = (scaled[a, b] + scaled[a + half, b + half]) + (scaled[a, b + half] + scaled[a + half, b])
                g[a, b] = jnp.maximum(total, 0.0) if a == b else total
        groups = [groups[a] + groups[a + half] for a in range(half)]
    combined = w[0] * parts_ref[0]
    for k in range(1, 8):
        combined = combined + w[k] * parts_ref[k]
    new_momentum = DECAY * momentum_ref[...] + combined
    new_weight = weight_ref[...] - STEP_SIZE * new_momentum
    new_momentum_ref[...] = new_momentum
    new_weight_ref[...] = new_weight
    half_ref[...] = new_weight.astype(jnp.bfloat16)


def update(gram, parts, weight, momentum):
    rows, cols = weight.shape
    tile = 32
    flat = pl.BlockSpec((tile, cols), lambda t: (t, 0))
    return pl.pallas_call(
        update_kernel,
        grid=(rows // tile,),
        in_specs=[
            pl.BlockSpec(gram.shape, lambda t: (0, 0)),
            pl.BlockSpec((8, tile, cols), lambda t: (0, t, 0)),
            flat,
            flat,
        ],
        out_specs=[flat, flat, flat],
        out_shape=[
            jax.ShapeDtypeStruct((rows, cols), F32),
            jax.ShapeDtypeStruct((rows, cols), F32),
            jax.ShapeDtypeStruct((rows, cols), jnp.bfloat16),
        ],
        compiler_params=pltpu.CompilerParams(vmem_limit_bytes=32 * 2**20),
    )(gram, parts, weight, momentum)


def project_kernel(sets, last, place, left_ref, *refs):
    held, (start_ref, out_ref) = refs[: len(sets)], refs[len(sets) :]
    total = start_ref[...]
    for offsets, ref in zip(sets, held):
        parts = []
        for j, i, e in offsets:
            block = (lax.rem(place[0] - j + NY, NY) * NX + lax.rem(place[1] - i + NX, NX)) * NZ + lax.rem(
                place[2] + e, NZ
            )
            parts.append(left_ref[:, pl.ds(pl.multiple_of(block * BLK, BLK), BLK)])
        total = total + jnp.dot(jnp.concatenate(parts, 1), ref[...], preferred_element_type=F32)
    out_ref[...] = total.astype(out_ref.dtype)


def project(place, left, sets, held, start, last):
    vmem = pl.BlockSpec(memory_space=pltpu.VMEM)
    return pl.pallas_call(
        functools.partial(project_kernel, sets, last),
        in_specs=[pl.BlockSpec(memory_space=pltpu.SMEM)] + [vmem] * (len(held) + 2),
        out_specs=vmem,
        out_shape=jax.ShapeDtypeStruct(start.shape, jnp.bfloat16 if last else F32),
        compiler_params=pltpu.CompilerParams(vmem_limit_bytes=40 * 2**20),
    )(place, left, *held, start)


def gather_and_project(place, own, next_tokens):
    partner = move_dp(own, dz=1)
    a = [own] + [move_dp(own, dx=k) for k in (1, 2, 3)]
    b = [partner] + [move_dp(partner, dy=k) for k in (1, 2, 3)]
    a = jnp.concatenate(a, 0)
    b = jnp.concatenate(b, 0)
    half = a.shape[0] // 2
    a1, a3, b1, b3 = move_dp(a, dy=1), move_dp(a, dy=3), move_dp(b, dx=1), move_dp(b, dx=3)
    row_a = lambda j: [(j, i, 0) for i in range(NX)]
    row_b = lambda i: [(j, i, 1) for j in range(NY)]
    total = jnp.zeros((next_tokens.shape[0], own.shape[1]), F32)
    total = project(place, next_tokens, [row_a(0), row_b(0)], [a, b], total, False)
    a2 = [move_dp(a1[:half], dy=1), move_dp(a3[half:], dy=3)]
    b2 = [move_dp(b1[:half], dx=1), move_dp(b3[half:], dx=3)]
    sets = [row_a(1), row_a(3), row_b(1), row_b(3)]
    total = project(place, next_tokens, sets, [a1, a3, b1, b3], total, False)
    sets = [row_a(2)[:2], row_a(2)[2:], row_b(2)[:2], row_b(2)[2:]]
    return project(place, next_tokens, sets, a2 + b2, total, True)


def shards(tokens, out_grad, weight, momentum, next_tokens):
    dp, mp = lax.axis_index("dp"), lax.axis_index("mp")
    y, x, z = dp // (NX * NZ), dp // NZ % NX, dp % NZ
    tok_dev = tokens.shape[0]
    group = NX * NZ
    sent = []
    for k in (1, 2, 3):
        first = (((y + k) % NY) * group + mp) * BLK
        sent.append(move_dp(lax.dynamic_slice_in_dim(tokens, first, BLK, 1), dy=k))
    outs = [out_grad] + [move_dp(out_grad, dy=k) for k in (1, 2, 3)]
    piece = jnp.stack(sent)
    up, down = move_mp(piece, dh=1), move_mp(piece, dh=3)
    half = tok_dev // 2
    far = jnp.concatenate([move_mp(up[:, :half], dh=1), move_mp(down[:, half:], dh=3)], 1)
    mine = jnp.stack([piece, up, far, down])
    other = move_mp(mine, dc=1)
    place = jnp.stack([y, mp // NC, mp % NC]).astype(jnp.int32)
    grads, gram = grads_and_gram(turn(place, tokens, mine, other), outs)
    coded = mix(sum_mp(gram), grads, tok_dev).astype(jnp.float16)
    rings = [[ring * group + k for k in range(group)] for ring in range(NY)]
    parts = decode(lax.all_to_all(coded, "dp", 0, 0, axis_index_groups=rings))
    new_weight, new_momentum, weight_half = update(sum_mp(gram8(parts)), parts, weight, momentum)
    here = jnp.stack([y, x, z]).astype(jnp.int32)
    projected = gather_and_project(here, weight_half, next_tokens)
    return (new_weight, new_momentum, projected)


def solution(mesh):
    return jax.shard_map(
        shards,
        mesh=mesh,
        in_specs=(P("dp", None), P("dp", "mp"), P("dp", "mp"), P("dp", "mp"), P("dp", None)),
        out_specs=(P("dp", "mp"), P("dp", "mp"), P("dp", "mp")),
        check_vma=False,
    )
```

time: 743 us -> 288 us (0.39)
  waiting for transfers between devices: 558 us -> 137 us
  starting transfers between devices: 5.36 us -> 53.9 us
  blocking collectives: 79.4 us -> 31.3 us
  Pallas kernels: 0 us -> 43 us
  other arithmetic: 38.2 us -> 6.08 us
  matrix products: 19.4 us -> 0 us
  between operations: 16.8 us -> 1 us
  local copies, waits for them, and re-layouts: 24.8 us -> 15.2 us
    ppermute x5 -> x34, waiting for transfers between devices: 352 us -> 137 us  [the longest x21 108 us: move_dp(): return lax.ppermute(block, 'dp', route)]
    all_gather x1 -> x0, waiting for transfers between devices: 206 us -> none  [shards(): lax.all_gather(weight_half, 'dp', axis=0, tiled=True)]
    psum x5 -> x0, blocking collectives: 79.4 us -> none  [combine(): lax.psum((partial_sums[0], partial_sums[1], partial_sums[2]), 'mp')]
    ppermute x5 -> x34, starting transfers between devices: 5.33 us -> 53.9 us  [the longest x13 30.8 us: move_mp(): return lax.ppermute(block, 'mp', route)]
    pallas_call x0 -> x8, Pallas kernels: none -> 43 us  [the longest x1 16 us: grads_and_gram(): pl.pallas_call(grads_kernel, grid=(cols // span,), in_specs=[pl.BlockSpec...]
    all_to_all x0 -> x1, blocking collectives: none -> 31.3 us  [shards(): parts = decode(lax.all_to_all(coded, 'dp', 0, 0, axis_index_groups=rings))]
    add x4, other arithmetic: 20.6 us -> 0.61 us  [the longest x2 0.61 us: sum_mp(): return part + two + (one + three)]
    dot_general x2 -> x0, matrix products: 19.4 us -> none  [the longest x1 10.5 us: shards(): jnp.dot(next_tokens, lax.all_gather(weight_half, 'dp', axis=0, tiled=True...]
  transfers between devices with their start and end apart: 6 -> 34, of which waited for: 6 -> 22; matrix products, arithmetic and copies ran while one was open for 1% -> 1% of each run, Pallas kernels for 0% -> 3%
where the time goes in v1:
time: 288 us; the launch traced here: 287 us
  waiting for transfers between devices  137 us (48%)
  starting transfers between devices  53.9 us (19%)
  Pallas kernels  43 us (15%)
  blocking collectives  31.3 us (11%)
  local copies, waits for them, and re-layouts  15.2 us (5%)
  other arithmetic  6.08 us (2%)
    ppermute x21, waiting for transfers between devices, move_dp(): return lax.ppermute(block, 'dp', route)  108 us
    all_to_all x1, blocking collectives, shards(): parts = decode(lax.all_to_all(coded, 'dp', 0, 0, axis_index_groups=rings))  31.3 us
    ppermute x13, starting transfers between devices, move_mp(): return lax.ppermute(block, 'mp', route)  30.8 us
    ppermute x13, waiting for transfers between devices, move_mp(): return lax.ppermute(block, 'mp', route)  28.6 us
    ppermute x21, starting transfers between devices, move_dp(): return lax.ppermute(block, 'dp', route)  23.1 us
    pallas_call x1, Pallas kernels, grads_and_gram(): pl.pallas_call(grads_kernel, grid=(cols // span,), in_specs=[pl.BlockSpec...  16 us
    pallas_call x1, Pallas kernels, mix(): pl.pallas_call(functools.partial(mix_kernel, tok_dev), grid=(blocks,), in...  11.4 us
    unnamed x29, local copies, waits for them, and re-layouts  10.4 us
  transfers between devices with their start and end apart: 34, of which 22 were waited for; matrix products, arithmetic and copies ran while one was open for 1% of the time, Pallas kernels for 3%

profile of v1, /device:TPU:30, one launch (start us, length us, event | category | flops | bytes accessed | tf_op | source)
XLA Modules:
  0.0 287.2 jit_solution(17037857978504702936)
XLA Ops:
  4.7 3.7 %collective-permute-done = bf16[544,128]{1,0:T(8,128)(2,1)S(1)} collective-permute-done((bf16[544,128]{1,0:T(8,128)(2,1)S(1)}, bf16[544,128]{1,0:T(8,128)(2,1)S(1)}, u32[]{:S(2)}, u32[]{:S(2)}) %collective-permute-start) | collective-permute-done | bytes 139296 | tf_op jit(solution)/shard_map/ppermute | solution.py:28
  11.9 3.3 %collective-permute-start.3 = (bf16[3,544,128]{2,1,0:T(8,128)(2,1)S(1)}, bf16[3,544,128]{2,1,0:T(8,128)(2,1)S(1)}, u32[]{:S(2)}, u32[]{:S(2)}) collective-permute-start(bf16[3,544,128]{2,1,0:T(8,128)(2,1)S(1)} %get-tuple-element.17), channel_id=1, source_target_pairs={{0,2},{1,3},{2,4},{3,5},{4,6},{5,7},{6,0},{7,1},{8,10},{9,11},{10,... | collective-permute-start | bytes 1253384 | tf_op jit(solution)/shard_map/ppermute | solution.py:36
  15.3 3.1 %collective-permute-start.5 = (bf16[3,544,128]{2,1,0:T(8,128)(2,1)S(1)}, bf16[3,544,128]{2,1,0:T(8,128)(2,1)S(1)}, u32[]{:S(2)}, u32[]{:S(2)}) collective-permute-start(bf16[3,544,128]{2,1,0:T(8,128)(2,1)S(1)} %get-tuple-element.17), channel_id=1, source_target_pairs={{0,6},{1,7},{2,0},{3,1},{4,2},{5,3},{6,4},{7,5},{8,14},{9,15},{10,... | collective-permute-start | bytes 1253384 | tf_op jit(solution)/shard_map/ppermute | solution.py:36
  18.4 12.4 %collective-permute-done.3 = bf16[3,544,128]{2,1,0:T(8,128)(2,1)S(1)} collective-permute-done((bf16[3,544,128]{2,1,0:T(8,128)(2,1)S(1)}, bf16[3,544,128]{2,1,0:T(8,128)(2,1)S(1)}, u32[]{:S(2)}, u32[]{:S(2)}) %collective-permute-start.3) | collective-permute-done | bytes 417824 | tf_op jit(solution)/shard_map/ppermute | solution.py:36
  30.8 6.2 %collective-permute-start.4 = (bf16[3,272,128]{2,1,0:T(8,128)(2,1)S(1)}, bf16[3,272,128]{2,1,0:T(8,128)(2,1)S(1)}, u32[]{:S(2)}, u32[]{:S(2)}) collective-permute-start(bf16[3,272,128]{2,1,0:T(8,128)(2,1)S(1)} %slice.36), channel_id=1, source_target_pairs={{0,2},{1,3},{2,4},{3,5},{4,6},{5,7},{6,0},{7,1},{8,10},{9,11},{10,... | collective-permute-start | bytes 626696 | tf_op jit(solution)/shard_map/ppermute | solution.py:36
  37.5 2.8 collective-permute-start.6
  40.4 5.1 %collective-permute-done.4 = bf16[3,272,128]{2,1,0:T(8,128)(2,1)S(1)} collective-permute-done((bf16[3,272,128]{2,1,0:T(8,128)(2,1)S(1)}, bf16[3,272,128]{2,1,0:T(8,128)(2,1)S(1)}, u32[]{:S(2)}, u32[]{:S(2)}) %collective-permute-start.4) | collective-permute-done | bytes 208928 | tf_op jit(solution)/shard_map/ppermute | solution.py:36
  45.4 4.3 %collective-permute-done.6 = bf16[3,272,128]{2,1,0:T(8,128)(2,1)S(1)} collective-permute-done((bf16[3,272,128]{2,1,0:T(8,128)(2,1)S(1)}, bf16[3,272,128]{2,1,0:T(8,128)(2,1)S(1)}, u32[]{:S(2)}, u32[]{:S(2)}) %collective-permute-start.6) | collective-permute-done | bytes 208928 | tf_op jit(solution)/shard_map/ppermute | solution.py:36
  50.6 2.8 collective-permute-start.8
  56.3 2.9 %shard_map.76.turned_ref = bf16[4,1024,544]{2,1,0:T(8,128)(2,1)S(1)} custom-call(s32[3]{0:T(128)S(1)} %pad_add_fusion.place, bf16[544,4096]{1,0:T(8,128)(2,1)S(1)} %copy-done.2, bf16[4,3,544,128]{3,2,1,0:T(8,128)(2,1)S(1)} %pad_maximum_fusion.mine_ref, bf16[4,3,544,128]{3,2,1,0:T(8,128)(2,1)S(1)} %collective-permute-done.7.other_ref), custom_call_target="tpu_custom_call" | custom-call | tf_op jit(solution)/shard_map/pallas_call | solution.py:57
  61.5 41.0 %collective-permute-done.10.o3_ref = bf16[544,1024]{1,0:T(8,128)(2,1)} collective-permute-done((bf16[544,1024]{1,0:T(8,128)(2,1)}, bf16[544,1024]{1,0:T(8,128)(2,1)}, u32[]{:S(2)}, u32[]{:S(2)}) %collective-permute-start.10) | collective-permute-done | bytes 1114144 | tf_op jit(solution)/shard_map/ppermute | solution.py:28
  102.5 16.0 %shard_map.77 = (f32[8,4,128,1024]{3,2,1,0:T(8,128)}, f32[8,128]{1,0:T(8,128)S(1)}) custom-call(bf16[4,1024,544]{2,1,0:T(8,128)(2,1)} %copy-done.1, bf16[544,1024]{1,0:T(8,128)(2,1)} %o0_ref.1, bf16[544,1024]{1,0:T(8,128)(2,1)} %collective-permute-done.8.o1_ref, bf16[544,1024]{1,0:T(8,128)(2,1)} %collective-permute-done.9.o2_ref, ...), custom_call_target="tpu_custom_call" | custom-call | tf_op jit(solution)/shard_map/pallas_call | solution.py:111
  119.6 3.8 %collective-permute-start.12 = (f32[8,128]{1,0:T(8,128)S(1)}, f32[8,128]{1,0:T(8,128)S(1)}, u32[]{:S(2)}, u32[]{:S(2)}) collective-permute-start(f32[8,128]{1,0:T(8,128)S(1)} %add.95), channel_id=1, source_target_pairs={{0,4},{1,5},{2,6},{3,7},{4,0},{5,1},{6,2},{7,3},{8,12},{9,13},{10,... | collective-permute-start | bytes 12296 | tf_op jit(solution)/shard_map/ppermute | solution.py:36
  124.5 3.0 %collective-permute-start.14 = (f32[8,128]{1,0:T(8,128)S(1)}, f32[8,128]{1,0:T(8,128)S(1)}, u32[]{:S(2)}, u32[]{:S(2)}) collective-permute-start(f32[8,128]{1,0:T(8,128)S(1)} %add.95), channel_id=1, source_target_pairs={{0,6},{1,7},{2,0},{3,1},{4,2},{5,3},{6,4},{7,5},{8,14},{9,15},{10,... | collective-permute-start | bytes 12296 | tf_op jit(solution)/shard_map/ppermute | solution.py:36
  129.8 11.4 %shard_map.78 = f32[8,136,1024]{2,1,0:T(8,128)} custom-call(f32[8,128]{1,0:T(8,128)} %add_add_fusion.1.gram_ref, f32[8,4,128,1024]{3,2,1,0:T(8,128)} %get-tuple-element.9.grads_ref), custom_call_target="tpu_custom_call" | custom-call | tf_op jit(solution)/shard_map/pallas_call | solution.py:183
  143.9 31.3 %all_to_all.5 = f16[8,136,1024]{2,1,0:T(8,128)(2,1)S(1)} all-to-all(f16[8,136,1024]{2,1,0:T(8,128)(2,1)S(1)} %convert_element_type.12), channel_id=1, replica_groups={{0,8,16,24,32,40,48,56},{64,72,80,88,96,104,112,120},{128,136,144,152,1..., dimensions={0} | all-to-all | bytes 4456448 | tf_op jit(solution)/shard_map/all_to_all | solution.py:343
  180.3 3.0 %collective-permute-start.16 = (f32[40,128]{1,0:T(8,128)S(1)}, f32[40,128]{1,0:T(8,128)S(1)}, u32[]{:S(2)}, u32[]{:S(2)}) collective-permute-start(f32[40,128]{1,0:T(8,128)S(1)} %add.102), channel_id=1, source_target_pairs={{0,4},{1,5},{2,6},{3,7},{4,0},{5,1},{6,2},{7,3},{8,12},{9,13},{10,... | collective-permute-start | bytes 61448 | tf_op jit(solution)/shard_map/ppermute | solution.py:36
  196.6 3.0 %collective-permute-done.26 = bf16[128,1024]{1,0:T(8,128)(2,1)S(1)} collective-permute-done((bf16[128,1024]{1,0:T(8,128)(2,1)S(1)}, bf16[128,1024]{1,0:T(8,128)(2,1)S(1)}, u32[]{:S(2)}, u32[]{:S(2)}) %collective-permute-start.26) | collective-permute-done | bytes 262176 | tf_op jit(solution)/shard_map/ppermute | solution.py:28
  199.6 3.0 %collective-permute-start.27 = (bf16[128,1024]{1,0:T(8,128)(2,1)S(1)}, bf16[128,1024]{1,0:T(8,128)(2,1)S(1)}, u32[]{:S(2)}, u32[]{:S(2)}) collective-permute-start(bf16[128,1024]{1,0:T(8,128)(2,1)S(1)} %collective-permute-done.26), channel_id=1, source_target_pairs={{0,64},{8,72},{16,80},{24,88},{32,96},{40,104},{48,112},{56,120},{... | collective-permute-start | bytes 786440 | tf_op jit(solution)/shard_map/ppermute | solution.py:28
  208.3 3.0 %collective-permute-start.22 = (bf16[512,1024]{1,0:T(8,128)(2,1)S(1)}, bf16[512,1024]{1,0:T(8,128)(2,1)S(1)}, u32[]{:S(2)}, u32[]{:S(2)}) collective-permute-start(bf16[512,1024]{1,0:T(8,128)(2,1)S(1)} %constant_dynamic-update-slice_fusion.refs_0_), channel_id=1, source_target_pairs={{0,64},{8,72},{16,80},{24,88},{32,96},{40,104},{48,112},{56,120},{... | collective-permute-start | bytes 3145736 | tf_op jit(solution)/shard_map/ppermute | solution.py:28
  212.7 29.9 %collective-permute-done.29 = bf16[128,1024]{1,0:T(8,128)(2,1)S(1)} collective-permute-done((bf16[128,1024]{1,0:T(8,128)(2,1)S(1)}, bf16[128,1024]{1,0:T(8,128)(2,1)S(1)}, u32[]{:S(2)}, u32[]{:S(2)}) %collective-permute-start.29) | collective-permute-done | bytes 262176 | tf_op jit(solution)/shard_map/ppermute | solution.py:28
  248.5 17.8 %collective-permute-done.30.refs_2_ = bf16[512,1024]{1,0:T(8,128)(2,1)S(1)} collective-permute-done((bf16[512,1024]{1,0:T(8,128)(2,1)S(1)}, bf16[512,1024]{1,0:T(8,128)(2,1)S(1)}, u32[]{:S(2)}, u32[]{:S(2)}) %collective-permute-start.30) | collective-permute-done | bytes 1048608 | tf_op jit(solution)/shard_map/ppermute | solution.py:28
  277.9 3.0 %shard_map.82.refs_4_ = f32[544,1024]{1,0:T(8,128)S(1)} custom-call(s32[3]{0:T(128)S(1)} %pad_add_fusion.1.place, bf16[544,4096]{1,0:T(8,128)(2,1)S(1)} %copy-done, bf16[512,1024]{1,0:T(8,128)(2,1)S(1)} %collective-permute-done.22.refs_0_, bf16[512,1024]{1,0:T(8,128)(2,1)S(1)} %collective-permute-done.24.refs_1_, ...), custom_call_target="tpu_custom_call" | custom-call | tf_op jit(solution)/shard_map/pallas_call | solution.py:294
  283.3 3.9 %shard_map.83 = bf16[544,1024]{1,0:T(8,128)(2,1)} custom-call(s32[3]{0:T(128)S(1)} %pad_add_fusion.1.place, bf16[544,4096]{1,0:T(8,128)(2,1)S(1)} %copy-done, bf16[256,1024]{1,0:T(8,128)(2,1)} %collective-permute-done.23.refs_0_, bf16[256,1024]{1,0:T(8,128)(2,1)} %collective-permute-done.25.refs_1_, bf16[256,1024]{1,0:T(8,128)(2,1)} %collective-permute-done.31.refs_2_, ...), custom_call_target="tpu_custom_call" | custom-call | tf_op jit(solution)/shard_map/pallas_call | solution.py:294
  (104 shorter events, 66.4 us)
Async XLA Ops:
  2.1 7.8 %collective-permute-start.1 = (bf16[544,128]{1,0:T(8,128)(2,1)S(1)}, bf16[544,128]{1,0:T(8,128)(2,1)S(1)}, u32[]{:S(2)}, u32[]{:S(2)}) collective-permute-start(bf16[544,128]{1,0:T(8,128)(2,1)S(1)} %get-tuple-element.14), channel_id=1, source_target_pairs={{0,128},{8,136},{16,144},{24,152},{32,160},{40,168},{48,176},{56,1... | collective-permute-start | bytes 417800 | tf_op jit(solution)/shard_map/ppermute | solution.py:28
  11.9 18.9 %collective-permute-start.3 = (bf16[3,544,128]{2,1,0:T(8,128)(2,1)S(1)}, bf16[3,544,128]{2,1,0:T(8,128)(2,1)S(1)}, u32[]{:S(2)}, u32[]{:S(2)}) collective-permute-start(bf16[3,544,128]{2,1,0:T(8,128)(2,1)S(1)} %get-tuple-element.17), channel_id=1, source_target_pairs={{0,2},{1,3},{2,4},{3,5},{4,6},{5,7},{6,0},{7,1},{8,10},{9,11},{10,... | collective-permute-start | bytes 1253384 | tf_op jit(solution)/shard_map/ppermute | solution.py:36
  15.3 22.2 %collective-permute-start.5 = (bf16[3,544,128]{2,1,0:T(8,128)(2,1)S(1)}, bf16[3,544,128]{2,1,0:T(8,128)(2,1)S(1)}, u32[]{:S(2)}, u32[]{:S(2)}) collective-permute-start(bf16[3,544,128]{2,1,0:T(8,128)(2,1)S(1)} %get-tuple-element.17), channel_id=1, source_target_pairs={{0,6},{1,7},{2,0},{3,1},{4,2},{5,3},{6,4},{7,5},{8,14},{9,15},{10,... | collective-permute-start | bytes 1253384 | tf_op jit(solution)/shard_map/ppermute | solution.py:36
  30.8 14.6 %collective-permute-start.4 = (bf16[3,272,128]{2,1,0:T(8,128)(2,1)S(1)}, bf16[3,272,128]{2,1,0:T(8,128)(2,1)S(1)}, u32[]{:S(2)}, u32[]{:S(2)}) collective-permute-start(bf16[3,272,128]{2,1,0:T(8,128)(2,1)S(1)} %slice.36), channel_id=1, source_target_pairs={{0,2},{1,3},{2,4},{3,5},{4,6},{5,7},{6,0},{7,1},{8,10},{9,11},{10,... | collective-permute-start | bytes 626696 | tf_op jit(solution)/shard_map/ppermute | solution.py:36
  37.5 12.2 %collective-permute-start.6 = (bf16[3,272,128]{2,1,0:T(8,128)(2,1)S(1)}, bf16[3,272,128]{2,1,0:T(8,128)(2,1)S(1)}, u32[]{:S(2)}, u32[]{:S(2)}) collective-permute-start(bf16[3,272,128]{2,1,0:T(8,128)(2,1)S(1)} %slice.37), channel_id=1, source_target_pairs={{0,6},{1,7},{2,0},{3,1},{4,2},{5,3},{6,4},{7,5},{8,14},{9,15},{10,... | collective-permute-start | bytes 626696 | tf_op jit(solution)/shard_map/ppermute | solution.py:36
  50.1 52.4 %collective-permute-start.10 = (bf16[544,1024]{1,0:T(8,128)(2,1)}, bf16[544,1024]{1,0:T(8,128)(2,1)}, u32[]{:S(2)}, u32[]{:S(2)}) collective-permute-start(bf16[544,1024]{1,0:T(8,128)(2,1)} %o0_ref.1), channel_id=1, source_target_pairs={{0,192},{8,200},{16,208},{24,216},{32,224},{40,232},{48,240},{56,2... | collective-permute-start | bytes 3342344 | tf_op jit(solution)/shard_map/ppermute | solution.py:28
  50.6 51.9 %collective-permute-start.8 = (bf16[544,1024]{1,0:T(8,128)(2,1)}, bf16[544,1024]{1,0:T(8,128)(2,1)}, u32[]{:S(2)}, u32[]{:S(2)}) collective-permute-start(bf16[544,1024]{1,0:T(8,128)(2,1)} %o0_ref.1), channel_id=1, source_target_pairs={{0,64},{8,72},{16,80},{24,88},{32,96},{40,104},{48,112},{56,120},{... | collective-permute-start | bytes 3342344 | tf_op jit(solution)/shard_map/ppermute | solution.py:28
  53.4 49.1 %collective-permute-start.9 = (bf16[544,1024]{1,0:T(8,128)(2,1)}, bf16[544,1024]{1,0:T(8,128)(2,1)}, u32[]{:S(2)}, u32[]{:S(2)}) collective-permute-start(bf16[544,1024]{1,0:T(8,128)(2,1)} %o0_ref.1), channel_id=1, source_target_pairs={{0,128},{8,136},{16,144},{24,152},{32,160},{40,168},{48,176},{56,1... | collective-permute-start | bytes 3342344 | tf_op jit(solution)/shard_map/ppermute | solution.py:28
  119.6 8.0 %collective-permute-start.12 = (f32[8,128]{1,0:T(8,128)S(1)}, f32[8,128]{1,0:T(8,128)S(1)}, u32[]{:S(2)}, u32[]{:S(2)}) collective-permute-start(f32[8,128]{1,0:T(8,128)S(1)} %add.95), channel_id=1, source_target_pairs={{0,4},{1,5},{2,6},{3,7},{4,0},{5,1},{6,2},{7,3},{8,12},{9,13},{10,... | collective-permute-start | bytes 12296 | tf_op jit(solution)/shard_map/ppermute | solution.py:36
  180.3 7.7 %collective-permute-start.16 = (f32[40,128]{1,0:T(8,128)S(1)}, f32[40,128]{1,0:T(8,128)S(1)}, u32[]{:S(2)}, u32[]{:S(2)}) collective-permute-start(f32[40,128]{1,0:T(8,128)S(1)} %add.102), channel_id=1, source_target_pairs={{0,4},{1,5},{2,6},{3,7},{4,0},{5,1},{6,2},{7,3},{8,12},{9,13},{10,... | collective-permute-start | bytes 61448 | tf_op jit(solution)/shard_map/ppermute | solution.py:36
  193.1 11.8 %collective-permute-start.19 = (bf16[128,1024]{1,0:T(8,128)(2,1)S(1)}, bf16[128,1024]{1,0:T(8,128)(2,1)S(1)}, u32[]{:S(2)}, u32[]{:S(2)}) collective-permute-start(bf16[128,1024]{1,0:T(8,128)(2,1)S(1)} %get-tuple-element.12), channel_id=1, source_target_pairs={{0,16},{8,24},{16,32},{24,40},{32,48},{40,56},{48,0},{56,8},{64,80... | collective-permute-start | bytes 786440 | tf_op jit(solution)/shard_map/ppermute | solution.py:28
  195.2 10.6 %collective-permute-start.20 = (bf16[128,1024]{1,0:T(8,128)(2,1)S(1)}, bf16[128,1024]{1,0:T(8,128)(2,1)S(1)}, u32[]{:S(2)}, u32[]{:S(2)}) collective-permute-start(bf16[128,1024]{1,0:T(8,128)(2,1)S(1)} %get-tuple-element.12), channel_id=1, source_target_pairs={{0,32},{8,40},{16,48},{24,56},{32,0},{40,8},{48,16},{56,24},{64,96... | collective-permute-start | bytes 786440 | tf_op jit(solution)/shard_map/ppermute | solution.py:28
  195.3 13.0 %collective-permute-start.21 = (bf16[128,1024]{1,0:T(8,128)(2,1)S(1)}, bf16[128,1024]{1,0:T(8,128)(2,1)S(1)}, u32[]{:S(2)}, u32[]{:S(2)}) collective-permute-start(bf16[128,1024]{1,0:T(8,128)(2,1)S(1)} %get-tuple-element.12), channel_id=1, source_target_pairs={{0,48},{8,56},{16,0},{24,8},{32,16},{40,24},{48,32},{56,40},{64,11... | collective-permute-start | bytes 786440 | tf_op jit(solution)/shard_map/ppermute | solution.py:28
  199.6 13.0 %collective-permute-start.27 = (bf16[128,1024]{1,0:T(8,128)(2,1)S(1)}, bf16[128,1024]{1,0:T(8,128)(2,1)S(1)}, u32[]{:S(2)}, u32[]{:S(2)}) collective-permute-start(bf16[128,1024]{1,0:T(8,128)(2,1)S(1)} %collective-permute-done.26), channel_id=1, source_target_pairs={{0,64},{8,72},{16,80},{24,88},{32,96},{40,104},{48,112},{56,120},{... | collective-permute-start | bytes 786440 | tf_op jit(solution)/shard_map/ppermute | solution.py:28
  202.6 10.1 %collective-permute-start.28 = (bf16[128,1024]{1,0:T(8,128)(2,1)S(1)}, bf16[128,1024]{1,0:T(8,128)(2,1)S(1)}, u32[]{:S(2)}, u32[]{:S(2)}) collective-permute-start(bf16[128,1024]{1,0:T(8,128)(2,1)S(1)} %collective-permute-done.26), channel_id=1, source_target_pairs={{0,128},{8,136},{16,144},{24,152},{32,160},{40,168},{48,176},{56,1... | collective-permute-start | bytes 786440 | tf_op jit(solution)/shard_map/ppermute | solution.py:28
  208.3 36.4 %collective-permute-start.22 = (bf16[512,1024]{1,0:T(8,128)(2,1)S(1)}, bf16[512,1024]{1,0:T(8,128)(2,1)S(1)}, u32[]{:S(2)}, u32[]{:S(2)}) collective-permute-start(bf16[512,1024]{1,0:T(8,128)(2,1)S(1)} %constant_dynamic-update-slice_fusion.refs_0_), channel_id=1, source_target_pairs={{0,64},{8,72},{16,80},{24,88},{32,96},{40,104},{48,112},{56,120},{... | collective-permute-start | bytes 3145736 | tf_op jit(solution)/shard_map/ppermute | solution.py:28
  211.3 34.3 %collective-permute-start.24 = (bf16[512,1024]{1,0:T(8,128)(2,1)S(1)}, bf16[512,1024]{1,0:T(8,128)(2,1)S(1)}, u32[]{:S(2)}, u32[]{:S(2)}) collective-permute-start(bf16[512,1024]{1,0:T(8,128)(2,1)S(1)} %constant_dynamic-update-slice_fusion.refs_0_), channel_id=1, source_target_pairs={{0,192},{8,200},{16,208},{24,216},{32,224},{40,232},{48,240},{56,2... | collective-permute-start | bytes 3145736 | tf_op jit(solution)/shard_map/ppermute | solution.py:28
  211.3 31.3 %collective-permute-start.29 = (bf16[128,1024]{1,0:T(8,128)(2,1)S(1)}, bf16[128,1024]{1,0:T(8,128)(2,1)S(1)}, u32[]{:S(2)}, u32[]{:S(2)}) collective-permute-start(bf16[128,1024]{1,0:T(8,128)(2,1)S(1)} %collective-permute-done.26), channel_id=1, source_target_pairs={{0,192},{8,200},{16,208},{24,216},{32,224},{40,232},{48,240},{56,2... | collective-permute-start | bytes 786440 | tf_op jit(solution)/shard_map/ppermute | solution.py:28
  242.6 23.6 %collective-permute-start.30 = (bf16[512,1024]{1,0:T(8,128)(2,1)S(1)}, bf16[512,1024]{1,0:T(8,128)(2,1)S(1)}, u32[]{:S(2)}, u32[]{:S(2)}) collective-permute-start(bf16[512,1024]{1,0:T(8,128)(2,1)S(1)} %constant_dynamic-update-slice_fusion.4.refs_1_), channel_id=1, source_target_pairs={{0,16},{8,24},{16,32},{24,40},{32,48},{40,56},{48,0},{56,8},{64,80... | collective-permute-start | bytes 3145736 | tf_op jit(solution)/shard_map/ppermute | solution.py:28
  242.7 25.9 %collective-permute-start.32 = (bf16[512,1024]{1,0:T(8,128)(2,1)S(1)}, bf16[512,1024]{1,0:T(8,128)(2,1)S(1)}, u32[]{:S(2)}, u32[]{:S(2)}) collective-permute-start(bf16[512,1024]{1,0:T(8,128)(2,1)S(1)} %constant_dynamic-update-slice_fusion.4.refs_1_), channel_id=1, source_target_pairs={{0,48},{8,56},{16,0},{24,8},{32,16},{40,24},{48,32},{56,40},{64,11... | collective-permute-start | bytes 3145736 | tf_op jit(solution)/shard_map/ppermute | solution.py:28
  245.6 35.4 %collective-permute-start.23 = (bf16[256,1024]{1,0:T(8,128)(2,1)}, bf16[256,1024]{1,0:T(8,128)(2,1)}, u32[]{:S(2)}, u32[]{:S(2)}) collective-permute-start(bf16[256,1024]{1,0:T(8,128)(2,1)} %slice.41), channel_id=1, source_target_pairs={{0,64},{8,72},{16,80},{24,88},{32,96},{40,104},{48,112},{56,120},{... | collective-permute-start | bytes 1572872 | tf_op jit(solution)/shard_map/ppermute | solution.py:28
  246.4 34.5 %collective-permute-start.25 = (bf16[256,1024]{1,0:T(8,128)(2,1)}, bf16[256,1024]{1,0:T(8,128)(2,1)}, u32[]{:S(2)}, u32[]{:S(2)}) collective-permute-start(bf16[256,1024]{1,0:T(8,128)(2,1)} %slice.42), channel_id=1, source_target_pairs={{0,192},{8,200},{16,208},{24,216},{32,224},{40,232},{48,240},{56,2... | collective-permute-start | bytes 1572872 | tf_op jit(solution)/shard_map/ppermute | solution.py:28
  267.1 13.9 %collective-permute-start.31 = (bf16[256,1024]{1,0:T(8,128)(2,1)}, bf16[256,1024]{1,0:T(8,128)(2,1)}, u32[]{:S(2)}, u32[]{:S(2)}) collective-permute-start(bf16[256,1024]{1,0:T(8,128)(2,1)} %slice.43), channel_id=1, source_target_pairs={{0,16},{8,24},{16,32},{24,40},{32,48},{40,56},{48,0},{56,8},{64,80... | collective-permute-start | bytes 1572872 | tf_op jit(solution)/shard_map/ppermute | solution.py:28
  270.4 12.9 %collective-permute-start.33 = (bf16[256,1024]{1,0:T(8,128)(2,1)}, bf16[256,1024]{1,0:T(8,128)(2,1)}, u32[]{:S(2)}, u32[]{:S(2)}) collective-permute-start(bf16[256,1024]{1,0:T(8,128)(2,1)} %slice.44), channel_id=1, source_target_pairs={{0,48},{8,56},{16,0},{24,8},{32,16},{40,24},{48,32},{56,40},{64,11... | collective-permute-start | bytes 1572872 | tf_op jit(solution)/shard_map/ppermute | solution.py:28
  (21 other events, 177.7 us)

commit v2 on v1

--- a/solution.py
+++ b/solution.py
@@ -147,7 +147,7 @@
     s = [
         jnp.sum(jnp.where(here, w[k] * (1.0 / tok_dev), 0.0), axis=1, keepdims=True)[:1] for k in range(4)
     ]
-    span = 256
+    span = 128
     for first in range(0, grads_ref.shape[3], span):
         lanes = pl.ds(first, span)
         mixed = (s[0] * grads_ref[0, 0, :, lanes] + s[2] * grads_ref[0, 2, :, lanes]) + (
@@ -275,49 +275,101 @@
     )(gram, parts, weight, momentum)
 
 
-def project_kernel(sets, last, place, left_ref, *refs):
-    held, (start_ref, out_ref) = refs[: len(sets)], refs[len(sets) :]
-    total = start_ref[...]
-    for offsets, ref in zip(sets, held):
-        parts = []
-        for j, i, e in offsets:
-            block = (lax.rem(place[0] - j + NY, NY) * NX + lax.rem(place[1] - i + NX, NX)) * NZ + lax.rem(
-                place[2] + e, NZ
-            )
-            parts.append(left_ref[:, pl.ds(pl.multiple_of(block * BLK, BLK), BLK)])
-        total = total + jnp.dot(jnp.concatenate(parts, 1), ref[...], preferred_element_type=F32)
-    out_ref[...] = total.astype(out_ref.dtype)
-
-
-def project(place, left, sets, held, start, last):
-    vmem = pl.BlockSpec(memory_space=pltpu.VMEM)
-    return pl.pallas_call(
-        functools.partial(project_kernel, sets, last),
-        in_specs=[pl.BlockSpec(memory_space=pltpu.SMEM)] + [vmem] * (len(held) + 2),
-        out_specs=vmem,
-        out_shape=jax.ShapeDtypeStruct(start.shape, jnp.bfloat16 if last else F32),
+def depth_block(place, j, i, e):
+    y, x, z = place[0], place[1], place[2]
+    return (lax.rem(y - j + NY, NY) * NX + lax.rem(x - i + NX, NX)) * NZ + lax.rem(z + e, NZ)
+
+
+def project_kernel(units, last, place, *refs):
+    mine, other = refs[:NX], refs[NX : 2 * NX]
+    held, start_ref = refs[2 * NX : 2 * NX + units], refs[2 * NX + units]
+    rest = refs[2 * NX + units + 1 :]
+    total_ref = rest[-1] if last else rest[0]
+    step = pl.program_id(0)
+
+    @pl.when(step == 0)
+    def _():
+        total_ref[...] = start_ref[...]
+
+    unit = held[0][...]
+    for u in range(1, units):
+        unit = jnp.where(step == u, held[u][...], unit)
+    rows = total_ref.shape[1]
+    for side, refs_of in enumerate((mine, other)):
+        left = jnp.concatenate([ref[...] for ref in refs_of], 1)
+        total_ref[side] += jnp.dot(left, unit, preferred_element_type=F32)
+
+    if last:
+
+        @pl.when(step == units - 1)
+        def _():
+            part = rows // NX
+            for k in range(NX):
+                first = pl.multiple_of(lax.rem(place[1] + k, NX) * part, part)
+                rest[k][...] = total_ref[:, pl.ds(first, part), :].astype(rest[k].dtype)
+
+
+def project(place, mine, other, held, start, first, stride, last):
+    units = len(held)
+    rows, cols = start.shape[1:]
+    left = [
+        pl.BlockSpec(
+            (rows, BLK),
+            lambda u, p, i=i: (0, depth_block(p, first[0] + u * stride[0], i, first[1] + u * stride[1])),
+        )
+        for i in range(NX)
+    ]
+    whole = lambda shape: pl.BlockSpec(shape, lambda u, p: (0,) * len(shape))
+    part = (2, rows // NX, cols)
+    return pl.pallas_call(
+        functools.partial(project_kernel, units, last),
+        grid_spec=pltpu.PrefetchScalarGridSpec(
+            num_scalar_prefetch=1,
+            grid=(units,),
+            in_specs=left + left + [whole(h.shape) for h in held] + [whole(start.shape)],
+            out_specs=[whole(part)] * NX if last else whole(start.shape),
+            scratch_shapes=[pltpu.VMEM(start.shape, F32)] if last else [],
+        ),
+        out_shape=[jax.ShapeDtypeStruct(part, jnp.bfloat16)] * NX if last else jax.ShapeDtypeStruct(start.shape, F32),
         compiler_params=pltpu.CompilerParams(vmem_limit_bytes=40 * 2**20),
-    )(place, left, *held, start)
-
-
-def gather_and_project(place, own, next_tokens):
-    partner = move_dp(own, dz=1)
-    a = [own] + [move_dp(own, dx=k) for k in (1, 2, 3)]
-    b = [partner] + [move_dp(partner, dy=k) for k in (1, 2, 3)]
-    a = jnp.concatenate(a, 0)
-    b = jnp.concatenate(b, 0)
-    half = a.shape[0] // 2
-    a1, a3, b1, b3 = move_dp(a, dy=1), move_dp(a, dy=3), move_dp(b, dx=1), move_dp(b, dx=3)
-    row_a = lambda j: [(j, i, 0) for i in range(NX)]
-    row_b = lambda i: [(j, i, 1) for j in range(NY)]
-    total = jnp.zeros((next_tokens.shape[0], own.shape[1]), F32)
-    total = project(place, next_tokens, [row_a(0), row_b(0)], [a, b], total, False)
-    a2 = [move_dp(a1[:half], dy=1), move_dp(a3[half:], dy=3)]
-    b2 = [move_dp(b1[:half], dx=1), move_dp(b3[half:], dx=3)]
-    sets = [row_a(1), row_a(3), row_b(1), row_b(3)]
-    total = project(place, next_tokens, sets, [a1, a3, b1, b3], total, False)
-    sets = [row_a(2)[:2], row_a(2)[2:], row_b(2)[:2], row_b(2)[2:]]
-    return project(place, next_tokens, sets, a2 + b2, total, True)
+    )(place, *([mine] * NX), *([other] * NX), *held, start)
+
+
+def assemble_kernel(place, p0_ref, p1_ref, p2_ref, p3_ref, out_ref):
+    _, part, cols = p0_ref.shape
+    for k, ref in enumerate((p0_ref, p1_ref, p2_ref, p3_ref)):
+        column = pl.multiple_of(lax.rem(place[1] - k + NX, NX) * cols, cols)
+        for side in range(2):
+            core = place[3] if side == 0 else 1 - place[3]
+            row = pl.multiple_of(core * part, 16)
+            out_ref[pl.ds(row, part), pl.ds(column, cols)] = ref[side]
+
+
+def assemble(place, parts):
+    _, part, cols = parts[0].shape
+    return pl.pallas_call(
+        assemble_kernel,
+        in_specs=[pl.BlockSpec(memory_space=pltpu.SMEM)] + [pl.BlockSpec(memory_space=pltpu.VMEM)] * NX,
+        out_specs=pl.BlockSpec(memory_space=pltpu.VMEM),
+        out_shape=jax.ShapeDtypeStruct((2 * part, NX * cols), jnp.bfloat16),
+    )(place, *parts)
+
+
+def gather_and_project(place, own, mine, other):
+    cols = own.shape[1] // NX
+    x = place[1]
+    pieces = [lax.dynamic_slice_in_dim(own, ((x + k) % NX) * cols, cols, 1) for k in range(NX)]
+    unit = jnp.concatenate([pieces[0]] + [move_dp(pieces[k], dx=k) for k in (1, 2, 3)], 0)
+    partner = move_dp(unit, dz=1)
+    own_ring = [move_dp(unit, dy=k) for k in (1, 2, 3)]
+    own_ring, partner = lax.optimization_barrier((own_ring, partner))
+    far_ring = [move_dp(partner, dy=k) for k in (1, 2, 3)]
+    total = jnp.zeros((2, mine.shape[0], cols), F32)
+    total = project(place, mine, other, [unit, partner], total, (0, 0), (0, 1), False)
+    total = project(place, mine, other, own_ring, total, (1, 0), (1, 0), False)
+    total, far_ring = lax.optimization_barrier((total, far_ring))
+    parts = project(place, mine, other, far_ring, total, (1, 1), (1, 0), True)
+    return assemble(place, [parts[0]] + [move_dp(parts[k], dx=k) for k in (1, 2, 3)])
 
 
 def shards(tokens, out_grad, weight, momentum, next_tokens):
@@ -325,25 +377,34 @@
     y, x, z = dp // (NX * NZ), dp // NZ % NX, dp % NZ
     tok_dev = tokens.shape[0]
     group = NX * NZ
+    here = jnp.stack([y, x, z, mp % NC]).astype(jnp.int32)
+    next_half = lax.dynamic_slice_in_dim(next_tokens, (mp % NC) * (tok_dev // 2), tok_dev // 2, 0)
+    x_rings = [[(a * NX + k) * NZ + b for k in range(NX)] for a in range(NY) for b in range(NZ)]
+    next_mine = lax.all_gather(next_half, "dp", axis_index_groups=x_rings, tiled=True)
     sent = []
     for k in (1, 2, 3):
         first = (((y + k) % NY) * group + mp) * BLK
         sent.append(move_dp(lax.dynamic_slice_in_dim(tokens, first, BLK, 1), dy=k))
-    outs = [out_grad] + [move_dp(out_grad, dy=k) for k in (1, 2, 3)]
+    sent, out_grad = lax.optimization_barrier((sent, out_grad))
+    outs = [move_dp(out_grad, dy=k) for k in (1, 2, 3)]
     piece = jnp.stack(sent)
     up, down = move_mp(piece, dh=1), move_mp(piece, dh=3)
     half = tok_dev // 2
     far = jnp.concatenate([move_mp(up[:, :half], dh=1), move_mp(down[:, half:], dh=3)], 1)
+    up, down, far, outs = lax.optimization_barrier((up, down, far, outs))
     mine = jnp.stack([piece, up, far, down])
     other = move_mp(mine, dc=1)
     place = jnp.stack([y, mp // NC, mp % NC]).astype(jnp.int32)
-    grads, gram = grads_and_gram(turn(place, tokens, mine, other), outs)
+    grads, gram = grads_and_gram(turn(place, tokens, mine, other), [out_grad] + outs)
     coded = mix(sum_mp(gram), grads, tok_dev).astype(jnp.float16)
     rings = [[ring * group + k for k in range(group)] for ring in range(NY)]
-    parts = decode(lax.all_to_all(coded, "dp", 0, 0, axis_index_groups=rings))
+    coded, next_mine = lax.optimization_barrier((coded, next_mine))
+    next_other = move_mp(next_mine, dc=1)
+    landed = lax.all_to_all(coded, "dp", 0, 0, axis_index_groups=rings)
+    landed, next_other = lax.optimization_barrier((landed, next_other))
+    parts = decode(landed)
     new_weight, new_momentum, weight_half = update(sum_mp(gram8(parts)), parts, weight, momentum)
-    here = jnp.stack([y, x, z]).astype(jnp.int32)
-    projected = gather_and_project(here, weight_half, next_tokens)
+    projected = gather_and_project(here, weight_half, next_mine, next_other)
     return (new_weight, new_momentum, projected)
 
 

time: 288 us -> 259 us (0.90)
  waiting for transfers between devices: 137 us -> 77.8 us
  between operations: 1 us -> 14.4 us
  Pallas kernels: 43 us -> 51.7 us
  local copies, waits for them, and re-layouts: 15.2 us -> 21.6 us
    ppermute x21 -> x19, waiting for transfers between devices: 108 us -> 39.2 us  [move_dp(): return lax.ppermute(block, 'dp', route)]
    ppermute x13 -> x14, waiting for transfers between devices: 28.6 us -> 38.5 us  [move_mp(): return lax.ppermute(block, 'mp', route)]
    pallas_call x3 -> x4, Pallas kernels: 8.8 us -> 17.6 us  [the longest x3 15.3 us: project(): pl.pallas_call(functools.partial(project_kernel, units, last), grid_spec=...]
    unnamed x29 -> x41, local copies, waits for them, and re-layouts: 10.4 us -> 17 us
    slice x4 -> x0, local copies, waits for them, and re-layouts: 3.4 us -> none  [the longest x2 1.7 us: gather_and_project(): a2 = [move_dp(a1[:half], dy=1), move_dp(a3[half:], dy=3)]]
    dynamic_slice x0 -> x2, local copies, waits for them, and re-layouts: none -> 3.35 us  [the longest x1 3.32 us: shards(): lax.dynamic_slice_in_dim(next_tokens, mp % NC * (tok_dev // 2), tok_dev /...]
    ppermute x21 -> x19, starting transfers between devices: 23.1 us -> 20.3 us  [move_dp(): return lax.ppermute(block, 'dp', route)]
    ppermute x13 -> x14, starting transfers between devices: 30.8 us -> 32.2 us  [move_mp(): return lax.ppermute(block, 'mp', route)]
  transfers between devices with their start and end apart: 34 -> 34, of which waited for: 22 -> 21; matrix products, arithmetic and copies ran while one was open for 1% -> 2% of each run, Pallas kernels for 3% -> 16%
where the time goes in v2:
time: 259 us; the launch traced here: 256 us
  waiting for transfers between devices  77.8 us (30%)
  starting transfers between devices  52.5 us (20%)
  Pallas kernels  51.7 us (20%)
  blocking collectives  31.9 us (12%)
  local copies, waits for them, and re-layouts  21.6 us (8%)
  between operations  14.4 us (6%)
  other arithmetic  6.1 us (2%)
    ppermute x19, waiting for transfers between devices, move_dp(): return lax.ppermute(block, 'dp', route)  39.2 us
    ppermute x14, waiting for transfers between devices, move_mp(): return lax.ppermute(block, 'mp', route)  38.5 us
    ppermute x14, starting transfers between devices, move_mp(): return lax.ppermute(block, 'mp', route)  32.2 us
    all_to_all x1, blocking collectives, shards(): landed = lax.all_to_all(coded, 'dp', 0, 0, axis_index_groups=rings)  31.9 us
    ppermute x19, starting transfers between devices, move_dp(): return lax.ppermute(block, 'dp', route)  20.3 us
    unnamed x41, local copies, waits for them, and re-layouts  17 us
    pallas_call x1, Pallas kernels, grads_and_gram(): pl.pallas_call(grads_kernel, grid=(cols // span,), in_specs=[pl.BlockSpec...  15.9 us
    pallas_call x3, Pallas kernels, project(): pl.pallas_call(functools.partial(project_kernel, units, last), grid_spec=...  15.3 us
  transfers between devices with their start and end apart: 34, of which 21 were waited for; matrix products, arithmetic and copies ran while one was open for 2% of the time, Pallas kernels for 16%

profile of v2, /device:TPU:30, one launch (start us, length us, event | category | flops | bytes accessed | tf_op | source)
XLA Modules:
  0.0 256.0 jit_solution(8081281984914400553)
XLA Ops:
  7.2 3.3 %constant_dynamic-slice_fusion.4 = bf16[272,4096]{1,0:T(8,128)(2,1)} fusion(bf16[544,4096]{1,0:T(8,128)(2,1)} %param.9, s32[]{:T(128)S(6)} %select_n.94), kind=kLoop, calls=%fused_computation.25 | loop fusion | bytes 4456452 | tf_op jit(solution)/shard_map/dynamic_slice | solution.py:381
  14.6 3.7 %collective-permute-done = bf16[544,128]{1,0:T(8,128)(2,1)S(1)} collective-permute-done((bf16[544,128]{1,0:T(8,128)(2,1)S(1)}, bf16[544,128]{1,0:T(8,128)(2,1)S(1)}, u32[]{:S(2)}, u32[]{:S(2)}) %collective-permute-start) | collective-permute-done | bytes 139296 | tf_op jit(solution)/shard_map/ppermute | solution.py:28
  25.1 6.4 %collective-permute-start.4 = (bf16[3,544,128]{2,1,0:T(8,128)(2,1)S(1)}, bf16[3,544,128]{2,1,0:T(8,128)(2,1)S(1)}, u32[]{:S(2)}, u32[]{:S(2)}) collective-permute-start(bf16[3,544,128]{2,1,0:T(8,128)(2,1)S(1)} %get-tuple-element.69), channel_id=1, source_target_pairs={{0,6},{1,7},{2,0},{3,1},{4,2},{5,3},{6,4},{7,5},{8,14},{9,15},{10,... | collective-permute-start | bytes 1253384 | tf_op jit(solution)/shard_map/ppermute | solution.py:36
  31.5 16.5 %collective-permute-done.4 = bf16[3,544,128]{2,1,0:T(8,128)(2,1)S(1)} collective-permute-done((bf16[3,544,128]{2,1,0:T(8,128)(2,1)S(1)}, bf16[3,544,128]{2,1,0:T(8,128)(2,1)S(1)}, u32[]{:S(2)}, u32[]{:S(2)}) %collective-permute-start.4) | collective-permute-done | bytes 417824 | tf_op jit(solution)/shard_map/ppermute | solution.py:36
  47.9 4.7 %collective-permute-start.6 = (bf16[3,272,128]{2,1,0:T(8,128)(2,1)S(1)}, bf16[3,272,128]{2,1,0:T(8,128)(2,1)S(1)}, u32[]{:S(2)}, u32[]{:S(2)}) collective-permute-start(bf16[3,272,128]{2,1,0:T(8,128)(2,1)S(1)} %slice.21), channel_id=1, source_target_pairs={{0,6},{1,7},{2,0},{3,1},{4,2},{5,3},{6,4},{7,5},{8,14},{9,15},{10,... | collective-permute-start | bytes 626696 | tf_op jit(solution)/shard_map/ppermute | solution.py:36
  52.8 5.8 %collective-permute-done.6 = bf16[3,272,128]{2,1,0:T(8,128)(2,1)S(1)} collective-permute-done((bf16[3,272,128]{2,1,0:T(8,128)(2,1)S(1)}, bf16[3,272,128]{2,1,0:T(8,128)(2,1)S(1)}, u32[]{:S(2)}, u32[]{:S(2)}) %collective-permute-start.6) | collective-permute-done | bytes 208928 | tf_op jit(solution)/shard_map/ppermute | solution.py:36
  58.5 5.6 %collective-permute-done.5 = bf16[3,272,128]{2,1,0:T(8,128)(2,1)S(1)} collective-permute-done((bf16[3,272,128]{2,1,0:T(8,128)(2,1)S(1)}, bf16[3,272,128]{2,1,0:T(8,128)(2,1)S(1)}, u32[]{:S(2)}, u32[]{:S(2)}) %collective-permute-start.5) | collective-permute-done | bytes 208928 | tf_op jit(solution)/shard_map/ppermute | solution.py:36
  66.2 7.3 %collective-permute-done.9.o3_ref = bf16[544,1024]{1,0:T(8,128)(2,1)S(1)} collective-permute-done((bf16[544,1024]{1,0:T(8,128)(2,1)S(1)}, bf16[544,1024]{1,0:T(8,128)(2,1)S(1)}, u32[]{:S(2)}, u32[]{:S(2)}) %collective-permute-start.9) | collective-permute-done | bytes 1114144 | tf_op jit(solution)/shard_map/ppermute | solution.py:28
  74.9 3.4 %collective-permute-done.10.other_ref = bf16[4,3,544,128]{3,2,1,0:T(8,128)(2,1)S(1)} collective-permute-done((bf16[4,3,544,128]{3,2,1,0:T(8,128)(2,1)S(1)}, bf16[4,3,544,128]{3,2,1,0:T(8,128)(2,1)S(1)}, u32[]{:S(2)}, u32[]{:S(2)}) %collective-permute-start.10) | collective-permute-done | bytes 1671200 | tf_op jit(solution)/shard_map/ppermute | solution.py:36
  85.9 15.9 %shard_map.77 = (f32[8,4,128,1024]{3,2,1,0:T(8,128)}, f32[8,128]{1,0:T(8,128)S(1)}) custom-call(bf16[4,1024,544]{2,1,0:T(8,128)(2,1)} %copy-done.3, bf16[544,1024]{1,0:T(8,128)(2,1)S(1)} %copy-done.6, bf16[544,1024]{1,0:T(8,128)(2,1)S(1)} %copy-done.8, bf16[544,1024]{1,0:T(8,128)(2,1)S(1)} %copy-done.10, bf16[544,1024]{1,0:T(8,128)(2,1)S(1)} %copy-done.12), custom_call_target="tpu_custom_call" | custom-call | tf_op jit(solution)/shard_map/pallas_call | solution.py:111
  103.0 3.3 %collective-permute-start.13 = (f32[8,128]{1,0:T(8,128)S(1)}, f32[8,128]{1,0:T(8,128)S(1)}, u32[]{:S(2)}, u32[]{:S(2)}) collective-permute-start(f32[8,128]{1,0:T(8,128)S(1)} %add.133), channel_id=1, source_target_pairs={{0,2},{1,3},{2,4},{3,5},{4,6},{5,7},{6,0},{7,1},{8,10},{9,11},{10,... | collective-permute-start | bytes 12296 | tf_op jit(solution)/shard_map/ppermute | solution.py:36
  106.3 3.0 %collective-permute-start.14 = (f32[8,128]{1,0:T(8,128)S(1)}, f32[8,128]{1,0:T(8,128)S(1)}, u32[]{:S(2)}, u32[]{:S(2)}) collective-permute-start(f32[8,128]{1,0:T(8,128)S(1)} %add.133), channel_id=1, source_target_pairs={{0,6},{1,7},{2,0},{3,1},{4,2},{5,3},{6,4},{7,5},{8,14},{9,15},{10,... | collective-permute-start | bytes 12296 | tf_op jit(solution)/shard_map/ppermute | solution.py:36
  109.3 5.0 %collective-permute-start.12 = (f32[8,128]{1,0:T(8,128)S(1)}, f32[8,128]{1,0:T(8,128)S(1)}, u32[]{:S(2)}, u32[]{:S(2)}) collective-permute-start(f32[8,128]{1,0:T(8,128)S(1)} %add.133), channel_id=1, source_target_pairs={{0,4},{1,5},{2,6},{3,7},{4,0},{5,1},{6,2},{7,3},{8,12},{9,13},{10,... | collective-permute-start | bytes 12296 | tf_op jit(solution)/shard_map/ppermute | solution.py:36
  117.4 11.4 %shard_map.78 = f32[8,136,1024]{2,1,0:T(8,128)} custom-call(f32[8,128]{1,0:T(8,128)} %add_add_fusion.1.gram_ref, f32[8,4,128,1024]{3,2,1,0:T(8,128)} %get-tuple-element.45.grads_ref), custom_call_target="tpu_custom_call" | custom-call | tf_op jit(solution)/shard_map/pallas_call | solution.py:183
  131.7 31.9 %all_to_all.5 = f16[8,136,1024]{2,1,0:T(8,128)(2,1)S(1)} all-to-all(f16[8,136,1024]{2,1,0:T(8,128)(2,1)S(1)} %convert_element_type.12), channel_id=1, replica_groups={{0,8,16,24,32,40,48,56},{64,72,80,88,96,104,112,120},{128,136,144,152,1..., dimensions={0} | all-to-all | bytes 4456448 | tf_op jit(solution)/shard_map/all_to_all | solution.py:403
  174.8 5.0 %collective-permute-start.17 = (f32[40,128]{1,0:T(8,128)S(1)}, f32[40,128]{1,0:T(8,128)S(1)}, u32[]{:S(2)}, u32[]{:S(2)}) collective-permute-start(f32[40,128]{1,0:T(8,128)S(1)} %add.141), channel_id=1, source_target_pairs={{0,4},{1,5},{2,6},{3,7},{4,0},{5,1},{6,2},{7,3},{8,12},{9,13},{10,... | collective-permute-start | bytes 61448 | tf_op jit(solution)/shard_map/ppermute | solution.py:36
  188.1 3.0 %collective-permute-start.21 = (bf16[128,256]{1,0:T(8,128)(2,1)S(1)}, bf16[128,256]{1,0:T(8,128)(2,1)S(1)}, u32[]{:S(2)}, u32[]{:S(2)}) collective-permute-start(bf16[128,256]{1,0:T(8,128)(2,1)S(1)} %get-tuple-element.72), channel_id=1, source_target_pairs={{0,32},{8,40},{16,48},{24,56},{32,0},{40,8},{48,16},{56,24},{64,96... | collective-permute-start | bytes 196616 | tf_op jit(solution)/shard_map/ppermute | solution.py:28
  199.2 4.2 %collective-permute-done.23.refs_8_ = bf16[512,256]{1,0:T(8,128)(2,1)S(1)} collective-permute-done((bf16[512,256]{1,0:T(8,128)(2,1)S(1)}, bf16[512,256]{1,0:T(8,128)(2,1)S(1)}, u32[]{:S(2)}, u32[]{:S(2)}) %collective-permute-start.23) | collective-permute-done | bytes 262176 | tf_op jit(solution)/shard_map/ppermute | solution.py:28
  203.4 3.0 %collective-permute-done.24.refs_9_ = bf16[512,256]{1,0:T(8,128)(2,1)S(1)} collective-permute-done((bf16[512,256]{1,0:T(8,128)(2,1)S(1)}, bf16[512,256]{1,0:T(8,128)(2,1)S(1)}, u32[]{:S(2)}, u32[]{:S(2)}) %collective-permute-start.24) | collective-permute-done | bytes 262176 | tf_op jit(solution)/shard_map/ppermute | solution.py:28
  211.4 3.5 %copy-done = bf16[1088,4096]{1,0:T(8,128)(2,1)S(1)} copy-done((bf16[1088,4096]{1,0:T(8,128)(2,1)S(1)}, bf16[1088,4096]{1,0:T(8,128)(2,1)}, u32[]{:S(2)}) %copy-start) | copy-done | bytes 8912920
  214.9 4.0 %shard_map.81.refs_11_ = f32[2,1088,256]{2,1,0:T(8,128)S(1)} custom-call(s32[4]{0:T(128)S(1)} %pad_add_fusion.1.place, bf16[1088,4096]{1,0:T(8,128)(2,1)S(1)} %copy-done, bf16[1088,4096]{1,0:T(8,128)(2,1)S(1)} %copy-done, bf16[1088,4096]{1,0:T(8,128)(2,1)S(1)} %copy-done, bf16[1088,4096]{1,0:T(8,128)(2,1)S(1)} %copy-done, ...), custom_call_target="tpu_custom_call" | custom-call | tf_op jit(solution)/shard_map/pallas_call | solution.py:324
  218.9 5.6 %shard_map.82.refs_11_ = f32[2,1088,256]{2,1,0:T(8,128)S(1)} custom-call(s32[4]{0:T(128)S(1)} %pad_add_fusion.1.place, bf16[1088,4096]{1,0:T(8,128)(2,1)S(1)} %copy-done, bf16[1088,4096]{1,0:T(8,128)(2,1)S(1)} %copy-done, bf16[1088,4096]{1,0:T(8,128)(2,1)S(1)} %copy-done, bf16[1088,4096]{1,0:T(8,128)(2,1)S(1)} %copy-done, ...), custom_call_target="tpu_custom_call" | custom-call | tf_op jit(solution)/shard_map/pallas_call | solution.py:324
  224.6 5.7 %shard_map.83 = (bf16[2,272,256]{2,1,0:T(8,128)(2,1)S(1)}, bf16[2,272,256]{2,1,0:T(8,128)(2,1)S(1)}, bf16[2,272,256]{2,1,0:T(8,128)(2,1)S(1)}, bf16[2,272,256]{2,1,0:T(8,128)(2,1)S(1)}) custom-call(s32[4]{0:T(128)S(1)} %pad_add_fusion.1.place, bf16[1088,4096]{1,0:T(8,128)(2,1)S(1)} %copy-done, bf16[1088,4096]{1,0:T(8,128)(2,1)S(1)} %copy-done, ...), custom_call_target="tpu_custom_call" | custom-call | tf_op jit(solution)/shard_map/pallas_call | solution.py:324
  234.5 5.8 %collective-permute-done.30.p1_ref = bf16[2,272,256]{2,1,0:T(8,128)(2,1)S(1)} collective-permute-done((bf16[2,272,256]{2,1,0:T(8,128)(2,1)S(1)}, bf16[2,272,256]{2,1,0:T(8,128)(2,1)S(1)}, u32[]{:S(2)}, u32[]{:S(2)}) %collective-permute-start.30) | collective-permute-done | bytes 278560 | tf_op jit(solution)/shard_map/ppermute | solution.py:28
  (115 shorter events, 74.7 us)
Async XLA Ops:
  7.2 124.4 %all-gather.2.cloned.1.call-start = ((), (), s32[]{:S(2)}) async-start(), calls=%async_computation.1 | async-start | bytes 11141120 | tf_op jit(solution)/shard_map/all_gather | solution.py:383
  12.1 7.8 %collective-permute-start.1 = (bf16[544,128]{1,0:T(8,128)(2,1)S(1)}, bf16[544,128]{1,0:T(8,128)(2,1)S(1)}, u32[]{:S(2)}, u32[]{:S(2)}) collective-permute-start(bf16[544,128]{1,0:T(8,128)(2,1)S(1)} %get-tuple-element.66), channel_id=1, source_target_pairs={{0,128},{8,136},{16,144},{24,152},{32,160},{40,168},{48,176},{56,1... | collective-permute-start | bytes 417800 | tf_op jit(solution)/shard_map/ppermute | solution.py:28
  21.8 42.3 %collective-permute-start.7 = (bf16[544,1024]{1,0:T(8,128)(2,1)S(1)}, bf16[544,1024]{1,0:T(8,128)(2,1)S(1)}, u32[]{:S(2)}, u32[]{:S(2)}) collective-permute-start(bf16[544,1024]{1,0:T(8,128)(2,1)S(1)} %copy-done.5), channel_id=1, source_target_pairs={{0,64},{8,72},{16,80},{24,88},{32,96},{40,104},{48,112},{56,120},{... | collective-permute-start | bytes 3342344 | tf_op jit(solution)/shard_map/ppermute | solution.py:28
  22.9 42.2 %collective-permute-start.8 = (bf16[544,1024]{1,0:T(8,128)(2,1)S(1)}, bf16[544,1024]{1,0:T(8,128)(2,1)S(1)}, u32[]{:S(2)}, u32[]{:S(2)}) collective-permute-start(bf16[544,1024]{1,0:T(8,128)(2,1)S(1)} %copy-done.5), channel_id=1, source_target_pairs={{0,128},{8,136},{16,144},{24,152},{32,160},{40,168},{48,176},{56,1... | collective-permute-start | bytes 3342344 | tf_op jit(solution)/shard_map/ppermute | solution.py:28
  24.9 48.6 %collective-permute-start.9 = (bf16[544,1024]{1,0:T(8,128)(2,1)S(1)}, bf16[544,1024]{1,0:T(8,128)(2,1)S(1)}, u32[]{:S(2)}, u32[]{:S(2)}) collective-permute-start(bf16[544,1024]{1,0:T(8,128)(2,1)S(1)} %copy-done.5), channel_id=1, source_target_pairs={{0,192},{8,200},{16,208},{24,216},{32,224},{40,232},{48,240},{56,2... | collective-permute-start | bytes 3342344 | tf_op jit(solution)/shard_map/ppermute | solution.py:28
  25.1 22.8 %collective-permute-start.4 = (bf16[3,544,128]{2,1,0:T(8,128)(2,1)S(1)}, bf16[3,544,128]{2,1,0:T(8,128)(2,1)S(1)}, u32[]{:S(2)}, u32[]{:S(2)}) collective-permute-start(bf16[3,544,128]{2,1,0:T(8,128)(2,1)S(1)} %get-tuple-element.69), channel_id=1, source_target_pairs={{0,6},{1,7},{2,0},{3,1},{4,2},{5,3},{6,4},{7,5},{8,14},{9,15},{10,... | collective-permute-start | bytes 1253384 | tf_op jit(solution)/shard_map/ppermute | solution.py:36
  31.5 21.2 %collective-permute-start.3 = (bf16[3,544,128]{2,1,0:T(8,128)(2,1)S(1)}, bf16[3,544,128]{2,1,0:T(8,128)(2,1)S(1)}, u32[]{:S(2)}, u32[]{:S(2)}) collective-permute-start(bf16[3,544,128]{2,1,0:T(8,128)(2,1)S(1)} %get-tuple-element.69), channel_id=1, source_target_pairs={{0,2},{1,3},{2,4},{3,5},{4,6},{5,7},{6,0},{7,1},{8,10},{9,11},{10,... | collective-permute-start | bytes 1253384 | tf_op jit(solution)/shard_map/ppermute | solution.py:36
  47.9 10.6 %collective-permute-start.6 = (bf16[3,272,128]{2,1,0:T(8,128)(2,1)S(1)}, bf16[3,272,128]{2,1,0:T(8,128)(2,1)S(1)}, u32[]{:S(2)}, u32[]{:S(2)}) collective-permute-start(bf16[3,272,128]{2,1,0:T(8,128)(2,1)S(1)} %slice.21), channel_id=1, source_target_pairs={{0,6},{1,7},{2,0},{3,1},{4,2},{5,3},{6,4},{7,5},{8,14},{9,15},{10,... | collective-permute-start | bytes 626696 | tf_op jit(solution)/shard_map/ppermute | solution.py:36
  52.7 11.4 %collective-permute-start.5 = (bf16[3,272,128]{2,1,0:T(8,128)(2,1)S(1)}, bf16[3,272,128]{2,1,0:T(8,128)(2,1)S(1)}, u32[]{:S(2)}, u32[]{:S(2)}) collective-permute-start(bf16[3,272,128]{2,1,0:T(8,128)(2,1)S(1)} %slice.20), channel_id=1, source_target_pairs={{0,2},{1,3},{2,4},{3,5},{4,6},{5,7},{6,0},{7,1},{8,10},{9,11},{10,... | collective-permute-start | bytes 626696 | tf_op jit(solution)/shard_map/ppermute | solution.py:36
  103.0 11.3 %collective-permute-start.13 = (f32[8,128]{1,0:T(8,128)S(1)}, f32[8,128]{1,0:T(8,128)S(1)}, u32[]{:S(2)}, u32[]{:S(2)}) collective-permute-start(f32[8,128]{1,0:T(8,128)S(1)} %add.133), channel_id=1, source_target_pairs={{0,2},{1,3},{2,4},{3,5},{4,6},{5,7},{6,0},{7,1},{8,10},{9,11},{10,... | collective-permute-start | bytes 12296 | tf_op jit(solution)/shard_map/ppermute | solution.py:36
  106.3 8.1 %collective-permute-start.14 = (f32[8,128]{1,0:T(8,128)S(1)}, f32[8,128]{1,0:T(8,128)S(1)}, u32[]{:S(2)}, u32[]{:S(2)}) collective-permute-start(f32[8,128]{1,0:T(8,128)S(1)} %add.133), channel_id=1, source_target_pairs={{0,6},{1,7},{2,0},{3,1},{4,2},{5,3},{6,4},{7,5},{8,14},{9,15},{10,... | collective-permute-start | bytes 12296 | tf_op jit(solution)/shard_map/ppermute | solution.py:36
  131.6 32.0 %collective-permute-start.15 = (bf16[1088,4096]{1,0:T(8,128)(2,1)}, bf16[1088,4096]{1,0:T(8,128)(2,1)}, u32[]{:S(2)}, u32[]{:S(2)}) collective-permute-start(bf16[1088,4096]{1,0:T(8,128)(2,1)} %all-gather.2.cloned.1.call-done.refs_0_.refs_1_.refs_2_.refs_3_), channel_id=1, source_target_pairs={{0,1},{1,0},{2,3},{3,2},{4,5},{5,4},{6,7},{7,6},{8,9},{9,8},{10,11... | collective-permute-start | bytes 26738696 | tf_op jit(solution)/shard_map/ppermute | solution.py:36
  170.6 9.2 %collective-permute-start.18 = (f32[40,128]{1,0:T(8,128)S(1)}, f32[40,128]{1,0:T(8,128)S(1)}, u32[]{:S(2)}, u32[]{:S(2)}) collective-permute-start(f32[40,128]{1,0:T(8,128)S(1)} %add.141), channel_id=1, source_target_pairs={{0,2},{1,3},{2,4},{3,5},{4,6},{5,7},{6,0},{7,1},{8,10},{9,11},{10,... | collective-permute-start | bytes 61448 | tf_op jit(solution)/shard_map/ppermute | solution.py:36
  174.8 7.8 %collective-permute-start.17 = (f32[40,128]{1,0:T(8,128)S(1)}, f32[40,128]{1,0:T(8,128)S(1)}, u32[]{:S(2)}, u32[]{:S(2)}) collective-permute-start(f32[40,128]{1,0:T(8,128)S(1)} %add.141), channel_id=1, source_target_pairs={{0,4},{1,5},{2,6},{3,7},{4,0},{5,1},{6,2},{7,3},{8,12},{9,13},{10,... | collective-permute-start | bytes 61448 | tf_op jit(solution)/shard_map/ppermute | solution.py:36
  195.3 8.1 %collective-permute-start.23 = (bf16[512,256]{1,0:T(8,128)(2,1)S(1)}, bf16[512,256]{1,0:T(8,128)(2,1)S(1)}, u32[]{:S(2)}, u32[]{:S(2)}) collective-permute-start(bf16[512,256]{1,0:T(8,128)(2,1)S(1)} %pad_maximum_fusion.3.refs_8_), channel_id=1, source_target_pairs={{0,64},{8,72},{16,80},{24,88},{32,96},{40,104},{48,112},{56,120},{... | collective-permute-start | bytes 786440 | tf_op jit(solution)/shard_map/ppermute | solution.py:28
  197.1 9.4 %collective-permute-start.24 = (bf16[512,256]{1,0:T(8,128)(2,1)S(1)}, bf16[512,256]{1,0:T(8,128)(2,1)S(1)}, u32[]{:S(2)}, u32[]{:S(2)}) collective-permute-start(bf16[512,256]{1,0:T(8,128)(2,1)S(1)} %pad_maximum_fusion.3.refs_8_), channel_id=1, source_target_pairs={{0,128},{8,136},{16,144},{24,152},{32,160},{40,168},{48,176},{56,1... | collective-permute-start | bytes 786440 | tf_op jit(solution)/shard_map/ppermute | solution.py:28
  197.7 11.4 %collective-permute-start.25 = (bf16[512,256]{1,0:T(8,128)(2,1)S(1)}, bf16[512,256]{1,0:T(8,128)(2,1)S(1)}, u32[]{:S(2)}, u32[]{:S(2)}) collective-permute-start(bf16[512,256]{1,0:T(8,128)(2,1)S(1)} %pad_maximum_fusion.3.refs_8_), channel_id=1, source_target_pairs={{0,192},{8,200},{16,208},{24,216},{32,224},{40,232},{48,240},{56,2... | collective-permute-start | bytes 786440 | tf_op jit(solution)/shard_map/ppermute | solution.py:28
  198.5 10.6 %collective-permute-start.26 = (bf16[512,256]{1,0:T(8,128)(2,1)S(1)}, bf16[512,256]{1,0:T(8,128)(2,1)S(1)}, u32[]{:S(2)}, u32[]{:S(2)}) collective-permute-start(bf16[512,256]{1,0:T(8,128)(2,1)S(1)} %pad_maximum_fusion.3.refs_8_), channel_id=1, source_target_pairs={{0,8},{8,0},{16,24},{24,16},{32,40},{40,32},{48,56},{56,48},{64,72... | collective-permute-start | bytes 786440 | tf_op jit(solution)/shard_map/ppermute | solution.py:28
  209.1 15.4 %collective-permute-start.27 = (bf16[512,256]{1,0:T(8,128)(2,1)S(1)}, bf16[512,256]{1,0:T(8,128)(2,1)S(1)}, u32[]{:S(2)}, u32[]{:S(2)}) collective-permute-start(bf16[512,256]{1,0:T(8,128)(2,1)S(1)} %collective-permute-done.26.refs_9_), channel_id=1, source_target_pairs={{0,64},{8,72},{16,80},{24,88},{32,96},{40,104},{48,112},{56,120},{... | collective-permute-start | bytes 786440 | tf_op jit(solution)/shard_map/ppermute | solution.py:28
  209.8 14.8 %collective-permute-start.28 = (bf16[512,256]{1,0:T(8,128)(2,1)S(1)}, bf16[512,256]{1,0:T(8,128)(2,1)S(1)}, u32[]{:S(2)}, u32[]{:S(2)}) collective-permute-start(bf16[512,256]{1,0:T(8,128)(2,1)S(1)} %collective-permute-done.26.refs_9_), channel_id=1, source_target_pairs={{0,128},{8,136},{16,144},{24,152},{32,160},{40,168},{48,176},{56,1... | collective-permute-start | bytes 786440 | tf_op jit(solution)/shard_map/ppermute | solution.py:28
  210.4 14.2 %collective-permute-start.29 = (bf16[512,256]{1,0:T(8,128)(2,1)S(1)}, bf16[512,256]{1,0:T(8,128)(2,1)S(1)}, u32[]{:S(2)}, u32[]{:S(2)}) collective-permute-start(bf16[512,256]{1,0:T(8,128)(2,1)S(1)} %collective-permute-done.26.refs_9_), channel_id=1, source_target_pairs={{0,192},{8,200},{16,208},{24,216},{32,224},{40,232},{48,240},{56,2... | collective-permute-start | bytes 786440 | tf_op jit(solution)/shard_map/ppermute | solution.py:28
  231.0 9.3 %collective-permute-start.30 = (bf16[2,272,256]{2,1,0:T(8,128)(2,1)S(1)}, bf16[2,272,256]{2,1,0:T(8,128)(2,1)S(1)}, u32[]{:S(2)}, u32[]{:S(2)}) collective-permute-start(bf16[2,272,256]{2,1,0:T(8,128)(2,1)S(1)} %get-tuple-element.62), channel_id=1, source_target_pairs={{0,16},{8,24},{16,32},{24,40},{32,48},{40,56},{48,0},{56,8},{64,80... | collective-permute-start | bytes 835592 | tf_op jit(solution)/shard_map/ppermute | solution.py:28
  232.9 10.3 %collective-permute-start.31 = (bf16[2,272,256]{2,1,0:T(8,128)(2,1)S(1)}, bf16[2,272,256]{2,1,0:T(8,128)(2,1)S(1)}, u32[]{:S(2)}, u32[]{:S(2)}) collective-permute-start(bf16[2,272,256]{2,1,0:T(8,128)(2,1)S(1)} %get-tuple-element.63), channel_id=1, source_target_pairs={{0,32},{8,40},{16,48},{24,56},{32,0},{40,8},{48,16},{56,24},{64,96... | collective-permute-start | bytes 835592 | tf_op jit(solution)/shard_map/ppermute | solution.py:28
  233.8 12.3 %collective-permute-start.32 = (bf16[2,272,256]{2,1,0:T(8,128)(2,1)S(1)}, bf16[2,272,256]{2,1,0:T(8,128)(2,1)S(1)}, u32[]{:S(2)}, u32[]{:S(2)}) collective-permute-start(bf16[2,272,256]{2,1,0:T(8,128)(2,1)S(1)} %get-tuple-element.64), channel_id=1, source_target_pairs={{0,48},{8,56},{16,0},{24,8},{32,16},{40,24},{48,32},{56,40},{64,11... | collective-permute-start | bytes 835592 | tf_op jit(solution)/shard_map/ppermute | solution.py:28
  (30 other events, 163.5 us)
Sparse Core Ops, SparseCore 0:
  10.7 91.7 all-gather.1

commit v3 on v2

--- a/solution.py
+++ b/solution.py
@@ -42,45 +42,26 @@
     return (part + two) + (one + three)
 
 
-def turn_kernel(place, tokens_ref, mine_ref, other_ref, turned_ref):
-    core = place[2]
-    for which, ref in ((0, mine_ref), (1, other_ref)):
-        side = core if which == 0 else 1 - core
-        own = tokens_ref[:, pl.ds(pl.multiple_of(side * BLK, BLK), BLK)]
-        for k, cols in enumerate([own, ref[0, 0], ref[0, 1], ref[0, 2]]):
-            turned_ref[k, pl.ds(pl.multiple_of(side * BLK, BLK), BLK), :] = cols.T
-
-
-def turn(place, tokens, mine, other):
-    tok_dev = tokens.shape[0]
-    recv = pl.BlockSpec((1, 3, tok_dev, BLK), lambda j, p: (j, 0, 0, 0))
-    return pl.pallas_call(
-        turn_kernel,
-        grid_spec=pltpu.PrefetchScalarGridSpec(
-            num_scalar_prefetch=1,
-            grid=(NH,),
-            in_specs=[
-                pl.BlockSpec((tok_dev, 2 * BLK), lambda j, p: (0, p[0] * NH + lax.rem(p[1] - j + NH, NH))),
-                recv,
-                recv,
-            ],
-            out_specs=pl.BlockSpec((4, 2 * BLK, tok_dev), lambda j, p: (0, lax.rem(p[1] - j + NH, NH), 0)),
-        ),
-        out_shape=jax.ShapeDtypeStruct((4, 2 * NH * BLK, tok_dev), jnp.bfloat16),
-        compiler_params=pltpu.CompilerParams(vmem_limit_bytes=24 * 2**20),
-    )(place, tokens, mine, other)
-
-
-def grads_kernel(turned_ref, o0_ref, o1_ref, o2_ref, o3_ref, grads_ref, gram_ref, sums_ref):
+def grads_kernel(
+    place, tokens_ref, mine_ref, other_ref, o0_ref, o1_ref, o2_ref, o2b_ref, o3_ref, grads_ref, gram_ref, turned_ref, sums_ref
+):
     step = pl.program_id(0)
 
     @pl.when(step == 0)
     def _():
         sums_ref[...] = jnp.zeros_like(sums_ref)
+        for j in range(NH):
+            for which, ref in ((0, mine_ref), (1, other_ref)):
+                side = place[4] if which == 0 else 1 - place[4]
+                block = lax.rem(place[3] - j + NH, NH) * 2 + side
+                at = pl.ds(pl.multiple_of(block * BLK, BLK), BLK)
+                for k, cols in enumerate([tokens_ref[:, at], ref[j, 0], ref[j, 1], ref[j, 2]]):
+                    turned_ref[k, at, :] = cols.T
 
     blocks, _, _, span = grads_ref.shape
-    for k, o_ref in enumerate((o0_ref, o1_ref, o2_ref, o3_ref)):
-        product = jnp.dot(turned_ref[k], o_ref[...], preferred_element_type=F32)
+    o2 = jnp.where(step < pl.num_programs(0) // 2, o2_ref[...], o2b_ref[...])
+    for k, out in enumerate((o0_ref[...], o1_ref[...], o2, o3_ref[...])):
+        product = jnp.dot(turned_ref[k], out, preferred_element_type=F32)
         grads_ref[:, k] = product.reshape(blocks, BLK, span)
 
     def one_block(m, _):
@@ -103,26 +84,37 @@
         gram_ref[...] = jnp.broadcast_to(jnp.sum(rows.T, axis=0, keepdims=True), gram_ref.shape)
 
 
-def grads_and_gram(turned, outs):
+def grads_and_gram(place, tokens, mine, other, outs):
     tok_dev, cols = outs[0].shape
     span = 256
-    blocks = turned.shape[1] // BLK
-    out_cols = pl.BlockSpec((tok_dev, span), lambda n: (0, n))
+    blocks = NH * NC
+    half = cols // span // 2
+    out_cols = pl.BlockSpec((tok_dev, span), lambda n, p: (0, n))
+    first_half = pl.BlockSpec((tok_dev, span), lambda n, p: (0, jnp.minimum(n, half - 1)))
+    last_half = pl.BlockSpec((tok_dev, span), lambda n, p: (0, jnp.maximum(n - half, 0)))
+    landed = pl.BlockSpec(mine.shape, lambda n, p: (0, 0, 0, 0))
     return pl.pallas_call(
         grads_kernel,
-        grid=(cols // span,),
-        in_specs=[pl.BlockSpec(turned.shape, lambda n: (0, 0, 0)), out_cols, out_cols, out_cols, out_cols],
-        out_specs=[
-            pl.BlockSpec((blocks, 4, BLK, span), lambda n: (0, 0, 0, n)),
-            pl.BlockSpec((8, 128), lambda n: (0, 0)),
-        ],
+        grid_spec=pltpu.PrefetchScalarGridSpec(
+            num_scalar_prefetch=1,
+            grid=(cols // span,),
+            in_specs=[pl.BlockSpec((tok_dev, blocks * BLK), lambda n, p: (0, p[0])), landed, landed]
+            + [out_cols, out_cols, first_half, last_half, out_cols],
+            out_specs=[
+                pl.BlockSpec((blocks, 4, BLK, span), lambda n, p: (0, 0, 0, n)),
+                pl.BlockSpec((8, 128), lambda n, p: (0, 0)),
+            ],
+            scratch_shapes=[
+                pltpu.VMEM((4, blocks * BLK, tok_dev), jnp.bfloat16),
+                pltpu.VMEM((blocks, 16, 8, 128), F32),
+            ],
+        ),
         out_shape=[
             jax.ShapeDtypeStruct((blocks, 4, BLK, cols), F32),
             jax.ShapeDtypeStruct((8, 128), F32),
         ],
-        scratch_shapes=[pltpu.VMEM((blocks, 16, 8, 128), F32)],
-        compiler_params=pltpu.CompilerParams(vmem_limit_bytes=48 * 2**20),
-    )(turned, *outs)
+        compiler_params=pltpu.CompilerParams(vmem_limit_bytes=60 * 2**20),
+    )(place, tokens, mine, other, outs[0], outs[1], *outs[2], outs[3])
 
 
 def mix_kernel(tok_dev, gram_ref, grads_ref, coded_ref):
@@ -189,7 +181,7 @@
         ],
         out_specs=pl.BlockSpec((1, BLK + 8, cols), lambda m: (m, 0, 0)),
         out_shape=jax.ShapeDtypeStruct((blocks, BLK + 8, cols), F32),
-        compiler_params=pltpu.CompilerParams(vmem_limit_bytes=56 * 2**20),
+        compiler_params=pltpu.CompilerParams(vmem_limit_bytes=16 * 2**20),
     )(gram, grads)
 
 
@@ -280,16 +272,15 @@
     return (lax.rem(y - j + NY, NY) * NX + lax.rem(x - i + NX, NX)) * NZ + lax.rem(z + e, NZ)
 
 
-def project_kernel(units, last, place, *refs):
+def project_kernel(units, start, last, place, *refs):
     mine, other = refs[:NX], refs[NX : 2 * NX]
-    held, start_ref = refs[2 * NX : 2 * NX + units], refs[2 * NX + units]
-    rest = refs[2 * NX + units + 1 :]
-    total_ref = rest[-1] if last else rest[0]
+    held, rest = refs[2 * NX : 2 * NX + units], refs[2 * NX + units :]
+    total_ref = rest[-1]
     step = pl.program_id(0)
 
     @pl.when(step == 0)
     def _():
-        total_ref[...] = start_ref[...]
+        total_ref[...] = rest[0][...] if start else jnp.zeros_like(total_ref)
 
     unit = held[0][...]
     for u in range(1, units):
@@ -306,12 +297,14 @@
             part = rows // NX
             for k in range(NX):
                 first = pl.multiple_of(lax.rem(place[1] + k, NX) * part, part)
-                rest[k][...] = total_ref[:, pl.ds(first, part), :].astype(rest[k].dtype)
+                rest[1 + k][...] = total_ref[:, pl.ds(first, part), :].astype(rest[1 + k].dtype)
 
 
 def project(place, mine, other, held, start, first, stride, last):
     units = len(held)
-    rows, cols = start.shape[1:]
+    rows, cols = mine.shape[0], held[0].shape[1]
+    shape = (2, rows, cols)
+    begin = [] if start is None else [start]
     left = [
         pl.BlockSpec(
             (rows, BLK),
@@ -322,17 +315,17 @@
     whole = lambda shape: pl.BlockSpec(shape, lambda u, p: (0,) * len(shape))
     part = (2, rows // NX, cols)
     return pl.pallas_call(
-        functools.partial(project_kernel, units, last),
+        functools.partial(project_kernel, units, len(begin), last),
         grid_spec=pltpu.PrefetchScalarGridSpec(
             num_scalar_prefetch=1,
             grid=(units,),
-            in_specs=left + left + [whole(h.shape) for h in held] + [whole(start.shape)],
-            out_specs=[whole(part)] * NX if last else whole(start.shape),
-            scratch_shapes=[pltpu.VMEM(start.shape, F32)] if last else [],
+            in_specs=left + left + [whole(h.shape) for h in held] + [whole(shape)] * len(begin),
+            out_specs=[whole(part)] * NX if last else whole(shape),
+            scratch_shapes=[pltpu.VMEM(shape, F32)] if last else [],
         ),
-        out_shape=[jax.ShapeDtypeStruct(part, jnp.bfloat16)] * NX if last else jax.ShapeDtypeStruct(start.shape, F32),
+        out_shape=[jax.ShapeDtypeStruct(part, jnp.bfloat16)] * NX if last else jax.ShapeDtypeStruct(shape, F32),
         compiler_params=pltpu.CompilerParams(vmem_limit_bytes=40 * 2**20),
-    )(place, *([mine] * NX), *([other] * NX), *held, start)
+    )(place, *([mine] * NX), *([other] * NX), *held, *begin)
 
 
 def assemble_kernel(place, p0_ref, p1_ref, p2_ref, p3_ref, out_ref):
@@ -340,7 +333,7 @@
     for k, ref in enumerate((p0_ref, p1_ref, p2_ref, p3_ref)):
         column = pl.multiple_of(lax.rem(place[1] - k + NX, NX) * cols, cols)
         for side in range(2):
-            core = place[3] if side == 0 else 1 - place[3]
+            core = place[4] if side == 0 else 1 - place[4]
             row = pl.multiple_of(core * part, 16)
             out_ref[pl.ds(row, part), pl.ds(column, cols)] = ref[side]
 
@@ -362,10 +355,9 @@
     unit = jnp.concatenate([pieces[0]] + [move_dp(pieces[k], dx=k) for k in (1, 2, 3)], 0)
     partner = move_dp(unit, dz=1)
     own_ring = [move_dp(unit, dy=k) for k in (1, 2, 3)]
-    own_ring, partner = lax.optimization_barrier((own_ring, partner))
+    total = project(place, mine, other, [unit, partner], None, (0, 0), (0, 1), False)
+    own_ring, partner, total = lax.optimization_barrier((own_ring, partner, total))
     far_ring = [move_dp(partner, dy=k) for k in (1, 2, 3)]
-    total = jnp.zeros((2, mine.shape[0], cols), F32)
-    total = project(place, mine, other, [unit, partner], total, (0, 0), (0, 1), False)
     total = project(place, mine, other, own_ring, total, (1, 0), (1, 0), False)
     total, far_ring = lax.optimization_barrier((total, far_ring))
     parts = project(place, mine, other, far_ring, total, (1, 1), (1, 0), True)
@@ -377,25 +369,29 @@
     y, x, z = dp // (NX * NZ), dp // NZ % NX, dp % NZ
     tok_dev = tokens.shape[0]
     group = NX * NZ
-    here = jnp.stack([y, x, z, mp % NC]).astype(jnp.int32)
-    next_half = lax.dynamic_slice_in_dim(next_tokens, (mp % NC) * (tok_dev // 2), tok_dev // 2, 0)
-    x_rings = [[(a * NX + k) * NZ + b for k in range(NX)] for a in range(NY) for b in range(NZ)]
-    next_mine = lax.all_gather(next_half, "dp", axis_index_groups=x_rings, tiled=True)
+    here = jnp.stack([y, x, z, mp // NC, mp % NC]).astype(jnp.int32)
     sent = []
     for k in (1, 2, 3):
         first = (((y + k) % NY) * group + mp) * BLK
-        sent.append(move_dp(lax.dynamic_slice_in_dim(tokens, first, BLK, 1), dy=k))
-    sent, out_grad = lax.optimization_barrier((sent, out_grad))
-    outs = [move_dp(out_grad, dy=k) for k in (1, 2, 3)]
+        sent.append(lax.dynamic_slice_in_dim(tokens, first, BLK, 1))
+    sent, next_tokens = lax.optimization_barrier((sent, next_tokens))
+    sent = [move_dp(block, dy=k) for k, block in zip((1, 2, 3), sent)]
+    next_half = lax.dynamic_slice_in_dim(next_tokens, (mp % NC) * (tok_dev // 2), tok_dev // 2, 0)
+    sent, out_grad, next_half = lax.optimization_barrier((sent, out_grad, next_half))
+    x_rings = [[(a * NX + k) * NZ + b for k in range(NX)] for a in range(NY) for b in range(NZ)]
+    next_mine = lax.all_gather(next_half, "dp", axis_index_groups=x_rings, tiled=True)
     piece = jnp.stack(sent)
+    half, middle = tok_dev // 2, out_grad.shape[1] // 2
+    near = [move_dp(out_grad, dy=1), move_dp(out_grad, dy=3)]
     up, down = move_mp(piece, dh=1), move_mp(piece, dh=3)
-    half = tok_dev // 2
-    far = jnp.concatenate([move_mp(up[:, :half], dh=1), move_mp(down[:, half:], dh=3)], 1)
-    up, down, far, outs = lax.optimization_barrier((up, down, far, outs))
+    near, up, down = lax.optimization_barrier((near, up, down))
+    far_out = [move_dp(near[0][:, :middle], dy=1), move_dp(near[1][:, middle:], dy=3)]
+    far = [move_mp(up[:, :half], dh=1), move_mp(down[:, half:], dh=3)]
+    far, far_out, near = lax.optimization_barrier((far, far_out, near))
+    far = jnp.concatenate(far, 1)
     mine = jnp.stack([piece, up, far, down])
     other = move_mp(mine, dc=1)
-    place = jnp.stack([y, mp // NC, mp % NC]).astype(jnp.int32)
-    grads, gram = grads_and_gram(turn(place, tokens, mine, other), [out_grad] + outs)
+    grads, gram = grads_and_gram(here, tokens, mine, other, [out_grad, near[0], far_out, near[1]])
     coded = mix(sum_mp(gram), grads, tok_dev).astype(jnp.float16)
     rings = [[ring * group + k for k in range(group)] for ring in range(NY)]
     coded, next_mine = lax.optimization_barrier((coded, next_mine))

time: 259 us -> 235 us (0.907)
  waiting for transfers between devices: 77.8 us -> 63 us
  Pallas kernels: 51.7 us -> 44.1 us
    ppermute x19 -> x20, waiting for transfers between devices: 39.2 us -> 25.8 us  [move_dp(): return lax.ppermute(block, 'dp', route)]
    pallas_call x1, Pallas kernels: 11.4 us -> 4.44 us  [mix(): pl.pallas_call(functools.partial(mix_kernel, tok_dev), grid=(blocks,), in...]
    ppermute x14, waiting for transfers between devices: 38.5 us -> 35.1 us  [move_mp(): return lax.ppermute(block, 'mp', route)]
    unnamed x41 -> x33, local copies, waits for them, and re-layouts: 17 us -> 15 us
    ppermute x19 -> x20, starting transfers between devices: 20.3 us -> 21.4 us  [move_dp(): return lax.ppermute(block, 'dp', route)]
    pallas_call x5 -> x4, Pallas kernels: 34.1 us -> 33.4 us  [the longest x1 18.2 us: grads_and_gram(): pl.pallas_call(grads_kernel, grid_spec=pltpu.PrefetchScalarGridSpec(num_s...]
  transfers between devices with their start and end apart: 34 -> 35, of which waited for: 21 -> 24; matrix products, arithmetic and copies ran while one was open for 2% -> 2% of each run, Pallas kernels for 16% -> 14%
where the time goes in v3:
time: 235 us; the launch traced here: 230 us
  waiting for transfers between devices  63 us (27%)
  starting transfers between devices  51.5 us (22%)
  Pallas kernels  44.1 us (19%)
  blocking collectives  33.1 us (14%)
  local copies, waits for them, and re-layouts  20.4 us (9%)
  between operations  14.4 us (6%)
  other arithmetic  3.79 us (2%)
    ppermute x14, waiting for transfers between devices, move_mp(): return lax.ppermute(block, 'mp', route)  35.1 us
    all_to_all x1, blocking collectives, shards(): landed = lax.all_to_all(coded, 'dp', 0, 0, axis_index_groups=rings)  33.1 us
    ppermute x14, starting transfers between devices, move_mp(): return lax.ppermute(block, 'mp', route)  30.1 us
    ppermute x20, waiting for transfers between devices, move_dp(): return lax.ppermute(block, 'dp', route)  25.8 us
    ppermute x20, starting transfers between devices, move_dp(): return lax.ppermute(block, 'dp', route)  21.4 us
    pallas_call x1, Pallas kernels, grads_and_gram(): pl.pallas_call(grads_kernel, grid_spec=pltpu.PrefetchScalarGridSpec(num_s...  18.2 us
    pallas_call x3, Pallas kernels, project(): pl.pallas_call(functools.partial(project_kernel, units, len(begin), last)...  15.2 us
    unnamed x33, local copies, waits for them, and re-layouts  15 us
  transfers between devices with their start and end apart: 35, of which 24 were waited for; matrix products, arithmetic and copies ran while one was open for 2% of the time, Pallas kernels for 14%

profile of v3, /device:TPU:30, one launch (start us, length us, event | category | flops | bytes accessed | tf_op | source)
XLA Modules:
  0.0 230.4 jit_solution(354005962354588656)
XLA Ops:
  11.4 3.2 %constant_dynamic-slice_fusion.4 = bf16[272,4096]{1,0:T(8,128)(2,1)} fusion(bf16[544,4096]{1,0:T(8,128)(2,1)} %param.9, s32[]{:T(128)S(6)} %select_n.95), kind=kLoop, calls=%fused_computation.25 | loop fusion | bytes 4456452 | tf_op jit(solution)/shard_map/dynamic_slice | solution.py:379
  20.8 3.3 %collective-permute-start.5 = (bf16[3,544,128]{2,1,0:T(8,128)(2,1)S(1)}, bf16[3,544,128]{2,1,0:T(8,128)(2,1)S(1)}, u32[]{:S(2)}, u32[]{:S(2)}) collective-permute-start(bf16[3,544,128]{2,1,0:T(8,128)(2,1)S(1)} %get-tuple-element.89), channel_id=1, source_target_pairs={{0,2},{1,3},{2,4},{3,5},{4,6},{5,7},{6,0},{7,1},{8,10},{9,11},{10,... | collective-permute-start | bytes 1253384 | tf_op jit(solution)/shard_map/ppermute | solution.py:36
  24.1 3.1 %collective-permute-start.6 = (bf16[3,544,128]{2,1,0:T(8,128)(2,1)S(1)}, bf16[3,544,128]{2,1,0:T(8,128)(2,1)S(1)}, u32[]{:S(2)}, u32[]{:S(2)}) collective-permute-start(bf16[3,544,128]{2,1,0:T(8,128)(2,1)S(1)} %get-tuple-element.89), channel_id=1, source_target_pairs={{0,6},{1,7},{2,0},{3,1},{4,2},{5,3},{6,4},{7,5},{8,14},{9,15},{10,... | collective-permute-start | bytes 1253384 | tf_op jit(solution)/shard_map/ppermute | solution.py:36
  27.2 11.8 %collective-permute-done.5 = bf16[3,544,128]{2,1,0:T(8,128)(2,1)S(1)} collective-permute-done((bf16[3,544,128]{2,1,0:T(8,128)(2,1)S(1)}, bf16[3,544,128]{2,1,0:T(8,128)(2,1)S(1)}, u32[]{:S(2)}, u32[]{:S(2)}) %collective-permute-start.5) | collective-permute-done | bytes 417824 | tf_op jit(solution)/shard_map/ppermute | solution.py:36
  39.1 6.7 %collective-permute-done.6 = bf16[3,544,128]{2,1,0:T(8,128)(2,1)S(1)} collective-permute-done((bf16[3,544,128]{2,1,0:T(8,128)(2,1)S(1)}, bf16[3,544,128]{2,1,0:T(8,128)(2,1)S(1)}, u32[]{:S(2)}, u32[]{:S(2)}) %collective-permute-start.6) | collective-permute-done | bytes 417824 | tf_op jit(solution)/shard_map/ppermute | solution.py:36
  46.4 3.2 %collective-permute-start.9 = (bf16[544,512]{1,0:T(8,128)(2,1)S(1)}, bf16[544,512]{1,0:T(8,128)(2,1)}, u32[]{:S(2)}, u32[]{:S(2)}) collective-permute-start(bf16[544,512]{1,0:T(8,128)(2,1)S(1)} %slice.23), channel_id=1, source_target_pairs={{0,64},{8,72},{16,80},{24,88},{32,96},{40,104},{48,112},{56,120},{... | collective-permute-start | bytes 1671176 | tf_op jit(solution)/shard_map/ppermute | solution.py:28
  49.6 3.5 %collective-permute-start.7 = (bf16[3,272,128]{2,1,0:T(8,128)(2,1)S(1)}, bf16[3,272,128]{2,1,0:T(8,128)(2,1)S(1)}, u32[]{:S(2)}, u32[]{:S(2)}) collective-permute-start(bf16[3,272,128]{2,1,0:T(8,128)(2,1)S(1)} %slice.21), channel_id=1, source_target_pairs={{0,2},{1,3},{2,4},{3,5},{4,6},{5,7},{6,0},{7,1},{8,10},{9,11},{10,... | collective-permute-start | bytes 626696 | tf_op jit(solution)/shard_map/ppermute | solution.py:36
  53.1 3.0 %collective-permute-start.8 = (bf16[3,272,128]{2,1,0:T(8,128)(2,1)S(1)}, bf16[3,272,128]{2,1,0:T(8,128)(2,1)S(1)}, u32[]{:S(2)}, u32[]{:S(2)}) collective-permute-start(bf16[3,272,128]{2,1,0:T(8,128)(2,1)S(1)} %slice.22), channel_id=1, source_target_pairs={{0,6},{1,7},{2,0},{3,1},{4,2},{5,3},{6,4},{7,5},{8,14},{9,15},{10,... | collective-permute-start | bytes 626696 | tf_op jit(solution)/shard_map/ppermute | solution.py:36
  56.1 5.4 %collective-permute-done.7 = bf16[3,272,128]{2,1,0:T(8,128)(2,1)S(1)} collective-permute-done((bf16[3,272,128]{2,1,0:T(8,128)(2,1)S(1)}, bf16[3,272,128]{2,1,0:T(8,128)(2,1)S(1)}, u32[]{:S(2)}, u32[]{:S(2)}) %collective-permute-start.7) | collective-permute-done | bytes 208928 | tf_op jit(solution)/shard_map/ppermute | solution.py:36
  68.3 18.2 %shard_map.76 = (f32[8,4,128,1024]{3,2,1,0:T(8,128)}, f32[8,128]{1,0:T(8,128)}) custom-call(s32[5]{0:T(128)} %stack.50.place, bf16[544,4096]{1,0:T(8,128)(2,1)} %tokens_ref.1, bf16[4,3,544,128]{3,2,1,0:T(8,128)(2,1)} %copy-done.8, bf16[4,3,544,128]{3,2,1,0:T(8,128)(2,1)} %collective-permute-done.11.other_ref, bf16[544,1024]{1,0:T(8,128)(2,1)} %o0_ref, ...), custom_call_target="tpu_custom_call" | custom-call | tf_op jit(solution)/shard_map/pallas_call | solution.py:96
  88.6 3.4 %collective-permute-start.13 = (f32[8,128]{1,0:T(8,128)S(1)}, f32[8,128]{1,0:T(8,128)S(1)}, u32[]{:S(2)}, u32[]{:S(2)}) collective-permute-start(f32[8,128]{1,0:T(8,128)S(1)} %add.135), channel_id=1, source_target_pairs={{0,4},{1,5},{2,6},{3,7},{4,0},{5,1},{6,2},{7,3},{8,12},{9,13},{10,... | collective-permute-start | bytes 12296 | tf_op jit(solution)/shard_map/ppermute | solution.py:36
  93.5 2.8 %collective-permute-start.15 = (f32[8,128]{1,0:T(8,128)S(1)}, f32[8,128]{1,0:T(8,128)S(1)}, u32[]{:S(2)}, u32[]{:S(2)}) collective-permute-start(f32[8,128]{1,0:T(8,128)S(1)} %add.135), channel_id=1, source_target_pairs={{0,6},{1,7},{2,0},{3,1},{4,2},{5,3},{6,4},{7,5},{8,14},{9,15},{10,... | collective-permute-start | bytes 12296 | tf_op jit(solution)/shard_map/ppermute | solution.py:36
  98.0 5.8 %copy-done.3 = f32[8,4,128,1024]{3,2,1,0:T(8,128)S(1)} copy-done((f32[8,4,128,1024]{3,2,1,0:T(8,128)S(1)}, f32[8,4,128,1024]{3,2,1,0:T(8,128)}, u32[]{:S(2)}) %copy-start.3) | copy-done | bytes 16777240
  103.8 4.4 %shard_map.77 = f32[8,136,1024]{2,1,0:T(8,128)S(1)} custom-call(f32[8,128]{1,0:T(8,128)S(1)} %add_add_fusion.1.gram_ref, f32[8,4,128,1024]{3,2,1,0:T(8,128)S(1)} %copy-done.3), custom_call_target="tpu_custom_call" | custom-call | tf_op jit(solution)/shard_map/pallas_call | solution.py:175
  110.8 33.1 %all_to_all.5 = f16[8,136,1024]{2,1,0:T(8,128)(2,1)S(1)} all-to-all(f16[8,136,1024]{2,1,0:T(8,128)(2,1)S(1)} %convert_element_type.12), channel_id=1, replica_groups={{0,8,16,24,32,40,48,56},{64,72,80,88,96,104,112,120},{128,136,144,152,1..., dimensions={0} | all-to-all | bytes 4456448 | tf_op jit(solution)/shard_map/all_to_all | solution.py:399
  151.0 4.8 %collective-permute-start.18 = (f32[40,128]{1,0:T(8,128)S(1)}, f32[40,128]{1,0:T(8,128)S(1)}, u32[]{:S(2)}, u32[]{:S(2)}) collective-permute-start(f32[40,128]{1,0:T(8,128)S(1)} %add.142), channel_id=1, source_target_pairs={{0,4},{1,5},{2,6},{3,7},{4,0},{5,1},{6,2},{7,3},{8,12},{9,13},{10,... | collective-permute-start | bytes 61448 | tf_op jit(solution)/shard_map/ppermute | solution.py:36
  156.6 3.4 %collective-permute-start.20 = (f32[40,128]{1,0:T(8,128)S(1)}, f32[40,128]{1,0:T(8,128)S(1)}, u32[]{:S(2)}, u32[]{:S(2)}) collective-permute-start(f32[40,128]{1,0:T(8,128)S(1)} %add.142), channel_id=1, source_target_pairs={{0,6},{1,7},{2,0},{3,1},{4,2},{5,3},{6,4},{7,5},{8,14},{9,15},{10,... | collective-permute-start | bytes 61448 | tf_op jit(solution)/shard_map/ppermute | solution.py:36
  171.0 3.8 %collective-permute-done.22 = bf16[128,256]{1,0:T(8,128)(2,1)S(1)} collective-permute-done((bf16[128,256]{1,0:T(8,128)(2,1)S(1)}, bf16[128,256]{1,0:T(8,128)(2,1)S(1)}, u32[]{:S(2)}, u32[]{:S(2)}) %collective-permute-start.22) | collective-permute-done | bytes 65568 | tf_op jit(solution)/shard_map/ppermute | solution.py:28
  181.9 3.5 %copy-done = bf16[1088,4096]{1,0:T(8,128)(2,1)S(1)} copy-done((bf16[1088,4096]{1,0:T(8,128)(2,1)S(1)}, bf16[1088,4096]{1,0:T(8,128)(2,1)}, u32[]{:S(2)}) %copy-start) | copy-done | bytes 8912920
  185.5 4.0 %shard_map.80.refs_11_ = f32[2,1088,256]{2,1,0:T(8,128)S(1)} custom-call(s32[5]{0:T(128)S(1)} %copy-done.7, bf16[1088,4096]{1,0:T(8,128)(2,1)S(1)} %copy-done, bf16[1088,4096]{1,0:T(8,128)(2,1)S(1)} %copy-done, bf16[1088,4096]{1,0:T(8,128)(2,1)S(1)} %copy-done, bf16[1088,4096]{1,0:T(8,128)(2,1)S(1)} %copy-done, ...), custom_call_target="tpu_custom_call" | custom-call | tf_op jit(solution)/shard_map/pallas_call | solution.py:317
  192.5 5.6 %shard_map.81.refs_11_ = f32[2,1088,256]{2,1,0:T(8,128)S(1)} custom-call(s32[5]{0:T(128)S(1)} %copy-done.7, bf16[1088,4096]{1,0:T(8,128)(2,1)S(1)} %copy-done, bf16[1088,4096]{1,0:T(8,128)(2,1)S(1)} %copy-done, bf16[1088,4096]{1,0:T(8,128)(2,1)S(1)} %copy-done, bf16[1088,4096]{1,0:T(8,128)(2,1)S(1)} %copy-done, ...), custom_call_target="tpu_custom_call" | custom-call | tf_op jit(solution)/shard_map/pallas_call | solution.py:317
  201.3 5.7 %shard_map.82 = (bf16[2,272,256]{2,1,0:T(8,128)(2,1)S(1)}, bf16[2,272,256]{2,1,0:T(8,128)(2,1)S(1)}, bf16[2,272,256]{2,1,0:T(8,128)(2,1)S(1)}, bf16[2,272,256]{2,1,0:T(8,128)(2,1)S(1)}) custom-call(s32[5]{0:T(128)S(1)} %copy-done.7, bf16[1088,4096]{1,0:T(8,128)(2,1)S(1)} %copy-done, bf16[1088,4096]{1,0:T(8,128)(2,1)S(1)} %copy-done, ...), custom_call_target="tpu_custom_call" | custom-call | tf_op jit(solution)/shard_map/pallas_call | solution.py:317
  210.2 5.5 %collective-permute-done.31.p1_ref = bf16[2,272,256]{2,1,0:T(8,128)(2,1)S(1)} collective-permute-done((bf16[2,272,256]{2,1,0:T(8,128)(2,1)S(1)}, bf16[2,272,256]{2,1,0:T(8,128)(2,1)S(1)}, u32[]{:S(2)}, u32[]{:S(2)}) %collective-permute-start.31) | collective-permute-done | bytes 278560 | tf_op jit(solution)/shard_map/ppermute | solution.py:28
  217.6 2.9 %collective-permute-done.33.p3_ref = bf16[2,272,256]{2,1,0:T(8,128)(2,1)S(1)} collective-permute-done((bf16[2,272,256]{2,1,0:T(8,128)(2,1)S(1)}, bf16[2,272,256]{2,1,0:T(8,128)(2,1)S(1)}, u32[]{:S(2)}, u32[]{:S(2)}) %collective-permute-start.33) | collective-permute-done | bytes 278560 | tf_op jit(solution)/shard_map/ppermute | solution.py:28
  (108 shorter events, 65.8 us)
Async XLA Ops:
  7.2 103.6 %all-gather.2.cloned.1.call-start = ((), (), s32[]{:S(2)}) async-start(), calls=%async_computation.1 | async-start | bytes 11141120 | tf_op jit(solution)/shard_map/all_gather | solution.py:382
  8.5 6.6 %collective-permute-start = (bf16[544,128]{1,0:T(8,128)(2,1)S(1)}, bf16[544,128]{1,0:T(8,128)(2,1)S(1)}, u32[]{:S(2)}, u32[]{:S(2)}) collective-permute-start(bf16[544,128]{1,0:T(8,128)(2,1)S(1)} %get-tuple-element.44), channel_id=1, source_target_pairs={{0,64},{8,72},{16,80},{24,88},{32,96},{40,104},{48,112},{56,120},{... | collective-permute-start | bytes 417800 | tf_op jit(solution)/shard_map/ppermute | solution.py:28
  8.8 7.8 %collective-permute-start.1 = (bf16[544,128]{1,0:T(8,128)(2,1)S(1)}, bf16[544,128]{1,0:T(8,128)(2,1)S(1)}, u32[]{:S(2)}, u32[]{:S(2)}) collective-permute-start(bf16[544,128]{1,0:T(8,128)(2,1)S(1)} %get-tuple-element.45), channel_id=1, source_target_pairs={{0,128},{8,136},{16,144},{24,152},{32,160},{40,168},{48,176},{56,1... | collective-permute-start | bytes 417800 | tf_op jit(solution)/shard_map/ppermute | solution.py:28
  11.4 7.2 %collective-permute-start.2 = (bf16[544,128]{1,0:T(8,128)(2,1)S(1)}, bf16[544,128]{1,0:T(8,128)(2,1)S(1)}, u32[]{:S(2)}, u32[]{:S(2)}) collective-permute-start(bf16[544,128]{1,0:T(8,128)(2,1)S(1)} %get-tuple-element.46), channel_id=1, source_target_pairs={{0,192},{8,200},{16,208},{24,216},{32,224},{40,232},{48,240},{56,2... | collective-permute-start | bytes 417800 | tf_op jit(solution)/shard_map/ppermute | solution.py:28
  18.6 27.2 %collective-permute-start.3 = (bf16[544,1024]{1,0:T(8,128)(2,1)S(1)}, bf16[544,1024]{1,0:T(8,128)(2,1)S(1)}, u32[]{:S(2)}, u32[]{:S(2)}) collective-permute-start(bf16[544,1024]{1,0:T(8,128)(2,1)S(1)} %copy-done.11), channel_id=1, source_target_pairs={{0,64},{8,72},{16,80},{24,88},{32,96},{40,104},{48,112},{56,120},{... | collective-permute-start | bytes 3342344 | tf_op jit(solution)/shard_map/ppermute | solution.py:28
  19.7 26.4 %collective-permute-start.4 = (bf16[544,1024]{1,0:T(8,128)(2,1)S(1)}, bf16[544,1024]{1,0:T(8,128)(2,1)S(1)}, u32[]{:S(2)}, u32[]{:S(2)}) collective-permute-start(bf16[544,1024]{1,0:T(8,128)(2,1)S(1)} %copy-done.11), channel_id=1, source_target_pairs={{0,192},{8,200},{16,208},{24,216},{32,224},{40,232},{48,240},{56,2... | collective-permute-start | bytes 3342344 | tf_op jit(solution)/shard_map/ppermute | solution.py:28
  20.8 18.3 %collective-permute-start.5 = (bf16[3,544,128]{2,1,0:T(8,128)(2,1)S(1)}, bf16[3,544,128]{2,1,0:T(8,128)(2,1)S(1)}, u32[]{:S(2)}, u32[]{:S(2)}) collective-permute-start(bf16[3,544,128]{2,1,0:T(8,128)(2,1)S(1)} %get-tuple-element.89), channel_id=1, source_target_pairs={{0,2},{1,3},{2,4},{3,5},{4,6},{5,7},{6,0},{7,1},{8,10},{9,11},{10,... | collective-permute-start | bytes 1253384 | tf_op jit(solution)/shard_map/ppermute | solution.py:36
  24.1 21.6 %collective-permute-start.6 = (bf16[3,544,128]{2,1,0:T(8,128)(2,1)S(1)}, bf16[3,544,128]{2,1,0:T(8,128)(2,1)S(1)}, u32[]{:S(2)}, u32[]{:S(2)}) collective-permute-start(bf16[3,544,128]{2,1,0:T(8,128)(2,1)S(1)} %get-tuple-element.89), channel_id=1, source_target_pairs={{0,6},{1,7},{2,0},{3,1},{4,2},{5,3},{6,4},{7,5},{8,14},{9,15},{10,... | collective-permute-start | bytes 1253384 | tf_op jit(solution)/shard_map/ppermute | solution.py:36
  46.1 17.9 %collective-permute-start.10 = (bf16[544,512]{1,0:T(8,128)(2,1)S(1)}, bf16[544,512]{1,0:T(8,128)(2,1)S(1)}, u32[]{:S(2)}, u32[]{:S(2)}) collective-permute-start(bf16[544,512]{1,0:T(8,128)(2,1)S(1)} %slice.24), channel_id=1, source_target_pairs={{0,192},{8,200},{16,208},{24,216},{32,224},{40,232},{48,240},{56,2... | collective-permute-start | bytes 1671176 | tf_op jit(solution)/shard_map/ppermute | solution.py:28
  46.4 17.7 %collective-permute-start.9 = (bf16[544,512]{1,0:T(8,128)(2,1)S(1)}, bf16[544,512]{1,0:T(8,128)(2,1)}, u32[]{:S(2)}, u32[]{:S(2)}) collective-permute-start(bf16[544,512]{1,0:T(8,128)(2,1)S(1)} %slice.23), channel_id=1, source_target_pairs={{0,64},{8,72},{16,80},{24,88},{32,96},{40,104},{48,112},{56,120},{... | collective-permute-start | bytes 1671176 | tf_op jit(solution)/shard_map/ppermute | solution.py:28
  49.6 11.9 %collective-permute-start.7 = (bf16[3,272,128]{2,1,0:T(8,128)(2,1)S(1)}, bf16[3,272,128]{2,1,0:T(8,128)(2,1)S(1)}, u32[]{:S(2)}, u32[]{:S(2)}) collective-permute-start(bf16[3,272,128]{2,1,0:T(8,128)(2,1)S(1)} %slice.21), channel_id=1, source_target_pairs={{0,2},{1,3},{2,4},{3,5},{4,6},{5,7},{6,0},{7,1},{8,10},{9,11},{10,... | collective-permute-start | bytes 626696 | tf_op jit(solution)/shard_map/ppermute | solution.py:36
  53.1 10.9 %collective-permute-start.8 = (bf16[3,272,128]{2,1,0:T(8,128)(2,1)S(1)}, bf16[3,272,128]{2,1,0:T(8,128)(2,1)S(1)}, u32[]{:S(2)}, u32[]{:S(2)}) collective-permute-start(bf16[3,272,128]{2,1,0:T(8,128)(2,1)S(1)} %slice.22), channel_id=1, source_target_pairs={{0,6},{1,7},{2,0},{3,1},{4,2},{5,3},{6,4},{7,5},{8,14},{9,15},{10,... | collective-permute-start | bytes 626696 | tf_op jit(solution)/shard_map/ppermute | solution.py:36
  88.6 7.7 %collective-permute-start.13 = (f32[8,128]{1,0:T(8,128)S(1)}, f32[8,128]{1,0:T(8,128)S(1)}, u32[]{:S(2)}, u32[]{:S(2)}) collective-permute-start(f32[8,128]{1,0:T(8,128)S(1)} %add.135), channel_id=1, source_target_pairs={{0,4},{1,5},{2,6},{3,7},{4,0},{5,1},{6,2},{7,3},{8,12},{9,13},{10,... | collective-permute-start | bytes 12296 | tf_op jit(solution)/shard_map/ppermute | solution.py:36
  110.8 33.1 %collective-permute-start.16 = (bf16[1088,4096]{1,0:T(8,128)(2,1)}, bf16[1088,4096]{1,0:T(8,128)(2,1)}, u32[]{:S(2)}, u32[]{:S(2)}) collective-permute-start(bf16[1088,4096]{1,0:T(8,128)(2,1)} %all-gather.2.cloned.1.call-done.refs_0_.refs_1_.refs_2_.refs_3_), channel_id=1, source_target_pairs={{0,1},{1,0},{2,3},{3,2},{4,5},{5,4},{6,7},{7,6},{8,9},{9,8},{10,11... | collective-permute-start | bytes 26738696 | tf_op jit(solution)/shard_map/ppermute | solution.py:36
  151.0 9.0 %collective-permute-start.18 = (f32[40,128]{1,0:T(8,128)S(1)}, f32[40,128]{1,0:T(8,128)S(1)}, u32[]{:S(2)}, u32[]{:S(2)}) collective-permute-start(f32[40,128]{1,0:T(8,128)S(1)} %add.142), channel_id=1, source_target_pairs={{0,4},{1,5},{2,6},{3,7},{4,0},{5,1},{6,2},{7,3},{8,12},{9,13},{10,... | collective-permute-start | bytes 61448 | tf_op jit(solution)/shard_map/ppermute | solution.py:36
  176.3 13.2 %collective-permute-start.24 = (bf16[512,256]{1,0:T(8,128)(2,1)S(1)}, bf16[512,256]{1,0:T(8,128)(2,1)S(1)}, u32[]{:S(2)}, u32[]{:S(2)}) collective-permute-start(bf16[512,256]{1,0:T(8,128)(2,1)S(1)} %pad_maximum_fusion.2.refs_8_), channel_id=1, source_target_pairs={{0,64},{8,72},{16,80},{24,88},{32,96},{40,104},{48,112},{56,120},{... | collective-permute-start | bytes 786440 | tf_op jit(solution)/shard_map/ppermute | solution.py:28
  176.8 12.7 %collective-permute-start.25 = (bf16[512,256]{1,0:T(8,128)(2,1)S(1)}, bf16[512,256]{1,0:T(8,128)(2,1)S(1)}, u32[]{:S(2)}, u32[]{:S(2)}) collective-permute-start(bf16[512,256]{1,0:T(8,128)(2,1)S(1)} %pad_maximum_fusion.2.refs_8_), channel_id=1, source_target_pairs={{0,128},{8,136},{16,144},{24,152},{32,160},{40,168},{48,176},{56,1... | collective-permute-start | bytes 786440 | tf_op jit(solution)/shard_map/ppermute | solution.py:28
  179.2 10.3 %collective-permute-start.26 = (bf16[512,256]{1,0:T(8,128)(2,1)S(1)}, bf16[512,256]{1,0:T(8,128)(2,1)S(1)}, u32[]{:S(2)}, u32[]{:S(2)}) collective-permute-start(bf16[512,256]{1,0:T(8,128)(2,1)S(1)} %pad_maximum_fusion.2.refs_8_), channel_id=1, source_target_pairs={{0,192},{8,200},{16,208},{24,216},{32,224},{40,232},{48,240},{56,2... | collective-permute-start | bytes 786440 | tf_op jit(solution)/shard_map/ppermute | solution.py:28
  189.5 8.6 %collective-permute-start.28 = (bf16[512,256]{1,0:T(8,128)(2,1)S(1)}, bf16[512,256]{1,0:T(8,128)(2,1)S(1)}, u32[]{:S(2)}, u32[]{:S(2)}) collective-permute-start(bf16[512,256]{1,0:T(8,128)(2,1)S(1)} %collective-permute-done.27.refs_9_), channel_id=1, source_target_pairs={{0,64},{8,72},{16,80},{24,88},{32,96},{40,104},{48,112},{56,120},{... | collective-permute-start | bytes 786440 | tf_op jit(solution)/shard_map/ppermute | solution.py:28
  190.1 8.5 %collective-permute-start.29 = (bf16[512,256]{1,0:T(8,128)(2,1)S(1)}, bf16[512,256]{1,0:T(8,128)(2,1)S(1)}, u32[]{:S(2)}, u32[]{:S(2)}) collective-permute-start(bf16[512,256]{1,0:T(8,128)(2,1)S(1)} %collective-permute-done.27.refs_9_), channel_id=1, source_target_pairs={{0,128},{8,136},{16,144},{24,152},{32,160},{40,168},{48,176},{56,1... | collective-permute-start | bytes 786440 | tf_op jit(solution)/shard_map/ppermute | solution.py:28
  192.5 8.8 %collective-permute-start.30 = (bf16[512,256]{1,0:T(8,128)(2,1)S(1)}, bf16[512,256]{1,0:T(8,128)(2,1)S(1)}, u32[]{:S(2)}, u32[]{:S(2)}) collective-permute-start(bf16[512,256]{1,0:T(8,128)(2,1)S(1)} %collective-permute-done.27.refs_9_), channel_id=1, source_target_pairs={{0,192},{8,200},{16,208},{24,216},{32,224},{40,232},{48,240},{56,2... | collective-permute-start | bytes 786440 | tf_op jit(solution)/shard_map/ppermute | solution.py:28
  207.7 8.0 %collective-permute-start.31 = (bf16[2,272,256]{2,1,0:T(8,128)(2,1)S(1)}, bf16[2,272,256]{2,1,0:T(8,128)(2,1)S(1)}, u32[]{:S(2)}, u32[]{:S(2)}) collective-permute-start(bf16[2,272,256]{2,1,0:T(8,128)(2,1)S(1)} %get-tuple-element.82), channel_id=1, source_target_pairs={{0,16},{8,24},{16,32},{24,40},{32,48},{40,56},{48,0},{56,8},{64,80... | collective-permute-start | bytes 835592 | tf_op jit(solution)/shard_map/ppermute | solution.py:28
  208.7 8.9 %collective-permute-start.32 = (bf16[2,272,256]{2,1,0:T(8,128)(2,1)S(1)}, bf16[2,272,256]{2,1,0:T(8,128)(2,1)S(1)}, u32[]{:S(2)}, u32[]{:S(2)}) collective-permute-start(bf16[2,272,256]{2,1,0:T(8,128)(2,1)S(1)} %get-tuple-element.83), channel_id=1, source_target_pairs={{0,32},{8,40},{16,48},{24,56},{32,0},{40,8},{48,16},{56,24},{64,96... | collective-permute-start | bytes 835592 | tf_op jit(solution)/shard_map/ppermute | solution.py:28
  210.1 10.4 %collective-permute-start.33 = (bf16[2,272,256]{2,1,0:T(8,128)(2,1)S(1)}, bf16[2,272,256]{2,1,0:T(8,128)(2,1)S(1)}, u32[]{:S(2)}, u32[]{:S(2)}) collective-permute-start(bf16[2,272,256]{2,1,0:T(8,128)(2,1)S(1)} %get-tuple-element.84), channel_id=1, source_target_pairs={{0,48},{8,56},{16,0},{24,8},{32,16},{40,24},{48,32},{56,40},{64,11... | collective-permute-start | bytes 835592 | tf_op jit(solution)/shard_map/ppermute | solution.py:28
  (27 other events, 201.2 us)
Sparse Core Ops, SparseCore 0:
  18.7 92.0 all-gather.1

commit v4 on v3

--- a/solution.py
+++ b/solution.py
@@ -36,8 +36,11 @@
     return lax.ppermute(block, "mp", route)
 
 
-def sum_mp(part):
-    part = part + move_mp(part, dc=1)
+def sum_cores(part):
+    return part + move_mp(part, dc=1)
+
+
+def sum_z(part):
     one, two, three = move_mp(part, dh=1), move_mp(part, dh=2), move_mp(part, dh=3)
     return (part + two) + (one + three)
 
@@ -110,10 +113,10 @@
             ],
         ),
         out_shape=[
-            jax.ShapeDtypeStruct((blocks, 4, BLK, cols), F32),
+            pltpu.VMEM((blocks, 4, BLK, cols), F32),
             jax.ShapeDtypeStruct((8, 128), F32),
         ],
-        compiler_params=pltpu.CompilerParams(vmem_limit_bytes=60 * 2**20),
+        compiler_params=pltpu.CompilerParams(vmem_limit_bytes=44 * 2**20),
     )(place, tokens, mine, other, outs[0], outs[1], *outs[2], outs[3])
 
 
@@ -345,6 +348,7 @@
         in_specs=[pl.BlockSpec(memory_space=pltpu.SMEM)] + [pl.BlockSpec(memory_space=pltpu.VMEM)] * NX,
         out_specs=pl.BlockSpec(memory_space=pltpu.VMEM),
         out_shape=jax.ShapeDtypeStruct((2 * part, NX * cols), jnp.bfloat16),
+        compiler_params=pltpu.CompilerParams(vmem_limit_bytes=16 * 2**20),
     )(place, *parts)
 
 
@@ -392,14 +396,15 @@
     mine = jnp.stack([piece, up, far, down])
     other = move_mp(mine, dc=1)
     grads, gram = grads_and_gram(here, tokens, mine, other, [out_grad, near[0], far_out, near[1]])
-    coded = mix(sum_mp(gram), grads, tok_dev).astype(jnp.float16)
+    coded = mix(sum_z(sum_cores(gram)), grads, tok_dev).astype(jnp.float16)
     rings = [[ring * group + k for k in range(group)] for ring in range(NY)]
-    coded, next_mine = lax.optimization_barrier((coded, next_mine))
+    landed = lax.all_to_all(coded, "dp", 0, 0, axis_index_groups=rings)
+    parts = decode(landed)
+    gram = sum_cores(gram8(parts))
+    gram, next_mine = lax.optimization_barrier((gram, next_mine))
     next_other = move_mp(next_mine, dc=1)
-    landed = lax.all_to_all(coded, "dp", 0, 0, axis_index_groups=rings)
-    landed, next_other = lax.optimization_barrier((landed, next_other))
-    parts = decode(landed)
-    new_weight, new_momentum, weight_half = update(sum_mp(gram8(parts)), parts, weight, momentum)
+    new_weight, new_momentum, weight_half = update(sum_z(gram), parts, weight, momentum)
+    weight_half, next_other = lax.optimization_barrier((weight_half, next_other))
     projected = gather_and_project(here, weight_half, next_mine, next_other)
     return (new_weight, new_momentum, projected)
 

time: 235 us -> 226 us (0.962)
  local copies, waits for them, and re-layouts: 20.4 us -> 13 us
    unnamed x33 -> x23, local copies, waits for them, and re-layouts: 15 us -> 7.77 us
    ppermute x20, waiting for transfers between devices: 25.8 us -> 28.3 us  [move_dp(): return lax.ppermute(block, 'dp', route)]
  transfers between devices with their start and end apart: 35 -> 35, of which waited for: 24 -> 25; matrix products, arithmetic and copies ran while one was open for 2% -> 4% of each run, Pallas kernels for 14% -> 17%
where the time goes in v4:
time: 226 us; the launch traced here: 223 us
  waiting for transfers between devices  63.6 us (28%)
  starting transfers between devices  52.7 us (23%)
  Pallas kernels  44.6 us (20%)
  blocking collectives  31.1 us (14%)
  between operations  14.4 us (6%)
  local copies, waits for them, and re-layouts  13 us (6%)
  other arithmetic  3.79 us (2%)
    ppermute x14, waiting for transfers between devices, move_mp(): return lax.ppermute(block, 'mp', route)  35.2 us
    all_to_all x1, blocking collectives, shards(): landed = lax.all_to_all(coded, 'dp', 0, 0, axis_index_groups=rings)  31.1 us
    ppermute x14, starting transfers between devices, move_mp(): return lax.ppermute(block, 'mp', route)  31.1 us
    ppermute x20, waiting for transfers between devices, move_dp(): return lax.ppermute(block, 'dp', route)  28.3 us
    ppermute x20, starting transfers between devices, move_dp(): return lax.ppermute(block, 'dp', route)  21.6 us
    pallas_call x1, Pallas kernels, grads_and_gram(): pl.pallas_call(grads_kernel, grid_spec=pltpu.PrefetchScalarGridSpec(num_s...  19.4 us
    pallas_call x3, Pallas kernels, project(): pl.pallas_call(functools.partial(project_kernel, units, len(begin), last)...  15.2 us
    unnamed x23, local copies, waits for them, and re-layouts  7.77 us
  transfers between devices with their start and end apart: 35, of which 25 were waited for; matrix products, arithmetic and copies ran while one was open for 4% of the time, Pallas kernels for 17%

profile of v4, /device:TPU:30, one launch (start us, length us, event | category | flops | bytes accessed | tf_op | source)
XLA Modules:
  0.0 223.3 jit_solution(3305057413860077673)
XLA Ops:
  11.4 3.2 %constant_dynamic-slice_fusion.4 = bf16[272,4096]{1,0:T(8,128)(2,1)} fusion(bf16[544,4096]{1,0:T(8,128)(2,1)} %param.9, s32[]{:T(128)S(6)} %select_n.95), kind=kLoop, calls=%fused_computation.30 | loop fusion | bytes 4456452 | tf_op jit(solution)/shard_map/dynamic_slice | solution.py:383
  20.8 3.3 %collective-permute-start.5 = (bf16[3,544,128]{2,1,0:T(8,128)(2,1)S(1)}, bf16[3,544,128]{2,1,0:T(8,128)(2,1)S(1)}, u32[]{:S(2)}, u32[]{:S(2)}) collective-permute-start(bf16[3,544,128]{2,1,0:T(8,128)(2,1)S(1)} %get-tuple-element.89), channel_id=1, source_target_pairs={{0,2},{1,3},{2,4},{3,5},{4,6},{5,7},{6,0},{7,1},{8,10},{9,11},{10,... | collective-permute-start | bytes 1253384 | tf_op jit(solution)/shard_map/ppermute | solution.py:36
  24.1 3.1 %collective-permute-start.6 = (bf16[3,544,128]{2,1,0:T(8,128)(2,1)S(1)}, bf16[3,544,128]{2,1,0:T(8,128)(2,1)S(1)}, u32[]{:S(2)}, u32[]{:S(2)}) collective-permute-start(bf16[3,544,128]{2,1,0:T(8,128)(2,1)S(1)} %get-tuple-element.89), channel_id=1, source_target_pairs={{0,6},{1,7},{2,0},{3,1},{4,2},{5,3},{6,4},{7,5},{8,14},{9,15},{10,... | collective-permute-start | bytes 1253384 | tf_op jit(solution)/shard_map/ppermute | solution.py:36
  27.2 11.8 %collective-permute-done.5 = bf16[3,544,128]{2,1,0:T(8,128)(2,1)S(1)} collective-permute-done((bf16[3,544,128]{2,1,0:T(8,128)(2,1)S(1)}, bf16[3,544,128]{2,1,0:T(8,128)(2,1)S(1)}, u32[]{:S(2)}, u32[]{:S(2)}) %collective-permute-start.5) | collective-permute-done | bytes 417824 | tf_op jit(solution)/shard_map/ppermute | solution.py:36
  39.1 6.7 %collective-permute-done.6 = bf16[3,544,128]{2,1,0:T(8,128)(2,1)S(1)} collective-permute-done((bf16[3,544,128]{2,1,0:T(8,128)(2,1)S(1)}, bf16[3,544,128]{2,1,0:T(8,128)(2,1)S(1)}, u32[]{:S(2)}, u32[]{:S(2)}) %collective-permute-start.6) | collective-permute-done | bytes 417824 | tf_op jit(solution)/shard_map/ppermute | solution.py:36
  46.4 3.2 %collective-permute-start.9 = (bf16[544,512]{1,0:T(8,128)(2,1)S(1)}, bf16[544,512]{1,0:T(8,128)(2,1)}, u32[]{:S(2)}, u32[]{:S(2)}) collective-permute-start(bf16[544,512]{1,0:T(8,128)(2,1)S(1)} %slice.23), channel_id=1, source_target_pairs={{0,64},{8,72},{16,80},{24,88},{32,96},{40,104},{48,112},{56,120},{... | collective-permute-start | bytes 1671176 | tf_op jit(solution)/shard_map/ppermute | solution.py:28
  49.6 3.5 %collective-permute-start.7 = (bf16[3,272,128]{2,1,0:T(8,128)(2,1)S(1)}, bf16[3,272,128]{2,1,0:T(8,128)(2,1)S(1)}, u32[]{:S(2)}, u32[]{:S(2)}) collective-permute-start(bf16[3,272,128]{2,1,0:T(8,128)(2,1)S(1)} %slice.21), channel_id=1, source_target_pairs={{0,2},{1,3},{2,4},{3,5},{4,6},{5,7},{6,0},{7,1},{8,10},{9,11},{10,... | collective-permute-start | bytes 626696 | tf_op jit(solution)/shard_map/ppermute | solution.py:36
  53.1 3.0 %collective-permute-start.8 = (bf16[3,272,128]{2,1,0:T(8,128)(2,1)S(1)}, bf16[3,272,128]{2,1,0:T(8,128)(2,1)S(1)}, u32[]{:S(2)}, u32[]{:S(2)}) collective-permute-start(bf16[3,272,128]{2,1,0:T(8,128)(2,1)S(1)} %slice.22), channel_id=1, source_target_pairs={{0,6},{1,7},{2,0},{3,1},{4,2},{5,3},{6,4},{7,5},{8,14},{9,15},{10,... | collective-permute-start | bytes 626696 | tf_op jit(solution)/shard_map/ppermute | solution.py:36
  56.1 5.4 %collective-permute-done.7 = bf16[3,272,128]{2,1,0:T(8,128)(2,1)S(1)} collective-permute-done((bf16[3,272,128]{2,1,0:T(8,128)(2,1)S(1)}, bf16[3,272,128]{2,1,0:T(8,128)(2,1)S(1)}, u32[]{:S(2)}, u32[]{:S(2)}) %collective-permute-start.7) | collective-permute-done | bytes 208928 | tf_op jit(solution)/shard_map/ppermute | solution.py:36
  65.4 2.9 %collective-permute-done.11.other_ref = bf16[4,3,544,128]{3,2,1,0:T(8,128)(2,1)} collective-permute-done((bf16[4,3,544,128]{3,2,1,0:T(8,128)(2,1)S(1)}, bf16[4,3,544,128]{3,2,1,0:T(8,128)(2,1)}, u32[]{:S(2)}, u32[]{:S(2)}) %collective-permute-start.11) | collective-permute-done | bytes 1671200 | tf_op jit(solution)/shard_map/ppermute | solution.py:36
  68.3 19.4 %shard_map.76 = (f32[8,4,128,1024]{3,2,1,0:T(8,128)S(1)}, f32[8,128]{1,0:T(8,128)}) custom-call(s32[5]{0:T(128)} %stack.50.place, bf16[544,4096]{1,0:T(8,128)(2,1)} %tokens_ref.1, bf16[4,3,544,128]{3,2,1,0:T(8,128)(2,1)} %copy-done.6, bf16[4,3,544,128]{3,2,1,0:T(8,128)(2,1)} %collective-permute-done.11.other_ref, bf16[544,1024]{1,0:T(8,128)(2,1)} %o0_ref, ...), custom_call_target="tpu_custom_call" | custom-call | tf_op jit(solution)/shard_map/pallas_call | solution.py:99
  89.7 3.4 %collective-permute-start.13 = (f32[8,128]{1,0:T(8,128)S(1)}, f32[8,128]{1,0:T(8,128)S(1)}, u32[]{:S(2)}, u32[]{:S(2)}) collective-permute-start(f32[8,128]{1,0:T(8,128)S(1)} %add.135), channel_id=1, source_target_pairs={{0,4},{1,5},{2,6},{3,7},{4,0},{5,1},{6,2},{7,3},{8,12},{9,13},{10,... | collective-permute-start | bytes 12296 | tf_op jit(solution)/shard_map/ppermute | solution.py:36
  94.7 2.8 %collective-permute-start.15 = (f32[8,128]{1,0:T(8,128)S(1)}, f32[8,128]{1,0:T(8,128)S(1)}, u32[]{:S(2)}, u32[]{:S(2)}) collective-permute-start(f32[8,128]{1,0:T(8,128)S(1)} %add.135), channel_id=1, source_target_pairs={{0,6},{1,7},{2,0},{3,1},{4,2},{5,3},{6,4},{7,5},{8,14},{9,15},{10,... | collective-permute-start | bytes 12296 | tf_op jit(solution)/shard_map/ppermute | solution.py:36
  99.2 4.4 %shard_map.77 = f32[8,136,1024]{2,1,0:T(8,128)S(1)} custom-call(f32[8,128]{1,0:T(8,128)S(1)} %add_add_fusion.1.gram_ref, f32[8,4,128,1024]{3,2,1,0:T(8,128)S(1)} %get-tuple-element.63.grads_ref), custom_call_target="tpu_custom_call" | custom-call | tf_op jit(solution)/shard_map/pallas_call | solution.py:178
  104.1 31.1 %all_to_all.5 = f16[8,136,1024]{2,1,0:T(8,128)(2,1)S(1)} all-to-all(f16[8,136,1024]{2,1,0:T(8,128)(2,1)S(1)} %convert_element_type.12), channel_id=1, replica_groups={{0,8,16,24,32,40,48,56},{64,72,80,88,96,104,112,120},{128,136,144,152,1..., dimensions={0} | all-to-all | bytes 4456448 | tf_op jit(solution)/shard_map/all_to_all | solution.py:401
  142.4 5.7 %collective-permute-start.17 = (f32[40,128]{1,0:T(8,128)S(1)}, f32[40,128]{1,0:T(8,128)S(1)}, u32[]{:S(2)}, u32[]{:S(2)}) collective-permute-start(f32[40,128]{1,0:T(8,128)S(1)} %add.142), channel_id=1, source_target_pairs={{0,4},{1,5},{2,6},{3,7},{4,0},{5,1},{6,2},{7,3},{8,12},{9,13},{10,... | collective-permute-start | bytes 61448 | tf_op jit(solution)/shard_map/ppermute | solution.py:36
  149.0 3.3 %collective-permute-start.19 = (f32[40,128]{1,0:T(8,128)S(1)}, f32[40,128]{1,0:T(8,128)S(1)}, u32[]{:S(2)}, u32[]{:S(2)}) collective-permute-start(f32[40,128]{1,0:T(8,128)S(1)} %add.142), channel_id=1, source_target_pairs={{0,6},{1,7},{2,0},{3,1},{4,2},{5,3},{6,4},{7,5},{8,14},{9,15},{10,... | collective-permute-start | bytes 61448 | tf_op jit(solution)/shard_map/ppermute | solution.py:36
  170.8 2.8 %collective-permute-done.27.refs_9_ = bf16[512,256]{1,0:T(8,128)(2,1)S(1)} collective-permute-done((bf16[512,256]{1,0:T(8,128)(2,1)S(1)}, bf16[512,256]{1,0:T(8,128)(2,1)S(1)}, u32[]{:S(2)}, u32[]{:S(2)}) %collective-permute-start.27) | collective-permute-done | bytes 262176 | tf_op jit(solution)/shard_map/ppermute | solution.py:28
  173.6 3.5 %copy-done = bf16[1088,4096]{1,0:T(8,128)(2,1)S(1)} copy-done((bf16[1088,4096]{1,0:T(8,128)(2,1)S(1)}, bf16[1088,4096]{1,0:T(8,128)(2,1)}, u32[]{:S(2)}) %copy-start) | copy-done | bytes 8912920
  177.1 4.0 %shard_map.80.refs_11_ = f32[2,1088,256]{2,1,0:T(8,128)S(1)} custom-call(s32[5]{0:T(128)S(1)} %copy-done.5, bf16[1088,4096]{1,0:T(8,128)(2,1)S(1)} %copy-done, bf16[1088,4096]{1,0:T(8,128)(2,1)S(1)} %copy-done, bf16[1088,4096]{1,0:T(8,128)(2,1)S(1)} %copy-done, bf16[1088,4096]{1,0:T(8,128)(2,1)S(1)} %copy-done, ...), custom_call_target="tpu_custom_call" | custom-call | tf_op jit(solution)/shard_map/pallas_call | solution.py:320
  184.0 5.5 %shard_map.81.refs_11_ = f32[2,1088,256]{2,1,0:T(8,128)S(1)} custom-call(s32[5]{0:T(128)S(1)} %copy-done.5, bf16[1088,4096]{1,0:T(8,128)(2,1)S(1)} %copy-done, bf16[1088,4096]{1,0:T(8,128)(2,1)S(1)} %copy-done, bf16[1088,4096]{1,0:T(8,128)(2,1)S(1)} %copy-done, bf16[1088,4096]{1,0:T(8,128)(2,1)S(1)} %copy-done, ...), custom_call_target="tpu_custom_call" | custom-call | tf_op jit(solution)/shard_map/pallas_call | solution.py:320
  194.6 5.7 %shard_map.82 = (bf16[2,272,256]{2,1,0:T(8,128)(2,1)S(1)}, bf16[2,272,256]{2,1,0:T(8,128)(2,1)S(1)}, bf16[2,272,256]{2,1,0:T(8,128)(2,1)S(1)}, bf16[2,272,256]{2,1,0:T(8,128)(2,1)S(1)}) custom-call(s32[5]{0:T(128)S(1)} %copy-done.5, bf16[1088,4096]{1,0:T(8,128)(2,1)S(1)} %copy-done, bf16[1088,4096]{1,0:T(8,128)(2,1)S(1)} %copy-done, ...), custom_call_target="tpu_custom_call" | custom-call | tf_op jit(solution)/shard_map/pallas_call | solution.py:320
  203.1 6.7 %collective-permute-done.31.p1_ref = bf16[2,272,256]{2,1,0:T(8,128)(2,1)S(1)} collective-permute-done((bf16[2,272,256]{2,1,0:T(8,128)(2,1)S(1)}, bf16[2,272,256]{2,1,0:T(8,128)(2,1)S(1)}, u32[]{:S(2)}, u32[]{:S(2)}) %collective-permute-start.31) | collective-permute-done | bytes 278560 | tf_op jit(solution)/shard_map/ppermute | solution.py:28
  211.8 2.9 %collective-permute-done.33.p3_ref = bf16[2,272,256]{2,1,0:T(8,128)(2,1)S(1)} collective-permute-done((bf16[2,272,256]{2,1,0:T(8,128)(2,1)S(1)}, bf16[2,272,256]{2,1,0:T(8,128)(2,1)S(1)}, u32[]{:S(2)}, u32[]{:S(2)}) %collective-permute-start.33) | collective-permute-done | bytes 278560 | tf_op jit(solution)/shard_map/ppermute | solution.py:28
  (98 shorter events, 61.4 us)
Async XLA Ops:
  7.2 135.1 %all-gather.2.cloned.1.call-start = ((), (), s32[]{:S(2)}) async-start(), calls=%async_computation.1 | async-start | bytes 11141120 | tf_op jit(solution)/shard_map/all_gather | solution.py:386
  8.5 6.6 %collective-permute-start = (bf16[544,128]{1,0:T(8,128)(2,1)S(1)}, bf16[544,128]{1,0:T(8,128)(2,1)S(1)}, u32[]{:S(2)}, u32[]{:S(2)}) collective-permute-start(bf16[544,128]{1,0:T(8,128)(2,1)S(1)} %get-tuple-element.44), channel_id=1, source_target_pairs={{0,64},{8,72},{16,80},{24,88},{32,96},{40,104},{48,112},{56,120},{... | collective-permute-start | bytes 417800 | tf_op jit(solution)/shard_map/ppermute | solution.py:28
  8.8 7.8 %collective-permute-start.1 = (bf16[544,128]{1,0:T(8,128)(2,1)S(1)}, bf16[544,128]{1,0:T(8,128)(2,1)S(1)}, u32[]{:S(2)}, u32[]{:S(2)}) collective-permute-start(bf16[544,128]{1,0:T(8,128)(2,1)S(1)} %get-tuple-element.45), channel_id=1, source_target_pairs={{0,128},{8,136},{16,144},{24,152},{32,160},{40,168},{48,176},{56,1... | collective-permute-start | bytes 417800 | tf_op jit(solution)/shard_map/ppermute | solution.py:28
  11.4 7.2 %collective-permute-start.2 = (bf16[544,128]{1,0:T(8,128)(2,1)S(1)}, bf16[544,128]{1,0:T(8,128)(2,1)S(1)}, u32[]{:S(2)}, u32[]{:S(2)}) collective-permute-start(bf16[544,128]{1,0:T(8,128)(2,1)S(1)} %get-tuple-element.46), channel_id=1, source_target_pairs={{0,192},{8,200},{16,208},{24,216},{32,224},{40,232},{48,240},{56,2... | collective-permute-start | bytes 417800 | tf_op jit(solution)/shard_map/ppermute | solution.py:28
  18.6 27.2 %collective-permute-start.3 = (bf16[544,1024]{1,0:T(8,128)(2,1)S(1)}, bf16[544,1024]{1,0:T(8,128)(2,1)S(1)}, u32[]{:S(2)}, u32[]{:S(2)}) collective-permute-start(bf16[544,1024]{1,0:T(8,128)(2,1)S(1)} %copy-done.9), channel_id=1, source_target_pairs={{0,64},{8,72},{16,80},{24,88},{32,96},{40,104},{48,112},{56,120},{... | collective-permute-start | bytes 3342344 | tf_op jit(solution)/shard_map/ppermute | solution.py:28
  19.7 26.4 %collective-permute-start.4 = (bf16[544,1024]{1,0:T(8,128)(2,1)S(1)}, bf16[544,1024]{1,0:T(8,128)(2,1)S(1)}, u32[]{:S(2)}, u32[]{:S(2)}) collective-permute-start(bf16[544,1024]{1,0:T(8,128)(2,1)S(1)} %copy-done.9), channel_id=1, source_target_pairs={{0,192},{8,200},{16,208},{24,216},{32,224},{40,232},{48,240},{56,2... | collective-permute-start | bytes 3342344 | tf_op jit(solution)/shard_map/ppermute | solution.py:28
  20.8 18.3 %collective-permute-start.5 = (bf16[3,544,128]{2,1,0:T(8,128)(2,1)S(1)}, bf16[3,544,128]{2,1,0:T(8,128)(2,1)S(1)}, u32[]{:S(2)}, u32[]{:S(2)}) collective-permute-start(bf16[3,544,128]{2,1,0:T(8,128)(2,1)S(1)} %get-tuple-element.89), channel_id=1, source_target_pairs={{0,2},{1,3},{2,4},{3,5},{4,6},{5,7},{6,0},{7,1},{8,10},{9,11},{10,... | collective-permute-start | bytes 1253384 | tf_op jit(solution)/shard_map/ppermute | solution.py:36
  24.1 21.6 %collective-permute-start.6 = (bf16[3,544,128]{2,1,0:T(8,128)(2,1)S(1)}, bf16[3,544,128]{2,1,0:T(8,128)(2,1)S(1)}, u32[]{:S(2)}, u32[]{:S(2)}) collective-permute-start(bf16[3,544,128]{2,1,0:T(8,128)(2,1)S(1)} %get-tuple-element.89), channel_id=1, source_target_pairs={{0,6},{1,7},{2,0},{3,1},{4,2},{5,3},{6,4},{7,5},{8,14},{9,15},{10,... | collective-permute-start | bytes 1253384 | tf_op jit(solution)/shard_map/ppermute | solution.py:36
  46.1 17.9 %collective-permute-start.10 = (bf16[544,512]{1,0:T(8,128)(2,1)S(1)}, bf16[544,512]{1,0:T(8,128)(2,1)S(1)}, u32[]{:S(2)}, u32[]{:S(2)}) collective-permute-start(bf16[544,512]{1,0:T(8,128)(2,1)S(1)} %slice.24), channel_id=1, source_target_pairs={{0,192},{8,200},{16,208},{24,216},{32,224},{40,232},{48,240},{56,2... | collective-permute-start | bytes 1671176 | tf_op jit(solution)/shard_map/ppermute | solution.py:28
  46.4 17.7 %collective-permute-start.9 = (bf16[544,512]{1,0:T(8,128)(2,1)S(1)}, bf16[544,512]{1,0:T(8,128)(2,1)}, u32[]{:S(2)}, u32[]{:S(2)}) collective-permute-start(bf16[544,512]{1,0:T(8,128)(2,1)S(1)} %slice.23), channel_id=1, source_target_pairs={{0,64},{8,72},{16,80},{24,88},{32,96},{40,104},{48,112},{56,120},{... | collective-permute-start | bytes 1671176 | tf_op jit(solution)/shard_map/ppermute | solution.py:28
  49.6 11.9 %collective-permute-start.7 = (bf16[3,272,128]{2,1,0:T(8,128)(2,1)S(1)}, bf16[3,272,128]{2,1,0:T(8,128)(2,1)S(1)}, u32[]{:S(2)}, u32[]{:S(2)}) collective-permute-start(bf16[3,272,128]{2,1,0:T(8,128)(2,1)S(1)} %slice.21), channel_id=1, source_target_pairs={{0,2},{1,3},{2,4},{3,5},{4,6},{5,7},{6,0},{7,1},{8,10},{9,11},{10,... | collective-permute-start | bytes 626696 | tf_op jit(solution)/shard_map/ppermute | solution.py:36
  53.1 10.9 %collective-permute-start.8 = (bf16[3,272,128]{2,1,0:T(8,128)(2,1)S(1)}, bf16[3,272,128]{2,1,0:T(8,128)(2,1)S(1)}, u32[]{:S(2)}, u32[]{:S(2)}) collective-permute-start(bf16[3,272,128]{2,1,0:T(8,128)(2,1)S(1)} %slice.22), channel_id=1, source_target_pairs={{0,6},{1,7},{2,0},{3,1},{4,2},{5,3},{6,4},{7,5},{8,14},{9,15},{10,... | collective-permute-start | bytes 626696 | tf_op jit(solution)/shard_map/ppermute | solution.py:36
  89.7 7.7 %collective-permute-start.13 = (f32[8,128]{1,0:T(8,128)S(1)}, f32[8,128]{1,0:T(8,128)S(1)}, u32[]{:S(2)}, u32[]{:S(2)}) collective-permute-start(f32[8,128]{1,0:T(8,128)S(1)} %add.135), channel_id=1, source_target_pairs={{0,4},{1,5},{2,6},{3,7},{4,0},{5,1},{6,2},{7,3},{8,12},{9,13},{10,... | collective-permute-start | bytes 12296 | tf_op jit(solution)/shard_map/ppermute | solution.py:36
  142.2 16.4 %collective-permute-start.20 = (bf16[1088,4096]{1,0:T(8,128)(2,1)}, bf16[1088,4096]{1,0:T(8,128)(2,1)}, u32[]{:S(2)}, u32[]{:S(2)}) collective-permute-start(bf16[1088,4096]{1,0:T(8,128)(2,1)} %all-gather.2.cloned.1.call-done.refs_0_.refs_1_.refs_2_.refs_3_), channel_id=1, source_target_pairs={{0,1},{1,0},{2,3},{3,2},{4,5},{5,4},{6,7},{7,6},{8,9},{9,8},{10,11... | collective-permute-start | bytes 26738696 | tf_op jit(solution)/shard_map/ppermute | solution.py:36
  142.4 9.8 %collective-permute-start.17 = (f32[40,128]{1,0:T(8,128)S(1)}, f32[40,128]{1,0:T(8,128)S(1)}, u32[]{:S(2)}, u32[]{:S(2)}) collective-permute-start(f32[40,128]{1,0:T(8,128)S(1)} %add.142), channel_id=1, source_target_pairs={{0,4},{1,5},{2,6},{3,7},{4,0},{5,1},{6,2},{7,3},{8,12},{9,13},{10,... | collective-permute-start | bytes 61448 | tf_op jit(solution)/shard_map/ppermute | solution.py:36
  167.9 13.2 %collective-permute-start.24 = (bf16[512,256]{1,0:T(8,128)(2,1)S(1)}, bf16[512,256]{1,0:T(8,128)(2,1)S(1)}, u32[]{:S(2)}, u32[]{:S(2)}) collective-permute-start(bf16[512,256]{1,0:T(8,128)(2,1)S(1)} %pad_maximum_fusion.2.refs_8_), channel_id=1, source_target_pairs={{0,64},{8,72},{16,80},{24,88},{32,96},{40,104},{48,112},{56,120},{... | collective-permute-start | bytes 786440 | tf_op jit(solution)/shard_map/ppermute | solution.py:28
  169.2 12.0 %collective-permute-start.25 = (bf16[512,256]{1,0:T(8,128)(2,1)S(1)}, bf16[512,256]{1,0:T(8,128)(2,1)S(1)}, u32[]{:S(2)}, u32[]{:S(2)}) collective-permute-start(bf16[512,256]{1,0:T(8,128)(2,1)S(1)} %pad_maximum_fusion.2.refs_8_), channel_id=1, source_target_pairs={{0,128},{8,136},{16,144},{24,152},{32,160},{40,168},{48,176},{56,1... | collective-permute-start | bytes 786440 | tf_op jit(solution)/shard_map/ppermute | solution.py:28
  170.8 10.5 %collective-permute-start.26 = (bf16[512,256]{1,0:T(8,128)(2,1)S(1)}, bf16[512,256]{1,0:T(8,128)(2,1)S(1)}, u32[]{:S(2)}, u32[]{:S(2)}) collective-permute-start(bf16[512,256]{1,0:T(8,128)(2,1)S(1)} %pad_maximum_fusion.2.refs_8_), channel_id=1, source_target_pairs={{0,192},{8,200},{16,208},{24,216},{32,224},{40,232},{48,240},{56,2... | collective-permute-start | bytes 786440 | tf_op jit(solution)/shard_map/ppermute | solution.py:28
  181.3 9.0 %collective-permute-start.28 = (bf16[512,256]{1,0:T(8,128)(2,1)S(1)}, bf16[512,256]{1,0:T(8,128)(2,1)S(1)}, u32[]{:S(2)}, u32[]{:S(2)}) collective-permute-start(bf16[512,256]{1,0:T(8,128)(2,1)S(1)} %collective-permute-done.27.refs_9_), channel_id=1, source_target_pairs={{0,64},{8,72},{16,80},{24,88},{32,96},{40,104},{48,112},{56,120},{... | collective-permute-start | bytes 786440 | tf_op jit(solution)/shard_map/ppermute | solution.py:28
  182.7 9.2 %collective-permute-start.29 = (bf16[512,256]{1,0:T(8,128)(2,1)S(1)}, bf16[512,256]{1,0:T(8,128)(2,1)S(1)}, u32[]{:S(2)}, u32[]{:S(2)}) collective-permute-start(bf16[512,256]{1,0:T(8,128)(2,1)S(1)} %collective-permute-done.27.refs_9_), channel_id=1, source_target_pairs={{0,128},{8,136},{16,144},{24,152},{32,160},{40,168},{48,176},{56,1... | collective-permute-start | bytes 786440 | tf_op jit(solution)/shard_map/ppermute | solution.py:28
  184.0 10.6 %collective-permute-start.30 = (bf16[512,256]{1,0:T(8,128)(2,1)S(1)}, bf16[512,256]{1,0:T(8,128)(2,1)S(1)}, u32[]{:S(2)}, u32[]{:S(2)}) collective-permute-start(bf16[512,256]{1,0:T(8,128)(2,1)S(1)} %collective-permute-done.27.refs_9_), channel_id=1, source_target_pairs={{0,192},{8,200},{16,208},{24,216},{32,224},{40,232},{48,240},{56,2... | collective-permute-start | bytes 786440 | tf_op jit(solution)/shard_map/ppermute | solution.py:28
  200.2 9.5 %collective-permute-start.31 = (bf16[2,272,256]{2,1,0:T(8,128)(2,1)S(1)}, bf16[2,272,256]{2,1,0:T(8,128)(2,1)S(1)}, u32[]{:S(2)}, u32[]{:S(2)}) collective-permute-start(bf16[2,272,256]{2,1,0:T(8,128)(2,1)S(1)} %get-tuple-element.82), channel_id=1, source_target_pairs={{0,16},{8,24},{16,32},{24,40},{32,48},{40,56},{48,0},{56,8},{64,80... | collective-permute-start | bytes 835592 | tf_op jit(solution)/shard_map/ppermute | solution.py:28
  201.1 10.8 %collective-permute-start.32 = (bf16[2,272,256]{2,1,0:T(8,128)(2,1)S(1)}, bf16[2,272,256]{2,1,0:T(8,128)(2,1)S(1)}, u32[]{:S(2)}, u32[]{:S(2)}) collective-permute-start(bf16[2,272,256]{2,1,0:T(8,128)(2,1)S(1)} %get-tuple-element.83), channel_id=1, source_target_pairs={{0,32},{8,40},{16,48},{24,56},{32,0},{40,8},{48,16},{56,24},{64,96... | collective-permute-start | bytes 835592 | tf_op jit(solution)/shard_map/ppermute | solution.py:28
  202.3 12.4 %collective-permute-start.33 = (bf16[2,272,256]{2,1,0:T(8,128)(2,1)S(1)}, bf16[2,272,256]{2,1,0:T(8,128)(2,1)S(1)}, u32[]{:S(2)}, u32[]{:S(2)}) collective-permute-start(bf16[2,272,256]{2,1,0:T(8,128)(2,1)S(1)} %get-tuple-element.84), channel_id=1, source_target_pairs={{0,48},{8,56},{16,0},{24,8},{32,16},{40,24},{48,32},{56,40},{64,11... | collective-permute-start | bytes 835592 | tf_op jit(solution)/shard_map/ppermute | solution.py:28
  (22 other events, 188.0 us)
Sparse Core Ops, SparseCore 0:
  18.7 92.6 all-gather.1

commit v5 on v4

--- a/solution.py
+++ b/solution.py
@@ -381,7 +381,8 @@
     sent, next_tokens = lax.optimization_barrier((sent, next_tokens))
     sent = [move_dp(block, dy=k) for k, block in zip((1, 2, 3), sent)]
     next_half = lax.dynamic_slice_in_dim(next_tokens, (mp % NC) * (tok_dev // 2), tok_dev // 2, 0)
-    sent, out_grad, next_half = lax.optimization_barrier((sent, out_grad, next_half))
+    out_grad, next_half = lax.optimization_barrier((out_grad, next_half))
+    sent, next_half = lax.optimization_barrier((sent, next_half))
     x_rings = [[(a * NX + k) * NZ + b for k in range(NX)] for a in range(NY) for b in range(NZ)]
     next_mine = lax.all_gather(next_half, "dp", axis_index_groups=x_rings, tiled=True)
     piece = jnp.stack(sent)

time: 226 us -> 226 us (level)
  no operation moved by 1% of the time
where the time goes in v5:
time: 226 us; the launch traced here: 223 us
  waiting for transfers between devices  63.6 us (28%)
  starting transfers between devices  52.7 us (23%)
  Pallas kernels  44.6 us (20%)
  blocking collectives  31.1 us (14%)
  between operations  14.4 us (6%)
  local copies, waits for them, and re-layouts  13 us (6%)
  other arithmetic  3.79 us (2%)
    ppermute x14, waiting for transfers between devices, move_mp(): return lax.ppermute(block, 'mp', route)  35.2 us
    all_to_all x1, blocking collectives, shards(): landed = lax.all_to_all(coded, 'dp', 0, 0, axis_index_groups=rings)  31.1 us
    ppermute x14, starting transfers between devices, move_mp(): return lax.ppermute(block, 'mp', route)  31.1 us
    ppermute x20, waiting for transfers between devices, move_dp(): return lax.ppermute(block, 'dp', route)  28.3 us
    ppermute x20, starting transfers between devices, move_dp(): return lax.ppermute(block, 'dp', route)  21.6 us
    pallas_call x1, Pallas kernels, grads_and_gram(): pl.pallas_call(grads_kernel, grid_spec=pltpu.PrefetchScalarGridSpec(num_s...  19.4 us
    pallas_call x3, Pallas kernels, project(): pl.pallas_call(functools.partial(project_kernel, units, len(begin), last)...  15.2 us
    unnamed x23, local copies, waits for them, and re-layouts  7.77 us
  transfers between devices with their start and end apart: 35, of which 25 were waited for; matrix products, arithmetic and copies ran while one was open for 4% of the time, Pallas kernels for 17%

profile of v5, /device:TPU:30, one launch (start us, length us, event | category | flops | bytes accessed | tf_op | source)
XLA Modules:
  0.0 223.3 jit_solution(3305057413860077673)
XLA Ops:
  11.4 3.2 %constant_dynamic-slice_fusion.4 = bf16[272,4096]{1,0:T(8,128)(2,1)} fusion(bf16[544,4096]{1,0:T(8,128)(2,1)} %param.9, s32[]{:T(128)S(6)} %select_n.95), kind=kLoop, calls=%fused_computation.30 | loop fusion | bytes 4456452 | tf_op jit(solution)/shard_map/dynamic_slice | solution.py:383
  20.8 3.3 %collective-permute-start.5 = (bf16[3,544,128]{2,1,0:T(8,128)(2,1)S(1)}, bf16[3,544,128]{2,1,0:T(8,128)(2,1)S(1)}, u32[]{:S(2)}, u32[]{:S(2)}) collective-permute-start(bf16[3,544,128]{2,1,0:T(8,128)(2,1)S(1)} %get-tuple-element.91), channel_id=1, source_target_pairs={{0,2},{1,3},{2,4},{3,5},{4,6},{5,7},{6,0},{7,1},{8,10},{9,11},{10,... | collective-permute-start | bytes 1253384 | tf_op jit(solution)/shard_map/ppermute | solution.py:36
  24.1 3.1 %collective-permute-start.6 = (bf16[3,544,128]{2,1,0:T(8,128)(2,1)S(1)}, bf16[3,544,128]{2,1,0:T(8,128)(2,1)S(1)}, u32[]{:S(2)}, u32[]{:S(2)}) collective-permute-start(bf16[3,544,128]{2,1,0:T(8,128)(2,1)S(1)} %get-tuple-element.91), channel_id=1, source_target_pairs={{0,6},{1,7},{2,0},{3,1},{4,2},{5,3},{6,4},{7,5},{8,14},{9,15},{10,... | collective-permute-start | bytes 1253384 | tf_op jit(solution)/shard_map/ppermute | solution.py:36
  27.2 11.8 %collective-permute-done.5 = bf16[3,544,128]{2,1,0:T(8,128)(2,1)S(1)} collective-permute-done((bf16[3,544,128]{2,1,0:T(8,128)(2,1)S(1)}, bf16[3,544,128]{2,1,0:T(8,128)(2,1)S(1)}, u32[]{:S(2)}, u32[]{:S(2)}) %collective-permute-start.5) | collective-permute-done | bytes 417824 | tf_op jit(solution)/shard_map/ppermute | solution.py:36
  39.1 6.7 %collective-permute-done.6 = bf16[3,544,128]{2,1,0:T(8,128)(2,1)S(1)} collective-permute-done((bf16[3,544,128]{2,1,0:T(8,128)(2,1)S(1)}, bf16[3,544,128]{2,1,0:T(8,128)(2,1)S(1)}, u32[]{:S(2)}, u32[]{:S(2)}) %collective-permute-start.6) | collective-permute-done | bytes 417824 | tf_op jit(solution)/shard_map/ppermute | solution.py:36
  46.4 3.2 %collective-permute-start.9 = (bf16[544,512]{1,0:T(8,128)(2,1)S(1)}, bf16[544,512]{1,0:T(8,128)(2,1)}, u32[]{:S(2)}, u32[]{:S(2)}) collective-permute-start(bf16[544,512]{1,0:T(8,128)(2,1)S(1)} %slice.23), channel_id=1, source_target_pairs={{0,64},{8,72},{16,80},{24,88},{32,96},{40,104},{48,112},{56,120},{... | collective-permute-start | bytes 1671176 | tf_op jit(solution)/shard_map/ppermute | solution.py:28
  49.6 3.5 %collective-permute-start.7 = (bf16[3,272,128]{2,1,0:T(8,128)(2,1)S(1)}, bf16[3,272,128]{2,1,0:T(8,128)(2,1)S(1)}, u32[]{:S(2)}, u32[]{:S(2)}) collective-permute-start(bf16[3,272,128]{2,1,0:T(8,128)(2,1)S(1)} %slice.21), channel_id=1, source_target_pairs={{0,2},{1,3},{2,4},{3,5},{4,6},{5,7},{6,0},{7,1},{8,10},{9,11},{10,... | collective-permute-start | bytes 626696 | tf_op jit(solution)/shard_map/ppermute | solution.py:36
  53.1 3.0 %collective-permute-start.8 = (bf16[3,272,128]{2,1,0:T(8,128)(2,1)S(1)}, bf16[3,272,128]{2,1,0:T(8,128)(2,1)S(1)}, u32[]{:S(2)}, u32[]{:S(2)}) collective-permute-start(bf16[3,272,128]{2,1,0:T(8,128)(2,1)S(1)} %slice.22), channel_id=1, source_target_pairs={{0,6},{1,7},{2,0},{3,1},{4,2},{5,3},{6,4},{7,5},{8,14},{9,15},{10,... | collective-permute-start | bytes 626696 | tf_op jit(solution)/shard_map/ppermute | solution.py:36
  56.1 5.4 %collective-permute-done.7 = bf16[3,272,128]{2,1,0:T(8,128)(2,1)S(1)} collective-permute-done((bf16[3,272,128]{2,1,0:T(8,128)(2,1)S(1)}, bf16[3,272,128]{2,1,0:T(8,128)(2,1)S(1)}, u32[]{:S(2)}, u32[]{:S(2)}) %collective-permute-start.7) | collective-permute-done | bytes 208928 | tf_op jit(solution)/shard_map/ppermute | solution.py:36
  65.4 2.9 %collective-permute-done.11.other_ref = bf16[4,3,544,128]{3,2,1,0:T(8,128)(2,1)} collective-permute-done((bf16[4,3,544,128]{3,2,1,0:T(8,128)(2,1)S(1)}, bf16[4,3,544,128]{3,2,1,0:T(8,128)(2,1)}, u32[]{:S(2)}, u32[]{:S(2)}) %collective-permute-start.11) | collective-permute-done | bytes 1671200 | tf_op jit(solution)/shard_map/ppermute | solution.py:36
  68.3 19.4 %shard_map.76 = (f32[8,4,128,1024]{3,2,1,0:T(8,128)S(1)}, f32[8,128]{1,0:T(8,128)}) custom-call(s32[5]{0:T(128)} %stack.50.place, bf16[544,4096]{1,0:T(8,128)(2,1)} %tokens_ref.1, bf16[4,3,544,128]{3,2,1,0:T(8,128)(2,1)} %copy-done.6, bf16[4,3,544,128]{3,2,1,0:T(8,128)(2,1)} %collective-permute-done.11.other_ref, bf16[544,1024]{1,0:T(8,128)(2,1)} %o0_ref, ...), custom_call_target="tpu_custom_call" | custom-call | tf_op jit(solution)/shard_map/pallas_call | solution.py:99
  89.7 3.4 %collective-permute-start.13 = (f32[8,128]{1,0:T(8,128)S(1)}, f32[8,128]{1,0:T(8,128)S(1)}, u32[]{:S(2)}, u32[]{:S(2)}) collective-permute-start(f32[8,128]{1,0:T(8,128)S(1)} %add.135), channel_id=1, source_target_pairs={{0,4},{1,5},{2,6},{3,7},{4,0},{5,1},{6,2},{7,3},{8,12},{9,13},{10,... | collective-permute-start | bytes 12296 | tf_op jit(solution)/shard_map/ppermute | solution.py:36
  94.7 2.8 %collective-permute-start.15 = (f32[8,128]{1,0:T(8,128)S(1)}, f32[8,128]{1,0:T(8,128)S(1)}, u32[]{:S(2)}, u32[]{:S(2)}) collective-permute-start(f32[8,128]{1,0:T(8,128)S(1)} %add.135), channel_id=1, source_target_pairs={{0,6},{1,7},{2,0},{3,1},{4,2},{5,3},{6,4},{7,5},{8,14},{9,15},{10,... | collective-permute-start | bytes 12296 | tf_op jit(solution)/shard_map/ppermute | solution.py:36
  99.2 4.4 %shard_map.77 = f32[8,136,1024]{2,1,0:T(8,128)S(1)} custom-call(f32[8,128]{1,0:T(8,128)S(1)} %add_add_fusion.1.gram_ref, f32[8,4,128,1024]{3,2,1,0:T(8,128)S(1)} %get-tuple-element.65.grads_ref), custom_call_target="tpu_custom_call" | custom-call | tf_op jit(solution)/shard_map/pallas_call | solution.py:178
  104.1 31.1 %all_to_all.5 = f16[8,136,1024]{2,1,0:T(8,128)(2,1)S(1)} all-to-all(f16[8,136,1024]{2,1,0:T(8,128)(2,1)S(1)} %convert_element_type.12), channel_id=1, replica_groups={{0,8,16,24,32,40,48,56},{64,72,80,88,96,104,112,120},{128,136,144,152,1..., dimensions={0} | all-to-all | bytes 4456448 | tf_op jit(solution)/shard_map/all_to_all | solution.py:402
  142.4 5.7 %collective-permute-start.17 = (f32[40,128]{1,0:T(8,128)S(1)}, f32[40,128]{1,0:T(8,128)S(1)}, u32[]{:S(2)}, u32[]{:S(2)}) collective-permute-start(f32[40,128]{1,0:T(8,128)S(1)} %add.142), channel_id=1, source_target_pairs={{0,4},{1,5},{2,6},{3,7},{4,0},{5,1},{6,2},{7,3},{8,12},{9,13},{10,... | collective-permute-start | bytes 61448 | tf_op jit(solution)/shard_map/ppermute | solution.py:36
  149.0 3.3 %collective-permute-start.19 = (f32[40,128]{1,0:T(8,128)S(1)}, f32[40,128]{1,0:T(8,128)S(1)}, u32[]{:S(2)}, u32[]{:S(2)}) collective-permute-start(f32[40,128]{1,0:T(8,128)S(1)} %add.142), channel_id=1, source_target_pairs={{0,6},{1,7},{2,0},{3,1},{4,2},{5,3},{6,4},{7,5},{8,14},{9,15},{10,... | collective-permute-start | bytes 61448 | tf_op jit(solution)/shard_map/ppermute | solution.py:36
  170.8 2.8 %collective-permute-done.27.refs_9_ = bf16[512,256]{1,0:T(8,128)(2,1)S(1)} collective-permute-done((bf16[512,256]{1,0:T(8,128)(2,1)S(1)}, bf16[512,256]{1,0:T(8,128)(2,1)S(1)}, u32[]{:S(2)}, u32[]{:S(2)}) %collective-permute-start.27) | collective-permute-done | bytes 262176 | tf_op jit(solution)/shard_map/ppermute | solution.py:28
  173.6 3.5 %copy-done = bf16[1088,4096]{1,0:T(8,128)(2,1)S(1)} copy-done((bf16[1088,4096]{1,0:T(8,128)(2,1)S(1)}, bf16[1088,4096]{1,0:T(8,128)(2,1)}, u32[]{:S(2)}) %copy-start) | copy-done | bytes 8912920
  177.1 4.0 %shard_map.80.refs_11_ = f32[2,1088,256]{2,1,0:T(8,128)S(1)} custom-call(s32[5]{0:T(128)S(1)} %copy-done.5, bf16[1088,4096]{1,0:T(8,128)(2,1)S(1)} %copy-done, bf16[1088,4096]{1,0:T(8,128)(2,1)S(1)} %copy-done, bf16[1088,4096]{1,0:T(8,128)(2,1)S(1)} %copy-done, bf16[1088,4096]{1,0:T(8,128)(2,1)S(1)} %copy-done, ...), custom_call_target="tpu_custom_call" | custom-call | tf_op jit(solution)/shard_map/pallas_call | solution.py:320
  184.0 5.5 %shard_map.81.refs_11_ = f32[2,1088,256]{2,1,0:T(8,128)S(1)} custom-call(s32[5]{0:T(128)S(1)} %copy-done.5, bf16[1088,4096]{1,0:T(8,128)(2,1)S(1)} %copy-done, bf16[1088,4096]{1,0:T(8,128)(2,1)S(1)} %copy-done, bf16[1088,4096]{1,0:T(8,128)(2,1)S(1)} %copy-done, bf16[1088,4096]{1,0:T(8,128)(2,1)S(1)} %copy-done, ...), custom_call_target="tpu_custom_call" | custom-call | tf_op jit(solution)/shard_map/pallas_call | solution.py:320
  194.6 5.7 %shard_map.82 = (bf16[2,272,256]{2,1,0:T(8,128)(2,1)S(1)}, bf16[2,272,256]{2,1,0:T(8,128)(2,1)S(1)}, bf16[2,272,256]{2,1,0:T(8,128)(2,1)S(1)}, bf16[2,272,256]{2,1,0:T(8,128)(2,1)S(1)}) custom-call(s32[5]{0:T(128)S(1)} %copy-done.5, bf16[1088,4096]{1,0:T(8,128)(2,1)S(1)} %copy-done, bf16[1088,4096]{1,0:T(8,128)(2,1)S(1)} %copy-done, ...), custom_call_target="tpu_custom_call" | custom-call | tf_op jit(solution)/shard_map/pallas_call | solution.py:320
  203.1 6.7 %collective-permute-done.31.p1_ref = bf16[2,272,256]{2,1,0:T(8,128)(2,1)S(1)} collective-permute-done((bf16[2,272,256]{2,1,0:T(8,128)(2,1)S(1)}, bf16[2,272,256]{2,1,0:T(8,128)(2,1)S(1)}, u32[]{:S(2)}, u32[]{:S(2)}) %collective-permute-start.31) | collective-permute-done | bytes 278560 | tf_op jit(solution)/shard_map/ppermute | solution.py:28
  211.8 2.9 %collective-permute-done.33.p3_ref = bf16[2,272,256]{2,1,0:T(8,128)(2,1)S(1)} collective-permute-done((bf16[2,272,256]{2,1,0:T(8,128)(2,1)S(1)}, bf16[2,272,256]{2,1,0:T(8,128)(2,1)S(1)}, u32[]{:S(2)}, u32[]{:S(2)}) %collective-permute-start.33) | collective-permute-done | bytes 278560 | tf_op jit(solution)/shard_map/ppermute | solution.py:28
  (98 shorter events, 61.4 us)
Async XLA Ops:
  7.2 135.1 %all-gather.2.cloned.1.call-start = ((), (), s32[]{:S(2)}) async-start(), calls=%async_computation.1 | async-start | bytes 11141120 | tf_op jit(solution)/shard_map/all_gather | solution.py:387
  8.5 6.6 %collective-permute-start = (bf16[544,128]{1,0:T(8,128)(2,1)S(1)}, bf16[544,128]{1,0:T(8,128)(2,1)S(1)}, u32[]{:S(2)}, u32[]{:S(2)}) collective-permute-start(bf16[544,128]{1,0:T(8,128)(2,1)S(1)} %get-tuple-element.45), channel_id=1, source_target_pairs={{0,64},{8,72},{16,80},{24,88},{32,96},{40,104},{48,112},{56,120},{... | collective-permute-start | bytes 417800 | tf_op jit(solution)/shard_map/ppermute | solution.py:28
  8.8 7.8 %collective-permute-start.1 = (bf16[544,128]{1,0:T(8,128)(2,1)S(1)}, bf16[544,128]{1,0:T(8,128)(2,1)S(1)}, u32[]{:S(2)}, u32[]{:S(2)}) collective-permute-start(bf16[544,128]{1,0:T(8,128)(2,1)S(1)} %get-tuple-element.46), channel_id=1, source_target_pairs={{0,128},{8,136},{16,144},{24,152},{32,160},{40,168},{48,176},{56,1... | collective-permute-start | bytes 417800 | tf_op jit(solution)/shard_map/ppermute | solution.py:28
  11.4 7.2 %collective-permute-start.2 = (bf16[544,128]{1,0:T(8,128)(2,1)S(1)}, bf16[544,128]{1,0:T(8,128)(2,1)S(1)}, u32[]{:S(2)}, u32[]{:S(2)}) collective-permute-start(bf16[544,128]{1,0:T(8,128)(2,1)S(1)} %get-tuple-element.47), channel_id=1, source_target_pairs={{0,192},{8,200},{16,208},{24,216},{32,224},{40,232},{48,240},{56,2... | collective-permute-start | bytes 417800 | tf_op jit(solution)/shard_map/ppermute | solution.py:28
  18.6 27.2 %collective-permute-start.3 = (bf16[544,1024]{1,0:T(8,128)(2,1)S(1)}, bf16[544,1024]{1,0:T(8,128)(2,1)S(1)}, u32[]{:S(2)}, u32[]{:S(2)}) collective-permute-start(bf16[544,1024]{1,0:T(8,128)(2,1)S(1)} %copy-done.9), channel_id=1, source_target_pairs={{0,64},{8,72},{16,80},{24,88},{32,96},{40,104},{48,112},{56,120},{... | collective-permute-start | bytes 3342344 | tf_op jit(solution)/shard_map/ppermute | solution.py:28
  19.7 26.4 %collective-permute-start.4 = (bf16[544,1024]{1,0:T(8,128)(2,1)S(1)}, bf16[544,1024]{1,0:T(8,128)(2,1)S(1)}, u32[]{:S(2)}, u32[]{:S(2)}) collective-permute-start(bf16[544,1024]{1,0:T(8,128)(2,1)S(1)} %copy-done.9), channel_id=1, source_target_pairs={{0,192},{8,200},{16,208},{24,216},{32,224},{40,232},{48,240},{56,2... | collective-permute-start | bytes 3342344 | tf_op jit(solution)/shard_map/ppermute | solution.py:28
  20.8 18.3 %collective-permute-start.5 = (bf16[3,544,128]{2,1,0:T(8,128)(2,1)S(1)}, bf16[3,544,128]{2,1,0:T(8,128)(2,1)S(1)}, u32[]{:S(2)}, u32[]{:S(2)}) collective-permute-start(bf16[3,544,128]{2,1,0:T(8,128)(2,1)S(1)} %get-tuple-element.91), channel_id=1, source_target_pairs={{0,2},{1,3},{2,4},{3,5},{4,6},{5,7},{6,0},{7,1},{8,10},{9,11},{10,... | collective-permute-start | bytes 1253384 | tf_op jit(solution)/shard_map/ppermute | solution.py:36
  24.1 21.6 %collective-permute-start.6 = (bf16[3,544,128]{2,1,0:T(8,128)(2,1)S(1)}, bf16[3,544,128]{2,1,0:T(8,128)(2,1)S(1)}, u32[]{:S(2)}, u32[]{:S(2)}) collective-permute-start(bf16[3,544,128]{2,1,0:T(8,128)(2,1)S(1)} %get-tuple-element.91), channel_id=1, source_target_pairs={{0,6},{1,7},{2,0},{3,1},{4,2},{5,3},{6,4},{7,5},{8,14},{9,15},{10,... | collective-permute-start | bytes 1253384 | tf_op jit(solution)/shard_map/ppermute | solution.py:36
  46.1 17.9 %collective-permute-start.10 = (bf16[544,512]{1,0:T(8,128)(2,1)S(1)}, bf16[544,512]{1,0:T(8,128)(2,1)S(1)}, u32[]{:S(2)}, u32[]{:S(2)}) collective-permute-start(bf16[544,512]{1,0:T(8,128)(2,1)S(1)} %slice.24), channel_id=1, source_target_pairs={{0,192},{8,200},{16,208},{24,216},{32,224},{40,232},{48,240},{56,2... | collective-permute-start | bytes 1671176 | tf_op jit(solution)/shard_map/ppermute | solution.py:28
  46.4 17.7 %collective-permute-start.9 = (bf16[544,512]{1,0:T(8,128)(2,1)S(1)}, bf16[544,512]{1,0:T(8,128)(2,1)}, u32[]{:S(2)}, u32[]{:S(2)}) collective-permute-start(bf16[544,512]{1,0:T(8,128)(2,1)S(1)} %slice.23), channel_id=1, source_target_pairs={{0,64},{8,72},{16,80},{24,88},{32,96},{40,104},{48,112},{56,120},{... | collective-permute-start | bytes 1671176 | tf_op jit(solution)/shard_map/ppermute | solution.py:28
  49.6 11.9 %collective-permute-start.7 = (bf16[3,272,128]{2,1,0:T(8,128)(2,1)S(1)}, bf16[3,272,128]{2,1,0:T(8,128)(2,1)S(1)}, u32[]{:S(2)}, u32[]{:S(2)}) collective-permute-start(bf16[3,272,128]{2,1,0:T(8,128)(2,1)S(1)} %slice.21), channel_id=1, source_target_pairs={{0,2},{1,3},{2,4},{3,5},{4,6},{5,7},{6,0},{7,1},{8,10},{9,11},{10,... | collective-permute-start | bytes 626696 | tf_op jit(solution)/shard_map/ppermute | solution.py:36
  53.1 10.9 %collective-permute-start.8 = (bf16[3,272,128]{2,1,0:T(8,128)(2,1)S(1)}, bf16[3,272,128]{2,1,0:T(8,128)(2,1)S(1)}, u32[]{:S(2)}, u32[]{:S(2)}) collective-permute-start(bf16[3,272,128]{2,1,0:T(8,128)(2,1)S(1)} %slice.22), channel_id=1, source_target_pairs={{0,6},{1,7},{2,0},{3,1},{4,2},{5,3},{6,4},{7,5},{8,14},{9,15},{10,... | collective-permute-start | bytes 626696 | tf_op jit(solution)/shard_map/ppermute | solution.py:36
  89.7 7.7 %collective-permute-start.13 = (f32[8,128]{1,0:T(8,128)S(1)}, f32[8,128]{1,0:T(8,128)S(1)}, u32[]{:S(2)}, u32[]{:S(2)}) collective-permute-start(f32[8,128]{1,0:T(8,128)S(1)} %add.135), channel_id=1, source_target_pairs={{0,4},{1,5},{2,6},{3,7},{4,0},{5,1},{6,2},{7,3},{8,12},{9,13},{10,... | collective-permute-start | bytes 12296 | tf_op jit(solution)/shard_map/ppermute | solution.py:36
  142.2 16.4 %collective-permute-start.20 = (bf16[1088,4096]{1,0:T(8,128)(2,1)}, bf16[1088,4096]{1,0:T(8,128)(2,1)}, u32[]{:S(2)}, u32[]{:S(2)}) collective-permute-start(bf16[1088,4096]{1,0:T(8,128)(2,1)} %all-gather.2.cloned.1.call-done.refs_0_.refs_1_.refs_2_.refs_3_), channel_id=1, source_target_pairs={{0,1},{1,0},{2,3},{3,2},{4,5},{5,4},{6,7},{7,6},{8,9},{9,8},{10,11... | collective-permute-start | bytes 26738696 | tf_op jit(solution)/shard_map/ppermute | solution.py:36
  142.4 9.8 %collective-permute-start.17 = (f32[40,128]{1,0:T(8,128)S(1)}, f32[40,128]{1,0:T(8,128)S(1)}, u32[]{:S(2)}, u32[]{:S(2)}) collective-permute-start(f32[40,128]{1,0:T(8,128)S(1)} %add.142), channel_id=1, source_target_pairs={{0,4},{1,5},{2,6},{3,7},{4,0},{5,1},{6,2},{7,3},{8,12},{9,13},{10,... | collective-permute-start | bytes 61448 | tf_op jit(solution)/shard_map/ppermute | solution.py:36
  167.9 13.2 %collective-permute-start.24 = (bf16[512,256]{1,0:T(8,128)(2,1)S(1)}, bf16[512,256]{1,0:T(8,128)(2,1)S(1)}, u32[]{:S(2)}, u32[]{:S(2)}) collective-permute-start(bf16[512,256]{1,0:T(8,128)(2,1)S(1)} %pad_maximum_fusion.2.refs_8_), channel_id=1, source_target_pairs={{0,64},{8,72},{16,80},{24,88},{32,96},{40,104},{48,112},{56,120},{... | collective-permute-start | bytes 786440 | tf_op jit(solution)/shard_map/ppermute | solution.py:28
  169.2 12.0 %collective-permute-start.25 = (bf16[512,256]{1,0:T(8,128)(2,1)S(1)}, bf16[512,256]{1,0:T(8,128)(2,1)S(1)}, u32[]{:S(2)}, u32[]{:S(2)}) collective-permute-start(bf16[512,256]{1,0:T(8,128)(2,1)S(1)} %pad_maximum_fusion.2.refs_8_), channel_id=1, source_target_pairs={{0,128},{8,136},{16,144},{24,152},{32,160},{40,168},{48,176},{56,1... | collective-permute-start | bytes 786440 | tf_op jit(solution)/shard_map/ppermute | solution.py:28
  170.8 10.5 %collective-permute-start.26 = (bf16[512,256]{1,0:T(8,128)(2,1)S(1)}, bf16[512,256]{1,0:T(8,128)(2,1)S(1)}, u32[]{:S(2)}, u32[]{:S(2)}) collective-permute-start(bf16[512,256]{1,0:T(8,128)(2,1)S(1)} %pad_maximum_fusion.2.refs_8_), channel_id=1, source_target_pairs={{0,192},{8,200},{16,208},{24,216},{32,224},{40,232},{48,240},{56,2... | collective-permute-start | bytes 786440 | tf_op jit(solution)/shard_map/ppermute | solution.py:28
  181.3 9.0 %collective-permute-start.28 = (bf16[512,256]{1,0:T(8,128)(2,1)S(1)}, bf16[512,256]{1,0:T(8,128)(2,1)S(1)}, u32[]{:S(2)}, u32[]{:S(2)}) collective-permute-start(bf16[512,256]{1,0:T(8,128)(2,1)S(1)} %collective-permute-done.27.refs_9_), channel_id=1, source_target_pairs={{0,64},{8,72},{16,80},{24,88},{32,96},{40,104},{48,112},{56,120},{... | collective-permute-start | bytes 786440 | tf_op jit(solution)/shard_map/ppermute | solution.py:28
  182.7 9.2 %collective-permute-start.29 = (bf16[512,256]{1,0:T(8,128)(2,1)S(1)}, bf16[512,256]{1,0:T(8,128)(2,1)S(1)}, u32[]{:S(2)}, u32[]{:S(2)}) collective-permute-start(bf16[512,256]{1,0:T(8,128)(2,1)S(1)} %collective-permute-done.27.refs_9_), channel_id=1, source_target_pairs={{0,128},{8,136},{16,144},{24,152},{32,160},{40,168},{48,176},{56,1... | collective-permute-start | bytes 786440 | tf_op jit(solution)/shard_map/ppermute | solution.py:28
  184.0 10.6 %collective-permute-start.30 = (bf16[512,256]{1,0:T(8,128)(2,1)S(1)}, bf16[512,256]{1,0:T(8,128)(2,1)S(1)}, u32[]{:S(2)}, u32[]{:S(2)}) collective-permute-start(bf16[512,256]{1,0:T(8,128)(2,1)S(1)} %collective-permute-done.27.refs_9_), channel_id=1, source_target_pairs={{0,192},{8,200},{16,208},{24,216},{32,224},{40,232},{48,240},{56,2... | collective-permute-start | bytes 786440 | tf_op jit(solution)/shard_map/ppermute | solution.py:28
  200.2 9.5 %collective-permute-start.31 = (bf16[2,272,256]{2,1,0:T(8,128)(2,1)S(1)}, bf16[2,272,256]{2,1,0:T(8,128)(2,1)S(1)}, u32[]{:S(2)}, u32[]{:S(2)}) collective-permute-start(bf16[2,272,256]{2,1,0:T(8,128)(2,1)S(1)} %get-tuple-element.84), channel_id=1, source_target_pairs={{0,16},{8,24},{16,32},{24,40},{32,48},{40,56},{48,0},{56,8},{64,80... | collective-permute-start | bytes 835592 | tf_op jit(solution)/shard_map/ppermute | solution.py:28
  201.1 10.8 %collective-permute-start.32 = (bf16[2,272,256]{2,1,0:T(8,128)(2,1)S(1)}, bf16[2,272,256]{2,1,0:T(8,128)(2,1)S(1)}, u32[]{:S(2)}, u32[]{:S(2)}) collective-permute-start(bf16[2,272,256]{2,1,0:T(8,128)(2,1)S(1)} %get-tuple-element.85), channel_id=1, source_target_pairs={{0,32},{8,40},{16,48},{24,56},{32,0},{40,8},{48,16},{56,24},{64,96... | collective-permute-start | bytes 835592 | tf_op jit(solution)/shard_map/ppermute | solution.py:28
  202.3 12.4 %collective-permute-start.33 = (bf16[2,272,256]{2,1,0:T(8,128)(2,1)S(1)}, bf16[2,272,256]{2,1,0:T(8,128)(2,1)S(1)}, u32[]{:S(2)}, u32[]{:S(2)}) collective-permute-start(bf16[2,272,256]{2,1,0:T(8,128)(2,1)S(1)} %get-tuple-element.86), channel_id=1, source_target_pairs={{0,48},{8,56},{16,0},{24,8},{32,16},{40,24},{48,32},{56,40},{64,11... | collective-permute-start | bytes 835592 | tf_op jit(solution)/shard_map/ppermute | solution.py:28
  (22 other events, 188.0 us)
Sparse Core Ops, SparseCore 0:
  18.7 92.6 all-gather.1
